TPU v7x, 32 devices: a whole 2x2x4 slice. The times are simulated.
32 devices in a mesh: dp: 8 (over y, x, core), fsdp: 4 (over z).
Axes of the slice: x: 2, y: 2, z: 4, core: 2. Of those that a mesh axis runs over, the one named last changes fastest.
Arguments:
- tokens: bfloat16 [8192, 1536], P(('dp', 'fsdp')), may hold values from -6 to 6
- gain_attn: bfloat16 [2, 1536], P(None, ('dp', 'fsdp')), may hold values from 0.099609375 to 1.8984375
- w_query: bfloat16 [2, 1536, 1536], P(None, ('dp', 'fsdp')), may hold values from -0.15625 to 0.15625
- w_key: bfloat16 [2, 1536, 768], P(None, ('dp', 'fsdp')), may hold values from -0.15625 to 0.15625
- w_value: bfloat16 [2, 1536, 768], P(None, ('dp', 'fsdp')), may hold values from -0.15625 to 0.15625
- w_out: bfloat16 [2, 1536, 1536], P(None, ('dp', 'fsdp')), may hold values from -1.25 to 1.25
- gain_ffn: bfloat16 [2, 1536], P(None, ('dp', 'fsdp')), may hold values from 0.099609375 to 1.8984375
- w_gate: bfloat16 [2, 1536, 4096], P(None, ('dp', 'fsdp')), may hold values from -0.15625 to 0.15625
- w_up: bfloat16 [2, 1536, 4096], P(None, ('dp', 'fsdp')), may hold values from -0.15625 to 0.15625
- w_down: bfloat16 [2, 4096, 1536], P(None, ('dp', 'fsdp')), may hold values from -0.09375 to 0.09375
- lengths: int32 [8, 4], P('dp'), may hold values from 1 to 128, 384 in all within a row
- cotangent: bfloat16 [8192, 1536], P(('dp', 'fsdp')), may hold values from -6 to 6
Outputs:
- layer_outputs: bfloat16 [2, 8192, 1536], P(None, ('dp', 'fsdp'))
- input_grad: float32 [8192, 1536], P(('dp', 'fsdp'))
- grad_gain_attn: float32 [2, 1536], P(None, ('dp', 'fsdp'))
- grad_w_query: float32 [2, 1536, 1536], P(None, ('dp', 'fsdp'))
- grad_w_key: float32 [2, 1536, 768], P(None, ('dp', 'fsdp'))
- grad_w_value: float32 [2, 1536, 768], P(None, ('dp', 'fsdp'))
- grad_w_out: float32 [2, 1536, 1536], P(None, ('dp', 'fsdp'))
- grad_gain_ffn: float32 [2, 1536], P(None, ('dp', 'fsdp'))
- grad_w_gate: float32 [2, 1536, 4096], P(None, ('dp', 'fsdp'))
- grad_w_up: float32 [2, 1536, 4096], P(None, ('dp', 'fsdp'))
- grad_w_down: float32 [2, 4096, 1536], P(None, ('dp', 'fsdp'))
Inputs may be any that keep to these rules, and one draw needn't show every extreme that they name: Each group's 4 continuation lengths sum to 384 and one of them is 128.
All inputs are finite; a program needn't handle non-finite values.
Results may differ from a plain program's by a relative error of at most 0.029.
Values may be sent and summed in bfloat16 or wider, within the bound.
A program may use at most 448 MiB of HBM per device.

v0:
```python
import math

import jax
import jax.numpy as jnp
from jax import lax
from jax.sharding import PartitionSpec as P

HEAD_DIM = 96


EPSILON = 1e-05
ROPE_BASE = 100000.0
NEGATIVE = -1e30


def layout(lengths_row, group_tok):
    places = jnp.arange(group_tok, dtype=jnp.int32)
    prompt_len = group_tok - jnp.sum(lengths_row)
    starts = prompt_len + jnp.cumsum(lengths_row) - lengths_row
    inside = places[:, None] >= starts[None, :]
    segment = jnp.sum(inside.astype(jnp.int32), axis=1)
    begins = jnp.max(jnp.where(inside, starts[None, :], 0), axis=1)
    position = jnp.where(segment > 0, places - begins + prompt_len, places)
    return (segment, position)


def rotate(values, position, direction):
    row_count = values.shape[0]
    shaped = values.reshape(row_count, -1, HEAD_DIM)
    halfway = HEAD_DIM // 2
    frequency = ROPE_BASE ** (-jnp.arange(halfway, dtype=jnp.float32) * 2.0 / HEAD_DIM)
    angles = position.astype(jnp.float32)[:, None] * frequency[None, :]
    cosine = jnp.cos(angles)[:, None, :]
    sine_part = direction * jnp.sin(angles)[:, None, :]
    first_half = shaped[..., :halfway]
    second_half = shaped[..., halfway:]
    turned = jnp.concatenate(
        [
            first_half * cosine - second_half * sine_part,
            second_half * cosine + first_half * sine_part,
        ],
        axis=-1,
    )
    return turned.reshape(values.shape)


def norm_apply(values, gain_vec):
    inv_rms = lax.rsqrt(jnp.mean(values * values, axis=-1, keepdims=True) + EPSILON)
    return values * inv_rms * gain_vec


def norm_back(values, gain_vec, incoming):
    inv_rms = lax.rsqrt(jnp.mean(values * values, axis=-1, keepdims=True) + EPSILON)
    weighted = incoming * gain_vec
    inner_sum = jnp.mean(weighted * values, axis=-1, keepdims=True)
    grad_values = inv_rms * weighted - values * inv_rms * inv_rms * inv_rms * inner_sum
    grad_gain = jnp.sum(incoming * values * inv_rms, axis=0)
    return (grad_values, grad_gain)


def matmul(left, right):
    return jnp.dot(left, right, preferred_element_type=jnp.float32)


def visibility(seg_rows, row_places, segment, places):
    same_seq = (seg_rows[:, None] == segment[None, :]) & (places[None, :] <= row_places[:, None])
    prompt_seen = (segment[None, :] == 0) & (seg_rows[:, None] > 0)
    return same_seq | prompt_seen


def head_slices(query_b, keys_all, head_index):
    row_count = query_b.shape[0]
    kv_width = keys_all.shape[1] // 2
    sharing = query_b.shape[1] // kv_width
    query_part = lax.dynamic_slice_in_dim(
        query_b, head_index * sharing * HEAD_DIM, sharing * HEAD_DIM, 1
    ).reshape(row_count, sharing, HEAD_DIM)
    key_part = lax.dynamic_slice_in_dim(keys_all, head_index * HEAD_DIM, HEAD_DIM, 1)
    value_part = lax.dynamic_slice_in_dim(keys_all, kv_width + head_index * HEAD_DIM, HEAD_DIM, 1)
    return (query_part, key_part, value_part)


def attend_forward(query_b, keys_all, visible):
    row_count = query_b.shape[0]
    kv_heads = keys_all.shape[1] // 2 // HEAD_DIM
    factor = 1.0 / math.sqrt(HEAD_DIM)

    def per_head(head_index):
        query_part, key_part, value_part = head_slices(query_b, keys_all, head_index)
        scores = (
            jnp.einsum("tgd,kd->gtk", query_part, key_part, preferred_element_type=jnp.float32)
            * factor
        )
        masked = jnp.where(visible[None], scores, NEGATIVE)
        peak_score = jnp.max(masked, axis=-1)
        exponent = jnp.where(visible[None], jnp.exp(masked - peak_score[..., None]), 0.0)
        totals = jnp.sum(exponent, axis=-1)
        probability = (exponent / totals[..., None]).astype(jnp.bfloat16)
        mixed_heads = jnp.einsum(
            "gtk,kd->tgd", probability, value_part, preferred_element_type=jnp.float32
        )
        return (mixed_heads.reshape(row_count, -1), peak_score, totals)

    mixed_heads, peak_score, totals = lax.map(per_head, jnp.arange(kv_heads, dtype=jnp.int32))
    return (jnp.transpose(mixed_heads, (1, 0, 2)).reshape(row_count, -1), peak_score, totals)


def attend_backward(query_b, keys_all, visible, peak_score, totals, grad_mixed):
    row_count = query_b.shape[0]
    kv_width = keys_all.shape[1] // 2
    kv_heads = kv_width // HEAD_DIM
    sharing = query_b.shape[1] // kv_width
    factor = 1.0 / math.sqrt(HEAD_DIM)

    def per_head(pieces):
        head_index, peak_head, total_head = pieces
        query_part, key_part, value_part = head_slices(query_b, keys_all, head_index)
        grad_part = lax.dynamic_slice_in_dim(
            grad_mixed, head_index * sharing * HEAD_DIM, sharing * HEAD_DIM, 1
        ).reshape(row_count, sharing, HEAD_DIM)
        scores = (
            jnp.einsum("tgd,kd->gtk", query_part, key_part, preferred_element_type=jnp.float32)
            * factor
        )
        masked = jnp.where(visible[None], scores, NEGATIVE)
        exponent = jnp.where(visible[None], jnp.exp(masked - peak_head[..., None]), 0.0)
        probability = exponent / total_head[..., None]
        prob_low = probability.astype(jnp.bfloat16)
        grad_probs = jnp.einsum(
            "tgd,kd->gtk", grad_part, value_part, preferred_element_type=jnp.float32
        )
        inner_sum = jnp.sum(probability * grad_probs, axis=-1, keepdims=True)
        grad_scores = (probability * (grad_probs - inner_sum)).astype(jnp.bfloat16)
        grad_query = (
            jnp.einsum("gtk,kd->tgd", grad_scores, key_part, preferred_element_type=jnp.float32)
            * factor
        )
        grad_key = (
            jnp.einsum("gtk,tgd->kd", grad_scores, query_part, preferred_element_type=jnp.float32)
            * factor
        )
        grad_value = jnp.einsum(
            "gtk,tgd->kd", prob_low, grad_part, preferred_element_type=jnp.float32
        )
        return (grad_query.reshape(row_count, -1), grad_key, grad_value)

    grad_query, grad_key, grad_value = lax.map(
        per_head, (jnp.arange(kv_heads, dtype=jnp.int32), peak_score, totals)
    )
    group_rows = keys_all.shape[0]
    key_terms = jnp.concatenate(
        [
            jnp.transpose(grad_key, (1, 0, 2)).reshape(group_rows, -1),
            jnp.transpose(grad_value, (1, 0, 2)).reshape(group_rows, -1),
        ],
        axis=1,
    )
    return (jnp.transpose(grad_query, (1, 0, 2)).reshape(row_count, -1), key_terms)


def fetch_attention(layer_index, gain_attn, w_query, w_key, w_value, w_out):
    return (
        lax.all_gather(gain_attn[layer_index], ("dp", "fsdp"), axis=0, tiled=True),
        lax.all_gather(w_query[layer_index], ("dp", "fsdp"), axis=0, tiled=True),
        lax.all_gather(w_key[layer_index], ("dp", "fsdp"), axis=0, tiled=True),
        lax.all_gather(w_value[layer_index], ("dp", "fsdp"), axis=0, tiled=True),
        lax.all_gather(w_out[layer_index], ("dp", "fsdp"), axis=0, tiled=True),
    )


def fetch_ffn(layer_index, gain_ffn, w_gate, w_up, w_down):
    return (
        lax.all_gather(gain_ffn[layer_index], ("dp", "fsdp"), axis=0, tiled=True),
        lax.all_gather(w_gate[layer_index], ("dp", "fsdp"), axis=0, tiled=True),
        lax.all_gather(w_up[layer_index], ("dp", "fsdp"), axis=0, tiled=True),
        lax.all_gather(w_down[layer_index], ("dp", "fsdp"), axis=0, tiled=True),
    )


def share_keys(stacked):
    return lax.all_gather(stacked, "fsdp", axis=0, tiled=True)


def layer_forward(hidden, attn_weights, ffn_weights, pos_rows, visible):
    gain_a, query_w, key_w, value_w, out_w = attn_weights
    gain_f, gate_w, upper_w, down_w = ffn_weights
    normed = norm_apply(hidden, gain_a.astype(jnp.float32)).astype(jnp.bfloat16)
    query_b = rotate(matmul(normed, query_w), pos_rows, 1.0).astype(jnp.bfloat16)
    key_b = rotate(matmul(normed, key_w), pos_rows, 1.0).astype(jnp.bfloat16)
    value_b = matmul(normed, value_w).astype(jnp.bfloat16)
    stacked = jnp.concatenate([key_b, value_b], axis=1)
    keys_all = share_keys(stacked)
    mixed_heads, peak_score, totals = attend_forward(query_b, keys_all, visible)
    mixed_b = mixed_heads.astype(jnp.bfloat16)
    middle = hidden + matmul(mixed_b, out_w)
    normed_ffn = norm_apply(middle, gain_f.astype(jnp.float32)).astype(jnp.bfloat16)
    gating = matmul(normed_ffn, gate_w)
    upward = matmul(normed_ffn, upper_w)
    activated = (jax.nn.silu(gating) * upward).astype(jnp.bfloat16)
    result = middle + matmul(activated, down_w)
    saved = (
        hidden,
        normed,
        query_b,
        stacked,
        keys_all,
        peak_score,
        totals,
        mixed_b,
        middle,
        normed_ffn,
        gating,
        upward,
        activated,
    )
    return (result, saved)


def layer_backward(upstream, saved, attn_weights, ffn_weights, keys_all, pos_rows, visible):
    (
        hidden,
        normed,
        query_b,
        stacked,
        unused_keys,
        peak_score,
        totals,
        mixed_b,
        middle,
        normed_ffn,
        gating,
        upward,
        activated,
    ) = saved
    gain_a, query_w, key_w, value_w, out_w = attn_weights
    gain_f, gate_w, upper_w, down_w = ffn_weights
    grad_branch = upstream.astype(jnp.bfloat16)
    grad_down_w = matmul(activated.T, grad_branch)
    grad_act = matmul(grad_branch, down_w.T)
    sigmoid_g = jax.nn.sigmoid(gating)
    grad_gate = (grad_act * upward * sigmoid_g * (1.0 + gating * (1.0 - sigmoid_g))).astype(
        jnp.bfloat16
    )
    grad_up = (grad_act * gating * sigmoid_g).astype(jnp.bfloat16)
    grad_gate_w = matmul(normed_ffn.T, grad_gate)
    grad_up_w = matmul(normed_ffn.T, grad_up)
    grad_normed_ffn = matmul(grad_gate, gate_w.T) + matmul(grad_up, upper_w.T)
    grad_middle_part, grad_gain_f = norm_back(middle, gain_f.astype(jnp.float32), grad_normed_ffn)
    ffn_blocks = (
        lax.psum_scatter(
            grad_gain_f.astype(jnp.bfloat16), "dp", scatter_dimension=0, tiled=True
        ).astype(jnp.float32),
        lax.psum_scatter(
            grad_gate_w.astype(jnp.bfloat16), "dp", scatter_dimension=0, tiled=True
        ).astype(jnp.float32),
        lax.psum_scatter(
            grad_up_w.astype(jnp.bfloat16), "dp", scatter_dimension=0, tiled=True
        ).astype(jnp.float32),
        lax.psum_scatter(
            grad_down_w.astype(jnp.bfloat16), "dp", scatter_dimension=0, tiled=True
        ).astype(jnp.float32),
    )
    ffn_grads = (
        lax.psum_scatter(
            ffn_blocks[0].astype(jnp.bfloat16), "fsdp", scatter_dimension=0, tiled=True
        ).astype(jnp.float32),
        lax.psum_scatter(
            ffn_blocks[1].astype(jnp.bfloat16), "fsdp", scatter_dimension=0, tiled=True
        ).astype(jnp.float32),
        lax.psum_scatter(
            ffn_blocks[2].astype(jnp.bfloat16), "fsdp", scatter_dimension=0, tiled=True
        ).astype(jnp.float32),
        lax.psum_scatter(
            ffn_blocks[3].astype(jnp.bfloat16), "fsdp", scatter_dimension=0, tiled=True
        ).astype(jnp.float32),
    )
    grad_middle = upstream + grad_middle_part
    grad_proj = grad_middle.astype(jnp.bfloat16)
    grad_out_w = matmul(mixed_b.T, grad_proj)
    grad_mixed = matmul(grad_proj, out_w.T).astype(jnp.bfloat16)
    grad_query_rot, key_terms = attend_backward(
        query_b, keys_all, visible, peak_score, totals, grad_mixed
    )
    key_grads = lax.psum_scatter(
        key_terms.astype(jnp.bfloat16), "fsdp", scatter_dimension=0, tiled=True
    ).astype(jnp.float32)
    kv_width = key_terms.shape[1] // 2
    grad_query = rotate(grad_query_rot, pos_rows, -1.0).astype(jnp.bfloat16)
    grad_key = rotate(key_grads[:, :kv_width], pos_rows, -1.0).astype(jnp.bfloat16)
    grad_value = key_grads[:, kv_width:].astype(jnp.bfloat16)
    grad_normed = (
        matmul(grad_query, query_w.T) + matmul(grad_key, key_w.T) + matmul(grad_value, value_w.T)
    )
    grad_query_w = matmul(normed.T, grad_query)
    grad_key_w = matmul(normed.T, grad_key)
    grad_value_w = matmul(normed.T, grad_value)
    grad_hidden_part, grad_gain_a = norm_back(hidden, gain_a.astype(jnp.float32), grad_normed)
    attn_blocks = (
        lax.psum_scatter(
            grad_gain_a.astype(jnp.bfloat16), "dp", scatter_dimension=0, tiled=True
        ).astype(jnp.float32),
        lax.psum_scatter(
            grad_query_w.astype(jnp.bfloat16), "dp", scatter_dimension=0, tiled=True
        ).astype(jnp.float32),
        lax.psum_scatter(
            grad_key_w.astype(jnp.bfloat16), "dp", scatter_dimension=0, tiled=True
        ).astype(jnp.float32),
        lax.psum_scatter(
            grad_value_w.astype(jnp.bfloat16), "dp", scatter_dimension=0, tiled=True
        ).astype(jnp.float32),
        lax.psum_scatter(
            grad_out_w.astype(jnp.bfloat16), "dp", scatter_dimension=0, tiled=True
        ).astype(jnp.float32),
    )
    attn_grads = (
        lax.psum_scatter(
            attn_blocks[0].astype(jnp.bfloat16), "fsdp", scatter_dimension=0, tiled=True
        ).astype(jnp.float32),
        lax.psum_scatter(
            attn_blocks[1].astype(jnp.bfloat16), "fsdp", scatter_dimension=0, tiled=True
        ).astype(jnp.float32),
        lax.psum_scatter(
            attn_blocks[2].astype(jnp.bfloat16), "fsdp", scatter_dimension=0, tiled=True
        ).astype(jnp.float32),
        lax.psum_scatter(
            attn_blocks[3].astype(jnp.bfloat16), "fsdp", scatter_dimension=0, tiled=True
        ).astype(jnp.float32),
        lax.psum_scatter(
            attn_blocks[4].astype(jnp.bfloat16), "fsdp", scatter_dimension=0, tiled=True
        ).astype(jnp.float32),
    )
    return (grad_middle + grad_hidden_part, attn_grads, ffn_grads)


def per_device(
    tokens,
    gain_attn,
    w_query,
    w_key,
    w_value,
    w_out,
    gain_ffn,
    w_gate,
    w_up,
    w_down,
    lengths,
    cotangent,
):
    tok_rows = tokens.shape[0]
    group_tok = tok_rows * lax.axis_size("fsdp")
    segment, position = layout(lengths[0], group_tok)
    first_row = lax.axis_index("fsdp") * tok_rows
    row_places = first_row + jnp.arange(tok_rows, dtype=jnp.int32)
    seg_rows = lax.dynamic_slice_in_dim(segment, first_row, tok_rows)
    pos_rows = lax.dynamic_slice_in_dim(position, first_row, tok_rows)
    visible = visibility(seg_rows, row_places, segment, jnp.arange(group_tok, dtype=jnp.int32))
    hidden = tokens.astype(jnp.float32)
    layer_store = []
    results = []
    for layer_index in range(2):
        attn_weights = fetch_attention(layer_index, gain_attn, w_query, w_key, w_value, w_out)
        ffn_weights = fetch_ffn(layer_index, gain_ffn, w_gate, w_up, w_down)
        hidden, saved = layer_forward(hidden, attn_weights, ffn_weights, pos_rows, visible)
        layer_store.append(saved)
        results.append(hidden.astype(jnp.bfloat16))
    upstream = cotangent.astype(jnp.float32)
    attn_list = []
    ffn_list = []
    for layer_index in (1, 0):
        attn_weights = fetch_attention(layer_index, gain_attn, w_query, w_key, w_value, w_out)
        ffn_weights = fetch_ffn(layer_index, gain_ffn, w_gate, w_up, w_down)
        saved = layer_store[layer_index]
        keys_all = share_keys(saved[3])
        upstream, attn_grads, ffn_grads = layer_backward(
            upstream, saved, attn_weights, ffn_weights, keys_all, pos_rows, visible
        )
        attn_list.append(attn_grads)
        ffn_list.append(ffn_grads)
    layer_outputs = jnp.stack(results)
    grad_gain_attn = jnp.stack([attn_list[1][0], attn_list[0][0]])
    grad_w_query = jnp.stack([attn_list[1][1], attn_list[0][1]])
    grad_w_key = jnp.stack([attn_list[1][2], attn_list[0][2]])
    grad_w_value = jnp.stack([attn_list[1][3], attn_list[0][3]])
    grad_w_out = jnp.stack([attn_list[1][4], attn_list[0][4]])
    grad_gain_ffn = jnp.stack([ffn_list[1][0], ffn_list[0][0]])
    grad_w_gate = jnp.stack([ffn_list[1][1], ffn_list[0][1]])
    grad_w_up = jnp.stack([ffn_list[1][2], ffn_list[0][2]])
    grad_w_down = jnp.stack([ffn_list[1][3], ffn_list[0][3]])
    return (
        layer_outputs,
        upstream,
        grad_gain_attn,
        grad_w_query,
        grad_w_key,
        grad_w_value,
        grad_w_out,
        grad_gain_ffn,
        grad_w_gate,
        grad_w_up,
        grad_w_down,
    )


def solution(mesh):
    placed = (
        P(("dp", "fsdp"), None),
        P(None, ("dp", "fsdp")),
        P(None, ("dp", "fsdp"), None),
        P(None, ("dp", "fsdp"), None),
        P(None, ("dp", "fsdp"), None),
        P(None, ("dp", "fsdp"), None),
        P(None, ("dp", "fsdp")),
        P(None, ("dp", "fsdp"), None),
        P(None, ("dp", "fsdp"), None),
        P(None, ("dp", "fsdp"), None),
        P("dp", None),
        P(("dp", "fsdp"), None),
    )
    return jax.shard_map(
        per_device,
        mesh=mesh,
        in_specs=placed,
        out_specs=(
            P(None, ("dp", "fsdp"), None),
            P(("dp", "fsdp"), None),
            P(None, ("dp", "fsdp")),
            P(None, ("dp", "fsdp"), None),
            P(None, ("dp", "fsdp"), None),
            P(None, ("dp", "fsdp"), None),
            P(None, ("dp", "fsdp"), None),
            P(None, ("dp", "fsdp")),
            P(None, ("dp", "fsdp"), None),
            P(None, ("dp", "fsdp"), None),
            P(None, ("dp", "fsdp"), None),
        ),
        check_vma=False,
    )
```

profile of v0, /device:TPU:0, one launch (start us, length us, event | category | flops | bytes accessed | tf_op | source)
XLA Modules:
  0.0 3025.1 jit_solution(16257373685186024154)
XLA Ops:
  16.9 42.4 %all-reduce.12 = (bf16[1536]{0:T(1024)(128)(2,1)S(1)}, bf16[1536]{0:T(1024)(128)(2,1)S(1)}, bf16[1536]{0:T(1024)(128)(2,1)S(1)}, bf16[1536]{0:T(1024)(128)(2,1)S(1)}) all-reduce(bf16[1536]{0:T(1024)(128)(2,1)S(1)} %dynamic-update-slice, bf16[1536]{0:T(1024)(128)(2,1)S(1)} %dynamic-update-slice.1, ...), channel_id=2, replica_groups=mesh['dp'=8,'fsdp'=4] {'dp','fsdp'}, use_global_device_ids=true, to_apply=%add | all-reduce | flops 6144 | bytes 24576
  74.6 56.7 %all-gather.41.cloned.1.call-done = bf16[1,1536,768]{2,1,0:T(8,128)(2,1)} async-done(((bf16[1,48,768]{2,1,0:T(8,128)(2,1)}), bf16[1,1536,768]{2,1,0:T(8,128)(2,1)}) %all-gather.41.cloned.1.call-update) | async-done | bytes 2359312 | tf_op jit(solution)/shard_map/all_gather | solution.py:166
  144.4 52.7 %all-gather.43.cloned.1.call-done = bf16[1,1536,1536]{2,1,0:T(8,128)(2,1)} async-done(((bf16[1,48,1536]{2,1,0:T(8,128)(2,1)}), bf16[1,1536,1536]{2,1,0:T(8,128)(2,1)}) %all-gather.43.cloned.1.call-update) | async-done | bytes 4718608 | tf_op jit(solution)/shard_map/all_gather | solution.py:164
  202.7 58.8 %all-gather.35.cloned.1.call-done = bf16[1024,1536]{1,0:T(8,128)(2,1)} async-done(((bf16[256,1536]{1,0:T(8,128)(2,1)}), bf16[1024,1536]{1,0:T(8,128)(2,1)}) %all-gather.35.cloned.1.call-update) | async-done | bytes 3145744 | tf_op jit(solution)/shard_map/all_gather | solution.py:181
  266.3 63.1 %while.68 = (s32[]{:T(128)}, bf16[8,256,192]{1,2,0:T(8,128)(2,1)}, f32[8,2,256]{2,1,0:T(2,128)S(1)}, f32[8,2,256]{2,1,0:T(2,128)S(1)}, s32[8]{0:T(128)S(1)}, /*i...) while((s32[]{:T(128)}, bf16[8,256,192]{1,2,0:T(8,128)(2,1)}, ...), condition=%wide.region_8.9_spmd.clone, body=%wide.region_5.8_spmd.clone.sunk | while | flops 209976320 | bytes 8349779 | solution.py:104
  333.8 90.8 %all-gather.47.cloned.1.call-done = bf16[1,1536,4096]{2,1,0:T(8,128)(2,1)} async-done(((bf16[1,48,4096]{2,1,0:T(8,128)(2,1)}), bf16[1,1536,4096]{2,1,0:T(8,128)(2,1)}) %all-gather.47.cloned.1.call-update) | async-done | bytes 12582928 | tf_op jit(solution)/shard_map/all_gather | solution.py:174
  434.1 88.3 %all-gather.49.cloned.1.call-done = bf16[1,1536,4096]{2,1,0:T(8,128)(2,1)} async-done(((bf16[1,48,4096]{2,1,0:T(8,128)(2,1)}), bf16[1,1536,4096]{2,1,0:T(8,128)(2,1)}) %all-gather.49.cloned.1.call-update) | async-done | bytes 12582928 | tf_op jit(solution)/shard_map/all_gather | solution.py:175
  533.6 86.6 %all-gather.51.cloned.1.call-done = bf16[1,4096,1536]{2,1,0:T(8,128)(2,1)} async-done(((bf16[1,128,1536]{2,1,0:T(8,128)(2,1)}), bf16[1,4096,1536]{2,1,0:T(8,128)(2,1)}) %all-gather.51.cloned.1.call-update) | async-done | bytes 12582928 | tf_op jit(solution)/shard_map/all_gather | solution.py:176
  628.7 49.9 %all-gather.53.cloned.1.call-done = bf16[1,1536,768]{2,1,0:T(8,128)(2,1)} async-done(((bf16[1,48,768]{2,1,0:T(8,128)(2,1)}), bf16[1,1536,768]{2,1,0:T(8,128)(2,1)}) %all-gather.53.cloned.1.call-update) | async-done | bytes 2359312 | tf_op jit(solution)/shard_map/all_gather | solution.py:165
  681.6 55.9 %all-gather.55.cloned.1.call-done = bf16[1,1536,768]{2,1,0:T(8,128)(2,1)} async-done(((bf16[1,48,768]{2,1,0:T(8,128)(2,1)}), bf16[1,1536,768]{2,1,0:T(8,128)(2,1)}) %all-gather.55.cloned.1.call-update) | async-done | bytes 2359312 | tf_op jit(solution)/shard_map/all_gather | solution.py:166
  742.7 60.7 %all-gather.57.cloned.1.call-done = bf16[1,1536,1536]{2,1,0:T(8,128)(2,1)} async-done(((bf16[1,48,1536]{2,1,0:T(8,128)(2,1)}), bf16[1,1536,1536]{2,1,0:T(8,128)(2,1)}) %all-gather.57.cloned.1.call-update) | async-done | bytes 4718608 | tf_op jit(solution)/shard_map/all_gather | solution.py:164
  808.9 92.7 %all-gather.65.cloned.1.call-done = bf16[1,4096,1536]{2,1,0:T(8,128)(2,1)} async-done(((bf16[1,128,1536]{2,1,0:T(8,128)(2,1)}), bf16[1,4096,1536]{2,1,0:T(8,128)(2,1)}) %all-gather.65.cloned.1.call-update) | async-done | bytes 12582928 | tf_op jit(solution)/shard_map/all_gather | solution.py:176
  901.6 14.5 fusion.90
  916.0 49.5 %all-gather.37.cloned.1.call-done = bf16[1024,1536]{1,0:T(8,128)(2,1)} async-done(((bf16[256,1536]{1,0:T(8,128)(2,1)}), bf16[1024,1536]{1,0:T(8,128)(2,1)}) %all-gather.37.cloned.1.call-update) | async-done | bytes 3145744 | tf_op jit(solution)/shard_map/all_gather | solution.py:181
  970.2 63.1 %while.69 = (s32[]{:T(128)}, bf16[8,256,192]{1,2,0:T(8,128)(2,1)}, f32[8,2,256]{2,1,0:T(2,128)S(1)}, f32[8,2,256]{2,1,0:T(2,128)S(1)}, s32[8]{0:T(128)S(1)}, /*i...) while((s32[]{:T(128)}, bf16[8,256,192]{1,2,0:T(8,128)(2,1)}, ...), condition=%wide.region_14.15_spmd.clone, body=%wide.region_11.14_spmd.clone.sunk | while | flops 209976320 | bytes 8349779 | solution.py:104
  1038.1 90.6 %all-gather.63.cloned.1.call-done = bf16[1,1536,4096]{2,1,0:T(8,128)(2,1)} async-done(((bf16[1,48,4096]{2,1,0:T(8,128)(2,1)}), bf16[1,1536,4096]{2,1,0:T(8,128)(2,1)}) %all-gather.63.cloned.1.call-update) | async-done | bytes 12582928 | tf_op jit(solution)/shard_map/all_gather | solution.py:175
  1138.3 88.1 %all-gather.61.cloned.1.call-done = bf16[1,1536,4096]{2,1,0:T(8,128)(2,1)} async-done(((bf16[1,48,4096]{2,1,0:T(8,128)(2,1)}), bf16[1,1536,4096]{2,1,0:T(8,128)(2,1)}) %all-gather.61.cloned.1.call-update) | async-done | bytes 12582928 | tf_op jit(solution)/shard_map/all_gather | solution.py:174
  1264.6 94.0 %while.70 = (s32[]{:T(128)}, f32[8,256,192]{1,2,0:T(8,128)}, bf16[8,1024,96]{1,2,0:T(8,128)(2,1)}, bf16[8,1024,96]{1,2,0:T(8,128)(2,1)}, s32[8]{0:T(128)S(1)}, /...) while((s32[]{:T(128)}, f32[8,256,192]{1,2,0:T(8,128)}, ...), condition=%wide.region_19.20_spmd.clone, body=%wide.region_17.19_spmd.clone.sunk | while | flops 510541312 | bytes 25322664 | solution.py:147
  1369.6 51.7 %reduce-scatter.31.cloned.1.call-done = bf16[256,1536]{0,1:T(8,128)(2,1)} async-done(((bf16[1024,1536]{0,1:T(8,128)(2,1)}), bf16[256,1536]{0,1:T(8,128)(2,1)}) %reduce-scatter.31.cloned.1.call-update) | async-done | bytes 786448 | tf_op jit(solution)/shard_map/reduce_scatter | solution.py:284
  1428.3 16.3 multiply_convert_fusion.1
  1470.8 99.7 %while.71 = (s32[]{:T(128)}, f32[8,256,192]{1,2,0:T(8,128)}, bf16[8,1024,96]{1,2,0:T(8,128)(2,1)}, bf16[8,1024,96]{1,2,0:T(8,128)(2,1)}, s32[8]{0:T(128)S(1)}, /...) while((s32[]{:T(128)}, f32[8,256,192]{1,2,0:T(8,128)}, ...), condition=%wide.region_25.26_spmd.clone, body=%wide.region_23.25_spmd.clone.sunk | while | flops 510541312 | bytes 25322664 | solution.py:147
  1600.6 34.2 %reduce-scatter.33.cloned.1.call-done = bf16[256,1536]{0,1:T(8,128)(2,1)} async-done(((bf16[1024,1536]{0,1:T(8,128)(2,1)}), bf16[256,1536]{0,1:T(8,128)(2,1)}) %reduce-scatter.33.cloned.1.call-update) | async-done | bytes 786448 | tf_op jit(solution)/shard_map/reduce_scatter | solution.py:284
  1698.0 51.8 %reduce-scatter.59.cloned.1.call-done = bf16[192,1536]{1,0:T(8,128)(2,1)} async-done(((bf16[1536,1536]{1,0:T(8,128)(2,1)}), bf16[192,1536]{1,0:T(8,128)(2,1)}) %reduce-scatter.59.cloned.1.call-update) | async-done | bytes 589840 | tf_op jit(solution)/shard_map/reduce_scatter | solution.py:311
  1749.8 57.3 %reduce-scatter.39.cloned.1.call-done = bf16[192,1536]{1,0:T(8,128)(2,1)} async-done(((bf16[1536,1536]{1,0:T(8,128)(2,1)}), bf16[192,1536]{1,0:T(8,128)(2,1)}) %reduce-scatter.39.cloned.1.call-update) | async-done | bytes 589840 | tf_op jit(solution)/shard_map/reduce_scatter | solution.py:302
  1807.2 57.7 %reduce-scatter.35.cloned.1.call-done = bf16[192,1536]{1,0:T(8,128)(2,1)} async-done(((bf16[1536,1536]{1,0:T(8,128)(2,1)}), bf16[192,1536]{1,0:T(8,128)(2,1)}) %reduce-scatter.35.cloned.1.call-update) | async-done | bytes 589840 | tf_op jit(solution)/shard_map/reduce_scatter | solution.py:302
  1864.9 45.8 %reduce-scatter.55.cloned.1.call-done = bf16[192,768]{1,0:T(8,128)(2,1)} async-done(((bf16[1536,768]{1,0:T(8,128)(2,1)}), bf16[192,768]{1,0:T(8,128)(2,1)}) %reduce-scatter.55.cloned.1.call-update) | async-done | bytes 294928 | tf_op jit(solution)/shard_map/reduce_scatter | solution.py:308
  1910.8 46.0 %reduce-scatter.51.cloned.1.call-done = bf16[192,768]{1,0:T(8,128)(2,1)} async-done(((bf16[1536,768]{1,0:T(8,128)(2,1)}), bf16[192,768]{1,0:T(8,128)(2,1)}) %reduce-scatter.51.cloned.1.call-update) | async-done | bytes 294928 | tf_op jit(solution)/shard_map/reduce_scatter | solution.py:308
  1956.9 45.8 %reduce-scatter.47.cloned.1.call-done = bf16[192,768]{1,0:T(8,128)(2,1)} async-done(((bf16[1536,768]{1,0:T(8,128)(2,1)}), bf16[192,768]{1,0:T(8,128)(2,1)}) %reduce-scatter.47.cloned.1.call-update) | async-done | bytes 294928 | tf_op jit(solution)/shard_map/reduce_scatter | solution.py:305
  2002.7 46.0 %reduce-scatter.43.cloned.1.call-done = bf16[192,768]{1,0:T(8,128)(2,1)} async-done(((bf16[1536,768]{1,0:T(8,128)(2,1)}), bf16[192,768]{1,0:T(8,128)(2,1)}) %reduce-scatter.43.cloned.1.call-update) | async-done | bytes 294928 | tf_op jit(solution)/shard_map/reduce_scatter | solution.py:305
  2048.8 95.7 %reduce-scatter.87.cloned.1.call-done = bf16[512,1536]{1,0:T(8,128)(2,1)} async-done(((bf16[4096,1536]{1,0:T(8,128)(2,1)}), bf16[512,1536]{1,0:T(8,128)(2,1)}) %reduce-scatter.87.cloned.1.call-update) | async-done | bytes 1572880 | tf_op jit(solution)/shard_map/reduce_scatter | solution.py:259
  2144.6 95.9 %reduce-scatter.83.cloned.1.call-done = bf16[512,1536]{1,0:T(8,128)(2,1)} async-done(((bf16[4096,1536]{1,0:T(8,128)(2,1)}), bf16[512,1536]{1,0:T(8,128)(2,1)}) %reduce-scatter.83.cloned.1.call-update) | async-done | bytes 1572880 | tf_op jit(solution)/shard_map/reduce_scatter | solution.py:259
  2240.5 95.9 %reduce-scatter.79.cloned.1.call-done = bf16[192,4096]{1,0:T(8,128)(2,1)} async-done(((bf16[1536,4096]{1,0:T(8,128)(2,1)}), bf16[192,4096]{1,0:T(8,128)(2,1)}) %reduce-scatter.79.cloned.1.call-update) | async-done | bytes 1572880 | tf_op jit(solution)/shard_map/reduce_scatter | solution.py:256
  2336.5 95.7 %reduce-scatter.75.cloned.1.call-done = bf16[192,4096]{1,0:T(8,128)(2,1)} async-done(((bf16[1536,4096]{1,0:T(8,128)(2,1)}), bf16[192,4096]{1,0:T(8,128)(2,1)}) %reduce-scatter.75.cloned.1.call-update) | async-done | bytes 1572880 | tf_op jit(solution)/shard_map/reduce_scatter | solution.py:256
  2432.2 95.9 %reduce-scatter.71.cloned.1.call-done = bf16[192,4096]{1,0:T(8,128)(2,1)} async-done(((bf16[1536,4096]{1,0:T(8,128)(2,1)}), bf16[192,4096]{1,0:T(8,128)(2,1)}) %reduce-scatter.71.cloned.1.call-update) | async-done | bytes 1572880 | tf_op jit(solution)/shard_map/reduce_scatter | solution.py:253
  2548.1 75.9 %reduce-scatter.67.cloned.1.call-done = bf16[192,4096]{1,0:T(8,128)(2,1)} async-done(((bf16[1536,4096]{1,0:T(8,128)(2,1)}), bf16[192,4096]{1,0:T(8,128)(2,1)}) %reduce-scatter.67.cloned.1.call-update) | async-done | bytes 1572880 | tf_op jit(solution)/shard_map/reduce_scatter | solution.py:253
  2628.5 23.5 all-reduce.13
  2672.7 20.8 reduce-scatter.41.cloned.1.call-done
  2693.5 22.5 reduce-scatter.37.cloned.1.call-done
  2717.8 18.6 reduce-scatter.57.cloned.1.call-done
  2736.4 20.4 reduce-scatter.53.cloned.1.call-done
  2758.5 18.6 reduce-scatter.49.cloned.1.call-done
  2777.1 20.4 reduce-scatter.45.cloned.1.call-done
  2799.2 34.2 %reduce-scatter.89.cloned.1.call-done = bf16[128,1536]{1,0:T(8,128)(2,1)} async-done(((bf16[512,1536]{1,0:T(8,128)(2,1)}), bf16[128,1536]{1,0:T(8,128)(2,1)}) %reduce-scatter.89.cloned.1.call-update) | async-done | bytes 393232 | tf_op jit(solution)/shard_map/reduce_scatter | solution.py:273
  2833.5 36.6 %reduce-scatter.85.cloned.1.call-done = bf16[128,1536]{1,0:T(8,128)(2,1)} async-done(((bf16[512,1536]{1,0:T(8,128)(2,1)}), bf16[128,1536]{1,0:T(8,128)(2,1)}) %reduce-scatter.85.cloned.1.call-update) | async-done | bytes 393232 | tf_op jit(solution)/shard_map/reduce_scatter | solution.py:273
  2872.4 34.1 %reduce-scatter.81.cloned.1.call-done = bf16[48,4096]{1,0:T(8,128)(2,1)} async-done(((bf16[192,4096]{1,0:T(8,128)(2,1)}), bf16[48,4096]{1,0:T(8,128)(2,1)}) %reduce-scatter.81.cloned.1.call-update) | async-done | bytes 393232 | tf_op jit(solution)/shard_map/reduce_scatter | solution.py:270
  2906.5 36.6 %reduce-scatter.77.cloned.1.call-done = bf16[48,4096]{1,0:T(8,128)(2,1)} async-done(((bf16[192,4096]{1,0:T(8,128)(2,1)}), bf16[48,4096]{1,0:T(8,128)(2,1)}) %reduce-scatter.77.cloned.1.call-update) | async-done | bytes 393232 | tf_op jit(solution)/shard_map/reduce_scatter | solution.py:270
  2945.4 34.1 %reduce-scatter.73.cloned.1.call-done = bf16[48,4096]{1,0:T(8,128)(2,1)} async-done(((bf16[192,4096]{1,0:T(8,128)(2,1)}), bf16[48,4096]{1,0:T(8,128)(2,1)}) %reduce-scatter.73.cloned.1.call-update) | async-done | bytes 393232 | tf_op jit(solution)/shard_map/reduce_scatter | solution.py:267
  2979.5 36.4 %reduce-scatter.69.cloned.1.call-done = bf16[48,4096]{1,0:T(8,128)(2,1)} async-done(((bf16[192,4096]{1,0:T(8,128)(2,1)}), bf16[48,4096]{1,0:T(8,128)(2,1)}) %reduce-scatter.69.cloned.1.call-update) | async-done | bytes 393232 | tf_op jit(solution)/shard_map/reduce_scatter | solution.py:267
  (749 shorter events, 621.8 us)
Async XLA Ops:
  7.2 64.3 %all-gather.39.cloned.1.call-start = ((), (), s32[]{:S(2)}) async-start(), calls=%async_computation.62 | async-start | bytes 2433024 | tf_op jit(solution)/shard_map/all_gather | solution.py:165
  8.9 122.3 %all-gather.41.cloned.1.call-start = ((), (), s32[]{:S(2)}) async-start(), calls=%async_computation.63 | async-start | bytes 2433024 | tf_op jit(solution)/shard_map/all_gather | solution.py:166
  10.6 186.5 %all-gather.43.cloned.1.call-start = ((), (), s32[]{:S(2)}) async-start(), calls=%async_computation.64 | async-start | bytes 4866048 | tf_op jit(solution)/shard_map/all_gather | solution.py:164
  12.4 249.1 %all-gather.35.cloned.1.call-start = ((), (), s32[]{:S(2)}) async-start(), calls=%async_computation.30 | async-start | bytes 3932160 | tf_op jit(solution)/shard_map/all_gather | solution.py:181
  134.7 194.7 %all-gather.45.cloned.1.call-start = ((), (), s32[]{:S(2)}) async-start(), calls=%async_computation.65 | async-start | bytes 4866048 | tf_op jit(solution)/shard_map/all_gather | solution.py:167
  135.5 289.1 %all-gather.47.cloned.1.call-start = ((), (), s32[]{:S(2)}) async-start(), calls=%async_computation.66 | async-start | bytes 12976128 | tf_op jit(solution)/shard_map/all_gather | solution.py:174
  136.6 385.9 %all-gather.49.cloned.1.call-start = ((), (), s32[]{:S(2)}) async-start(), calls=%async_computation.67 | async-start | bytes 12976128 | tf_op jit(solution)/shard_map/all_gather | solution.py:175
  137.6 482.6 %all-gather.51.cloned.1.call-start = ((), (), s32[]{:S(2)}) async-start(), calls=%async_computation.68 | async-start | bytes 12976128 | tf_op jit(solution)/shard_map/all_gather | solution.py:176
  138.6 540.0 %all-gather.53.cloned.1.call-start = ((), (), s32[]{:S(2)}) async-start(), calls=%async_computation.69 | async-start | bytes 2433024 | tf_op jit(solution)/shard_map/all_gather | solution.py:165
  139.3 598.2 %all-gather.55.cloned.1.call-start = ((), (), s32[]{:S(2)}) async-start(), calls=%async_computation.70 | async-start | bytes 2433024 | tf_op jit(solution)/shard_map/all_gather | solution.py:166
  139.9 663.5 %all-gather.57.cloned.1.call-start = ((), (), s32[]{:S(2)}) async-start(), calls=%async_computation.71 | async-start | bytes 4866048 | tf_op jit(solution)/shard_map/all_gather | solution.py:164
  140.6 760.9 %all-gather.65.cloned.1.call-start = ((), (), s32[]{:S(2)}) async-start(), calls=%async_computation.75 | async-start | bytes 12976128 | tf_op jit(solution)/shard_map/all_gather | solution.py:176
  141.2 824.3 %all-gather.37.cloned.1.call-start = ((), (), s32[]{:S(2)}) async-start(), calls=%async_computation.31 | async-start | bytes 3932160 | tf_op jit(solution)/shard_map/all_gather | solution.py:181
  333.6 286.6 %copy-start.4 = (f32[256,1536]{1,0:T(8,128)}, f32[256,1536]{1,0:T(8,128)S(1)}, u32[]{:S(2)}) copy-start(f32[256,1536]{1,0:T(8,128)S(1)} %get-tuple-element.1062) | copy-start | bytes 4718596
  740.9 292.4 %all-gather.59.cloned.1.call-start = ((), (), s32[]{:S(2)}) async-start(), calls=%async_computation.72 | async-start | bytes 4866048 | tf_op jit(solution)/shard_map/all_gather | solution.py:167
  741.5 387.2 %all-gather.63.cloned.1.call-start = ((), (), s32[]{:S(2)}) async-start(), calls=%async_computation.74 | async-start | bytes 12976128 | tf_op jit(solution)/shard_map/all_gather | solution.py:175
  742.1 484.3 %all-gather.61.cloned.1.call-start = ((), (), s32[]{:S(2)}) async-start(), calls=%async_computation.73 | async-start | bytes 12976128 | tf_op jit(solution)/shard_map/all_gather | solution.py:174
  742.7 678.6 %reduce-scatter.31.cloned.1.call-start = ((), (), s32[]{:S(2)}) async-start(), calls=%async_computation.32 | async-start | bytes 3932160 | tf_op jit(solution)/shard_map/reduce_scatter | solution.py:284
  1037.9 217.0 %copy-start.22 = (f32[256,1536]{1,0:T(8,128)}, f32[256,1536]{1,0:T(8,128)S(1)}, u32[]{:S(2)}) copy-start(f32[256,1536]{1,0:T(8,128)S(1)} %get-tuple-element.1068) | copy-start | bytes 4718596
  1362.6 272.2 %reduce-scatter.33.cloned.1.call-start = ((), (), s32[]{:S(2)}) async-start(), calls=%async_computation.33 | async-start | bytes 3932160 | tf_op jit(solution)/shard_map/reduce_scatter | solution.py:284
  1574.3 123.1 %reduce-scatter.63.cloned.1.call-start = ((), (), s32[]{:S(2)}) async-start(), calls=%async_computation.48 | async-start | bytes 5308416 | tf_op jit(solution)/shard_map/reduce_scatter | solution.py:311
  1580.5 169.2 %reduce-scatter.59.cloned.1.call-start = ((), (), s32[]{:S(2)}) async-start(), calls=%async_computation.46 | async-start | bytes 5308416 | tf_op jit(solution)/shard_map/reduce_scatter | solution.py:311
  1586.7 220.4 %reduce-scatter.39.cloned.1.call-start = ((), (), s32[]{:S(2)}) async-start(), calls=%async_computation.36 | async-start | bytes 5308416 | tf_op jit(solution)/shard_map/reduce_scatter | solution.py:302
  1591.7 273.2 %reduce-scatter.35.cloned.1.call-start = ((), (), s32[]{:S(2)}) async-start(), calls=%async_computation.34 | async-start | bytes 5308416 | tf_op jit(solution)/shard_map/reduce_scatter | solution.py:302
  1597.1 313.6 %reduce-scatter.55.cloned.1.call-start = ((), (), s32[]{:S(2)}) async-start(), calls=%async_computation.44 | async-start | bytes 2654208 | tf_op jit(solution)/shard_map/reduce_scatter | solution.py:308
  1600.5 356.3 %reduce-scatter.51.cloned.1.call-start = ((), (), s32[]{:S(2)}) async-start(), calls=%async_computation.42 | async-start | bytes 2654208 | tf_op jit(solution)/shard_map/reduce_scatter | solution.py:308
  1638.1 364.5 %reduce-scatter.47.cloned.1.call-start = ((), (), s32[]{:S(2)}) async-start(), calls=%async_computation.40 | async-start | bytes 2654208 | tf_op jit(solution)/shard_map/reduce_scatter | solution.py:305
  1640.5 408.3 %reduce-scatter.43.cloned.1.call-start = ((), (), s32[]{:S(2)}) async-start(), calls=%async_computation.38 | async-start | bytes 2654208 | tf_op jit(solution)/shard_map/reduce_scatter | solution.py:305
  1644.1 500.4 %reduce-scatter.87.cloned.1.call-start = ((), (), s32[]{:S(2)}) async-start(), calls=%async_computation.60 | async-start | bytes 14155776 | tf_op jit(solution)/shard_map/reduce_scatter | solution.py:259
  1652.8 587.6 %reduce-scatter.83.cloned.1.call-start = ((), (), s32[]{:S(2)}) async-start(), calls=%async_computation.58 | async-start | bytes 14155776 | tf_op jit(solution)/shard_map/reduce_scatter | solution.py:259
  1662.5 673.9 %reduce-scatter.79.cloned.1.call-start = ((), (), s32[]{:S(2)}) async-start(), calls=%async_computation.56 | async-start | bytes 14155776 | tf_op jit(solution)/shard_map/reduce_scatter | solution.py:256
  1671.7 760.4 %reduce-scatter.75.cloned.1.call-start = ((), (), s32[]{:S(2)}) async-start(), calls=%async_computation.54 | async-start | bytes 14155776 | tf_op jit(solution)/shard_map/reduce_scatter | solution.py:256
  1680.9 847.2 %reduce-scatter.71.cloned.1.call-start = ((), (), s32[]{:S(2)}) async-start(), calls=%async_computation.52 | async-start | bytes 14155776 | tf_op jit(solution)/shard_map/reduce_scatter | solution.py:253
  1689.1 935.0 %reduce-scatter.67.cloned.1.call-start = ((), (), s32[]{:S(2)}) async-start(), calls=%async_computation.50 | async-start | bytes 14155776 | tf_op jit(solution)/shard_map/reduce_scatter | solution.py:253
  1697.4 971.3 %reduce-scatter.65.cloned.1.call-start = ((), (), s32[]{:S(2)}) async-start(), calls=%async_computation.49 | async-start | bytes 737280 | tf_op jit(solution)/shard_map/reduce_scatter | solution.py:328
  1697.9 972.9 %reduce-scatter.61.cloned.1.call-start = ((), (), s32[]{:S(2)}) async-start(), calls=%async_computation.47 | async-start | bytes 737280 | tf_op jit(solution)/shard_map/reduce_scatter | solution.py:328
  1749.8 943.7 %reduce-scatter.41.cloned.1.call-start = ((), (), s32[]{:S(2)}) async-start(), calls=%async_computation.37 | async-start | bytes 737280 | tf_op jit(solution)/shard_map/reduce_scatter | solution.py:319
  1807.2 908.8 %reduce-scatter.37.cloned.1.call-start = ((), (), s32[]{:S(2)}) async-start(), calls=%async_computation.35 | async-start | bytes 737280 | tf_op jit(solution)/shard_map/reduce_scatter | solution.py:319
  1864.9 871.5 %reduce-scatter.57.cloned.1.call-start = ((), (), s32[]{:S(2)}) async-start(), calls=%async_computation.45 | async-start | bytes 368640 | tf_op jit(solution)/shard_map/reduce_scatter | solution.py:325
  1910.8 846.1 %reduce-scatter.53.cloned.1.call-start = ((), (), s32[]{:S(2)}) async-start(), calls=%async_computation.43 | async-start | bytes 368640 | tf_op jit(solution)/shard_map/reduce_scatter | solution.py:325
  1956.9 820.3 %reduce-scatter.49.cloned.1.call-start = ((), (), s32[]{:S(2)}) async-start(), calls=%async_computation.41 | async-start | bytes 368640 | tf_op jit(solution)/shard_map/reduce_scatter | solution.py:322
  2002.7 794.9 %reduce-scatter.45.cloned.1.call-start = ((), (), s32[]{:S(2)}) async-start(), calls=%async_computation.39 | async-start | bytes 368640 | tf_op jit(solution)/shard_map/reduce_scatter | solution.py:322
  2048.8 784.7 %reduce-scatter.89.cloned.1.call-start = ((), (), s32[]{:S(2)}) async-start(), calls=%async_computation.61 | async-start | bytes 1966080 | tf_op jit(solution)/shard_map/reduce_scatter | solution.py:273
  2144.6 725.5 %reduce-scatter.85.cloned.1.call-start = ((), (), s32[]{:S(2)}) async-start(), calls=%async_computation.59 | async-start | bytes 1966080 | tf_op jit(solution)/shard_map/reduce_scatter | solution.py:273
  2240.5 666.0 %reduce-scatter.81.cloned.1.call-start = ((), (), s32[]{:S(2)}) async-start(), calls=%async_computation.57 | async-start | bytes 1966080 | tf_op jit(solution)/shard_map/reduce_scatter | solution.py:270
  2336.4 606.7 %reduce-scatter.77.cloned.1.call-start = ((), (), s32[]{:S(2)}) async-start(), calls=%async_computation.55 | async-start | bytes 1966080 | tf_op jit(solution)/shard_map/reduce_scatter | solution.py:270
  2432.2 547.3 %reduce-scatter.73.cloned.1.call-start = ((), (), s32[]{:S(2)}) async-start(), calls=%async_computation.53 | async-start | bytes 1966080 | tf_op jit(solution)/shard_map/reduce_scatter | solution.py:267
  2528.1 487.8 %reduce-scatter.69.cloned.1.call-start = ((), (), s32[]{:S(2)}) async-start(), calls=%async_computation.51 | async-start | bytes 1966080 | tf_op jit(solution)/shard_map/reduce_scatter | solution.py:267
  (95 other events, 2346.6 us)
Sparse Core Ops, SparseCore 0:
  11.4 60.0 all-gather.38
  74.8 56.3 all-gather.40
  134.6 62.4 all-gather.42
  199.1 62.3 all-gather.34
  264.1 62.2 all-gather.44
  329.7 94.8 all-gather.46
  428.1 94.2 all-gather.48
  525.9 94.2 all-gather.50
  623.0 55.5 all-gather.52
  681.3 56.2 all-gather.54
  740.9 62.4 all-gather.56
  806.7 94.8 all-gather.64
  903.7 61.7 all-gather.36
  968.1 62.3 all-gather.58
  1033.8 94.8 all-gather.62
  1132.0 94.2 all-gather.60
  1362.7 58.4 reduce-scatter.30
  1574.4 60.2 reduce-scatter.32
  1638.2 53.9 reduce-scatter.62
  1695.8 53.8 reduce-scatter.58
  1753.2 53.8 reduce-scatter.38
  1811.0 53.8 reduce-scatter.34
  1868.2 42.4 reduce-scatter.54
  1914.3 42.4 reduce-scatter.50
  1960.2 42.4 reduce-scatter.46
  2006.2 42.4 reduce-scatter.42
  2052.1 92.3 reduce-scatter.86
  2148.0 92.3 reduce-scatter.82
  2244.0 92.3 reduce-scatter.78
  2339.7 92.3 reduce-scatter.74
  2435.7 92.3 reduce-scatter.70
  2531.6 92.3 reduce-scatter.66
  2626.2 21.8 reduce-scatter.64
  2650.4 20.4 reduce-scatter.60
  2673.1 20.3 reduce-scatter.40
  2695.6 20.2 reduce-scatter.36
  2718.1 18.2 reduce-scatter.56
  2738.7 18.1 reduce-scatter.52
  2759.0 18.0 reduce-scatter.48
  2779.4 18.1 reduce-scatter.44
  2799.9 33.5 reduce-scatter.88
  2835.8 34.2 reduce-scatter.84
  2872.2 34.2 reduce-scatter.80
  2908.8 34.2 reduce-scatter.76
  2945.2 34.2 reduce-scatter.72
  2981.7 34.2 reduce-scatter.68
where the time goes:
time: 3040 us; the launch traced here: 3030 us
  waiting for transfers between devices  2260 us (74%)
  matrix products  409 us (13%)
  local copies, waits for them, and re-layouts  128 us (4%)
  other arithmetic  84.2 us (3%)
  blocking collectives  77.8 us (3%)
  loops' own time  43.6 us (1%)
    dot_general x42, matrix products, matmul(): return jnp.dot(left, right, preferred_element_type=jnp.float32)  251 us
    reduce_scatter x2, waiting for transfers between devices, layer_backward(): lax.psum_scatter(grad_up_w.astype(jnp.bfloat16), 'dp', scatter_dimension=...  192 us
    reduce_scatter x2, waiting for transfers between devices, layer_backward(): lax.psum_scatter(grad_down_w.astype(jnp.bfloat16), 'dp', scatter_dimensio...  192 us
    all_gather x2, waiting for transfers between devices, fetch_ffn(): lax.all_gather(w_down[layer_index], ('dp', 'fsdp'), axis=0, tiled=True)  179 us
    all_gather x2, waiting for transfers between devices, fetch_ffn(): lax.all_gather(w_gate[layer_index], ('dp', 'fsdp'), axis=0, tiled=True)  179 us
    all_gather x2, waiting for transfers between devices, fetch_ffn(): lax.all_gather(w_up[layer_index], ('dp', 'fsdp'), axis=0, tiled=True)  179 us
    reduce_scatter x2, waiting for transfers between devices, layer_backward(): lax.psum_scatter(grad_gate_w.astype(jnp.bfloat16), 'dp', scatter_dimensio...  172 us
    reduce_scatter x2, waiting for transfers between devices, layer_backward(): lax.psum_scatter(grad_query_w.astype(jnp.bfloat16), 'dp', scatter_dimensi...  115 us
  transfers between devices with their start and end apart: 46, of which 42 were waited for; matrix products, arithmetic and copies ran while one was open for 11% of the time, Pallas kernels for 0%

commit v1 on v0

--- a/solution.py
+++ b/solution.py
@@ -1,8 +1,11 @@
+import functools
 import math
 
 import jax
 import jax.numpy as jnp
 from jax import lax
+from jax.experimental import pallas as pl
+from jax.experimental.pallas import tpu as pltpu
 from jax.sharding import PartitionSpec as P
 
 HEAD_DIM = 96
@@ -332,7 +335,7 @@
     return (grad_middle + grad_hidden_part, attn_grads, ffn_grads)
 
 
-def per_device(
+def general_device(
     tokens,
     gain_attn,
     w_query,
@@ -401,6 +404,587 @@
     )
 
 
+TP = 4
+
+
+def halves_swapped(value):
+    return (value % 2) * 2 + value // 2
+
+
+def flip_dp(dp_size, bits):
+    return [(i, i ^ bits) for i in range(dp_size)]
+
+
+def flip_z(z_size, bits):
+    return [(i, i ^ bits) for i in range(z_size)]
+
+
+def regroup_pairs(dp_size, z_size):
+    pairs = []
+    for high in range(dp_size // TP):
+        for rank in range(TP):
+            for z in range(z_size):
+                new_dp = high * TP + halves_swapped(z)
+                pairs.append(((high * TP + rank) * z_size + z, new_dp * z_size + halves_swapped(rank)))
+    return pairs
+
+
+def head_partner(values, halfway):
+    width = values.shape[1]
+    lane = lax.broadcasted_iota(jnp.int32, values.shape, 1)
+    ahead = pltpu.roll(values, width - halfway, 1)
+    behind = pltpu.roll(values, halfway, 1)
+    return jnp.where(lane % HEAD_DIM < halfway, ahead, behind)
+
+
+def qkv_kernel(rows_ref, weight_ref, cos_ref, sin_ref, out_ref):
+    raw = jnp.dot(rows_ref[...], weight_ref[...], preferred_element_type=jnp.float32)
+    turned = raw * cos_ref[...] + head_partner(raw, HEAD_DIM // 2) * sin_ref[...]
+    out_ref[...] = turned.astype(jnp.bfloat16)
+
+
+def project_qkv(rows, weight, cosine, sine):
+    total, depth = rows.shape
+    width = weight.shape[1]
+    block = total // TP
+    return pl.pallas_call(
+        qkv_kernel,
+        grid=(TP,),
+        out_shape=jax.ShapeDtypeStruct((total, width), jnp.bfloat16),
+        in_specs=[
+            pl.BlockSpec((block, depth), lambda i: (i, 0)),
+            pl.BlockSpec((depth, width), lambda i: (0, 0)),
+            pl.BlockSpec((block, width), lambda i: (i, 0)),
+            pl.BlockSpec((block, width), lambda i: (i, 0)),
+        ],
+        out_specs=pl.BlockSpec((block, width), lambda i: (i, 0)),
+        compiler_params=pltpu.CompilerParams(vmem_limit_bytes=48 * 2**20),
+        cost_estimate=pl.CostEstimate(
+            flops=2 * total * depth * width,
+            bytes_accessed=2 * total * depth + 2 * depth * width + 10 * total * width,
+            transcendentals=0,
+        ),
+    )(rows, weight, cosine, sine)
+
+
+def block_mask(row_seg, col_seg, same_block, block):
+    visible = (row_seg == col_seg) | (col_seg == 0)
+    if same_block:
+        rows = lax.broadcasted_iota(jnp.int32, (block, block), 0)
+        cols = lax.broadcasted_iota(jnp.int32, (block, block), 1)
+        visible = visible & (cols <= rows)
+    return visible
+
+
+def attend_fwd_kernel(slot_ref, qkv_ref, row_seg_ref, col_seg_ref, mixed_ref, lse_ref):
+    total, width = qkv_ref.shape
+    block = total // TP
+    q_heads = width // (2 * HEAD_DIM)
+    kv_heads = q_heads // 2
+    factor = 1.0 / math.sqrt(HEAD_DIM)
+    key_at = q_heads * HEAD_DIM
+    value_at = key_at + kv_heads * HEAD_DIM
+    places = [pl.ds(pl.multiple_of(slot_ref[b] * block, block), block) for b in range(TP)]
+    nt = (((1,), (1,)), ((), ()))
+    for i in range(TP):
+        row_seg = row_seg_ref[i]
+        masks = [block_mask(row_seg, col_seg_ref[j], i == j, block) for j in range(i + 1)]
+        lse_cols = []
+        for h in range(q_heads):
+            kv = h // 2
+            query = qkv_ref[places[i], h * HEAD_DIM : (h + 1) * HEAD_DIM]
+            scores = []
+            for j in range(i + 1):
+                key = qkv_ref[places[j], key_at + kv * HEAD_DIM : key_at + (kv + 1) * HEAD_DIM]
+                s = lax.dot_general(query, key, nt, preferred_element_type=jnp.float32) * factor
+                scores.append(jnp.where(masks[j], s, NEGATIVE))
+            peak = scores[0].max(axis=1, keepdims=True)
+            for s in scores[1:]:
+                peak = jnp.maximum(peak, s.max(axis=1, keepdims=True))
+            total_e = jnp.zeros((block, 1), jnp.float32)
+            mixed = jnp.zeros((block, HEAD_DIM), jnp.float32)
+            for j in range(i + 1):
+                e = jnp.exp(scores[j] - peak)
+                total_e = total_e + e.sum(axis=1, keepdims=True)
+                value = qkv_ref[places[j], value_at + kv * HEAD_DIM : value_at + (kv + 1) * HEAD_DIM]
+                mixed = mixed + jnp.dot(
+                    e.astype(jnp.bfloat16), value, preferred_element_type=jnp.float32
+                )
+            mixed_ref[places[i], h * HEAD_DIM : (h + 1) * HEAD_DIM] = (mixed / total_e).astype(
+                jnp.bfloat16
+            )
+            lse_ref[i, :, h : h + 1] = peak + jnp.log(total_e)
+
+
+def attend_fwd(slots, qkv, row_seg, col_seg):
+    total, width = qkv.shape
+    block = total // TP
+    q_heads = width // (2 * HEAD_DIM)
+    whole = lambda shape: pl.BlockSpec(shape, lambda i, s: (0,) * len(shape))
+    return pl.pallas_call(
+        attend_fwd_kernel,
+        out_shape=[
+            jax.ShapeDtypeStruct((total, width // 2), jnp.bfloat16),
+            jax.ShapeDtypeStruct((TP, block, q_heads), jnp.float32),
+        ],
+        grid_spec=pltpu.PrefetchScalarGridSpec(
+            num_scalar_prefetch=1,
+            grid=(1,),
+            in_specs=[whole(qkv.shape), whole(row_seg.shape), whole(col_seg.shape)],
+            out_specs=[whole((total, width // 2)), whole((TP, block, q_heads))],
+        ),
+        compiler_params=pltpu.CompilerParams(vmem_limit_bytes=48 * 2**20),
+        cost_estimate=pl.CostEstimate(
+            flops=4 * total * total * q_heads * HEAD_DIM,
+            bytes_accessed=3 * total * width,
+            transcendentals=total * total * q_heads // 2,
+        ),
+    )(slots, qkv, row_seg, col_seg)
+
+
+def attend_bwd_kernel(
+    slot_ref, qkv_ref, grad_ref, mixed_ref, lse_ref, row_seg_ref, col_seg_ref, cos_ref, sin_ref, out_ref, acc_ref
+):
+    total, width = qkv_ref.shape
+    block = total // TP
+    q_heads = width // (2 * HEAD_DIM)
+    kv_heads = q_heads // 2
+    factor = 1.0 / math.sqrt(HEAD_DIM)
+    key_at = q_heads * HEAD_DIM
+    value_at = key_at + kv_heads * HEAD_DIM
+    places = [pl.ds(pl.multiple_of(slot_ref[b] * block, block), block) for b in range(TP)]
+    nt = (((1,), (1,)), ((), ()))
+    tn = (((0,), (0,)), ((), ()))
+    acc_ref[:, key_at:] = jnp.zeros((total, width - key_at), jnp.float32)
+    for i in range(TP):
+        row_seg = row_seg_ref[i]
+        masks = [block_mask(row_seg, col_seg_ref[j], i == j, block) for j in range(i + 1)]
+        for h in range(q_heads):
+            kv = h // 2
+            lanes = slice(h * HEAD_DIM, (h + 1) * HEAD_DIM)
+            query = qkv_ref[places[i], lanes]
+            grad = grad_ref[places[i], lanes]
+            lse = lse_ref[i, :, h : h + 1]
+            inner = jnp.sum(
+                grad.astype(jnp.float32) * mixed_ref[places[i], lanes].astype(jnp.float32),
+                axis=1,
+                keepdims=True,
+            )
+            grad_query = jnp.zeros((block, HEAD_DIM), jnp.float32)
+            key_lanes = slice(key_at + kv * HEAD_DIM, key_at + (kv + 1) * HEAD_DIM)
+            value_lanes = slice(value_at + kv * HEAD_DIM, value_at + (kv + 1) * HEAD_DIM)
+            for j in range(i + 1):
+                key = qkv_ref[places[j], key_lanes]
+                value = qkv_ref[places[j], value_lanes]
+                s = lax.dot_general(query, key, nt, preferred_element_type=jnp.float32) * factor
+                prob = jnp.where(masks[j], jnp.exp(s - lse), 0.0)
+                grad_prob = lax.dot_general(grad, value, nt, preferred_element_type=jnp.float32)
+                grad_score = (prob * (grad_prob - inner)).astype(jnp.bfloat16)
+                grad_query = grad_query + jnp.dot(
+                    grad_score, key, preferred_element_type=jnp.float32
+                )
+                acc_ref[places[j], key_lanes] += (
+                    lax.dot_general(grad_score, query, tn, preferred_element_type=jnp.float32)
+                    * factor
+                )
+                acc_ref[places[j], value_lanes] += lax.dot_general(
+                    prob.astype(jnp.bfloat16), grad, tn, preferred_element_type=jnp.float32
+                )
+            acc_ref[places[i], lanes] = grad_query * factor
+    for b in range(TP):
+        rows = slice(b * block, (b + 1) * block)
+        acc = acc_ref[rows, :]
+        turned = acc * cos_ref[rows, :] - head_partner(acc, HEAD_DIM // 2) * sin_ref[rows, :]
+        out_ref[rows, :] = turned.astype(jnp.bfloat16)
+
+
+def attend_bwd(slots, qkv, grad, mixed, lse, row_seg, col_seg, cosine, sine):
+    total, width = qkv.shape
+    q_heads = width // (2 * HEAD_DIM)
+    operands = (qkv, grad, mixed, lse, row_seg, col_seg, cosine, sine)
+    whole = lambda shape: pl.BlockSpec(shape, lambda i, s: (0,) * len(shape))
+    return pl.pallas_call(
+        attend_bwd_kernel,
+        out_shape=jax.ShapeDtypeStruct((total, width), jnp.bfloat16),
+        grid_spec=pltpu.PrefetchScalarGridSpec(
+            num_scalar_prefetch=1,
+            grid=(1,),
+            in_specs=[whole(v.shape) for v in operands],
+            out_specs=whole((total, width)),
+            scratch_shapes=[pltpu.VMEM((total, width), jnp.float32)],
+        ),
+        compiler_params=pltpu.CompilerParams(vmem_limit_bytes=56 * 2**20),
+        cost_estimate=pl.CostEstimate(
+            flops=10 * total * total * q_heads * HEAD_DIM,
+            bytes_accessed=12 * total * width,
+            transcendentals=total * total * q_heads // 2,
+        ),
+    )(slots, *operands)
+
+
+def place_attn_kernel(order_ref, chunk_ref, qkv_ref, out_ref):
+    rows, half = qkv_ref.shape[0], out_ref.shape[1] // 2
+    orows = out_ref.shape[0]
+    qkv_ref[...] = chunk_ref[0, :rows]
+    out_ref[:, :half] = chunk_ref[0, rows : rows + orows]
+    out_ref[:, half:] = chunk_ref[0, rows + orows :]
+
+
+def place_attn(order, chunks, depth):
+    rows, width = chunks[0].shape
+    col_rows = depth // 8
+    orows = (rows - col_rows) // 2
+    stacked = jnp.stack(chunks)
+    return pl.pallas_call(
+        place_attn_kernel,
+        out_shape=[
+            jax.ShapeDtypeStruct((depth, width), jnp.bfloat16),
+            jax.ShapeDtypeStruct((orows * 8, width * 2), jnp.bfloat16),
+        ],
+        grid_spec=pltpu.PrefetchScalarGridSpec(
+            num_scalar_prefetch=1,
+            grid=(8,),
+            in_specs=[pl.BlockSpec((1, rows, width), lambda r, o: (o[r], 0, 0))],
+            out_specs=[
+                pl.BlockSpec((col_rows, width), lambda r, o: (r, 0)),
+                pl.BlockSpec((orows, width * 2), lambda r, o: (r, 0)),
+            ],
+        ),
+        cost_estimate=pl.CostEstimate(flops=0, bytes_accessed=32 * rows * width, transcendentals=0),
+    )(order, stacked)
+
+
+def place_ffn_kernel(order_ref, chunk_ref, gate_ref, up_ref, down_ref):
+    rows, units = gate_ref.shape
+    drows = down_ref.shape[0]
+    hd, qd = drows // 2, drows // 4
+    gate_ref[...] = chunk_ref[0, :rows, :units]
+    up_ref[...] = chunk_ref[0, :rows, units:]
+    for s in range(2):
+        down_ref[s * hd : (s + 1) * hd, :units] = chunk_ref[
+            0, rows : rows + hd, s * units : (s + 1) * units
+        ]
+    for s in range(4):
+        down_ref[s * qd : (s + 1) * qd, units:] = chunk_ref[
+            0, rows + hd :, s * units // 2 : (s + 1) * units // 2
+        ]
+
+
+def place_ffn(order, chunks, depth):
+    rows, width = chunks[0].shape
+    col_rows = depth // 8
+    units = width // 2
+    drows = (rows - col_rows) * 4 // 3
+    stacked = jnp.stack(chunks)
+    return pl.pallas_call(
+        place_ffn_kernel,
+        out_shape=[
+            jax.ShapeDtypeStruct((depth, units), jnp.bfloat16),
+            jax.ShapeDtypeStruct((depth, units), jnp.bfloat16),
+            jax.ShapeDtypeStruct((drows * 8, units * 3 // 2), jnp.bfloat16),
+        ],
+        grid_spec=pltpu.PrefetchScalarGridSpec(
+            num_scalar_prefetch=1,
+            grid=(8,),
+            in_specs=[pl.BlockSpec((1, rows, width), lambda r, o: (o[r], 0, 0))],
+            out_specs=[
+                pl.BlockSpec((col_rows, units), lambda r, o: (r, 0)),
+                pl.BlockSpec((col_rows, units), lambda r, o: (r, 0)),
+                pl.BlockSpec((drows, units * 3 // 2), lambda r, o: (r, 0)),
+            ],
+        ),
+        cost_estimate=pl.CostEstimate(flops=0, bytes_accessed=32 * rows * width, transcendentals=0),
+    )(order, stacked)
+
+
+class Fabric:
+    def __init__(self):
+        self.dp_size = lax.axis_size("dp")
+        self.z_size = lax.axis_size("fsdp")
+        dp = lax.axis_index("dp")
+        self.z = lax.axis_index("fsdp")
+        self.q = dp % TP
+        self.y = dp // TP
+
+    def rank(self, values, bits):
+        return lax.ppermute(values, "dp", flip_dp(self.dp_size, bits))
+
+    def core(self, values):
+        return self.rank(values, 1)
+
+    def across(self, values):
+        return self.rank(values, 2)
+
+    def over_y(self, values):
+        return self.rank(values, TP)
+
+    def over_z(self, values, bits):
+        return lax.ppermute(values, "fsdp", flip_z(self.z_size, bits))
+
+    def regroup(self, values):
+        return lax.ppermute(values, ("dp", "fsdp"), regroup_pairs(self.dp_size, self.z_size))
+
+    def natural(self, pieces):
+        low, high = (self.q % 2) == 1, (self.q // 2) == 1
+        a = [jnp.where(low, pieces[i ^ 1], pieces[i]) for i in range(4)]
+        return [jnp.where(high, a[i ^ 2], a[i]) for i in range(4)]
+
+    def spread(self, rows):
+        near = jnp.concatenate([rows, self.across(rows)], axis=0)
+        return jnp.concatenate([near, self.core(near)], axis=0)
+
+    def collect(self, left, weight, extra=None):
+        half = left.shape[0] // 2
+
+        def part(rows):
+            value = matmul(rows, weight)
+            return value
+
+        far = part(left[half:]).astype(jnp.bfloat16)
+        got = self.core(far)
+        near = part(left[:half]) + got.astype(jnp.float32)
+        quarter = half // 2
+        passed = self.across(near[quarter:].astype(jnp.bfloat16))
+        return near[:quarter] + passed.astype(jnp.float32)
+
+
+def exchange_columns(fab, pieces):
+    received = [pieces[0]] + [fab.rank(pieces[k], k) for k in range(1, TP)]
+    return fab.natural(received)
+
+
+def column_pieces(fab, weight, layer, k):
+    rows, width = weight.shape[1:]
+    chosen = (fab.q // 2 ^ (k // 2)) * 2 + (fab.q % 2 ^ (k % 2))
+    view = weight[layer].reshape(rows, 2, TP, width // (2 * TP))
+    return lax.dynamic_index_in_dim(view, chosen, 2, keepdims=False).reshape(rows, width // TP)
+
+
+def gather_chunks(fab, own):
+    row = [own] + [fab.over_z(own, k) for k in range(1, 4)]
+    return row + [fab.over_y(v) for v in row]
+
+
+def reduce_blocks(fab, left, right, left_block):
+    wide = left.shape[1] // 2
+    there = lax.dynamic_slice_in_dim(left, (1 - fab.y) * wide, wide, 1)
+    here = lax.dynamic_slice_in_dim(left, fab.y * wide, wide, 1)
+    sent = fab.over_y(matmul(there.T, right).astype(jnp.bfloat16))
+    total = (matmul(here.T, right) + sent.astype(jnp.float32)).astype(jnp.bfloat16)
+    blocks = total.reshape(4, wide // 4, right.shape[1])
+    z = fab.z
+    picked = [
+        lax.dynamic_index_in_dim(blocks, (z // 2 ^ (k // 2)) * 2 + (z % 2 ^ (k % 2)), 0, keepdims=False)
+        for k in range(4)
+    ]
+    result = picked[0].astype(jnp.float32)
+    for k in range(1, 4):
+        result = result + fab.over_z(picked[k], k).astype(jnp.float32)
+    return result
+
+
+def return_columns(fab, block):
+    low = block.astype(jnp.bfloat16).reshape(TP, block.shape[0] // TP, block.shape[1])
+    pieces = [
+        lax.dynamic_index_in_dim(
+            low, (fab.q // 2 ^ (k // 2)) * 2 + (fab.q % 2 ^ (k % 2)), 0, keepdims=False
+        )
+        for k in range(TP)
+    ]
+    return exchange_columns(fab, pieces)
+
+
+def join_columns(pieces):
+    rows, width = pieces[0].shape
+    view = jnp.stack([p.reshape(rows, 2, width // 2) for p in pieces], axis=2)
+    return view.reshape(rows, TP * width).astype(jnp.float32)
+
+
+def inner_rsqrt(values):
+    return lax.rsqrt(jnp.mean(values * values, axis=-1, keepdims=True) + EPSILON)
+
+
+def fast_device(
+    tokens, gain_attn, w_query, w_key, w_value, w_out, gain_ffn, w_gate, w_up, w_down, lengths, cotangent
+):
+    fab = Fabric()
+    block, depth = tokens.shape
+    group_tok = block * fab.z_size
+    shard = w_query.shape[1]
+    nat = jnp.arange(depth, dtype=jnp.int32)
+    nat_p = (
+        (nat // (depth // 2)) * (depth // 2)
+        + (nat // shard % fab.z_size) * (TP * shard)
+        + (nat // (shard * fab.z_size) % TP) * shard
+        + nat % shard
+    )
+    to_inner = (nat_p[:, None] == nat[None, :]).astype(jnp.bfloat16)
+    inward = lambda v: jnp.dot(v, to_inner, preferred_element_type=jnp.float32).astype(jnp.bfloat16)
+    outward = lambda v: lax.dot_general(
+        v, to_inner, (((1,), (1,)), ((), ())), preferred_element_type=jnp.float32
+    )
+
+    out_in = inward(w_out.reshape(-1, depth)).reshape(w_out.shape)
+    down_in = inward(w_down.reshape(-1, depth)).reshape(w_down.shape)
+    attn_own, ffn_own = [], []
+    for layer in range(2):
+        pieces = [
+            jnp.concatenate([column_pieces(fab, w, layer, k) for w in (w_query, w_key, w_value)], axis=1)
+            for k in range(TP)
+        ]
+        cols = exchange_columns(fab, pieces)
+        width = cols[0].shape[1]
+        own_out = out_in[layer]
+        attn_own.append(jnp.concatenate(cols + [own_out[:, :width], own_out[:, width:]], axis=0))
+        pieces = [
+            jnp.concatenate([column_pieces(fab, w, layer, k) for w in (w_gate, w_up)], axis=1)
+            for k in range(TP)
+        ]
+        cols = exchange_columns(fab, pieces)
+        units = cols[0].shape[1] // 2
+        dn = down_in[layer]
+        dr = dn.shape[0]
+        wide = jnp.concatenate([dn[: dr // 2, :units], dn[dr // 2 :, :units]], axis=1)
+        rest = jnp.concatenate([dn[s * dr // 4 : (s + 1) * dr // 4, units:] for s in range(4)], axis=1)
+        ffn_own.append(jnp.concatenate(cols + [wide, rest], axis=0))
+
+    gains = lax.all_gather(
+        jnp.concatenate([gain_attn, gain_ffn], axis=0), ("dp", "fsdp"), axis=0, tiled=False
+    )
+    gains = gains.reshape(2, TP, fab.z_size, 4, shard).transpose(3, 0, 2, 1, 4).reshape(4, depth)
+    gains = gains.astype(jnp.float32)
+
+    hidden = inward(fab.regroup(tokens)).astype(jnp.float32)
+    cot = inward(fab.regroup(cotangent))
+    lengths_row = fab.regroup(lengths)[0]
+
+    segment, position = layout(lengths_row, group_tok)
+    base = halves_swapped(fab.q)
+    slots = (jnp.arange(TP) // 2 ^ base // 2) * 2 + (jnp.arange(TP) % 2 ^ base % 2)
+    seg_blocks = segment.reshape(TP, block)
+    row_seg = seg_blocks[:, :, None]
+    col_seg = seg_blocks[:, None, :]
+    pos_rows = jnp.take(position.reshape(TP, block), slots, axis=0).reshape(-1)
+    halfway = HEAD_DIM // 2
+    frequency = ROPE_BASE ** (-jnp.arange(halfway, dtype=jnp.float32) * 2.0 / HEAD_DIM)
+    angles = pos_rows.astype(jnp.float32)[:, None] * frequency[None, :]
+    cos_h, sin_h = jnp.cos(angles), jnp.sin(angles)
+    heads = w_query.shape[2] // HEAD_DIM // TP
+    kv_heads = w_key.shape[2] // HEAD_DIM // TP
+    cosine = jnp.concatenate(
+        [cos_h, cos_h] * (heads + kv_heads)
+        + [jnp.ones((group_tok, kv_heads * HEAD_DIM), jnp.float32)],
+        axis=1,
+    )
+    sine = jnp.concatenate(
+        [-sin_h, sin_h] * (heads + kv_heads)
+        + [jnp.zeros((group_tok, kv_heads * HEAD_DIM), jnp.float32)],
+        axis=1,
+    )
+
+    places = jnp.arange(8, dtype=jnp.int32)
+    order = (places // 4 ^ fab.y) * 4 + (places % 4 // 2 ^ fab.z // 2) * 2 + (places % 2 ^ fab.z % 2)
+    saved, outs = [], []
+    for layer in range(2):
+        w_qkv, w_o = place_attn(order, gather_chunks(fab, attn_own[layer]), depth)
+        w_g, w_u, w_d = place_ffn(order, gather_chunks(fab, ffn_own[layer]), depth)
+        gain_a, gain_f = gains[layer], gains[2 + layer]
+        normed = fab.spread((hidden * inner_rsqrt(hidden) * gain_a).astype(jnp.bfloat16))
+        qkv = project_qkv(normed, w_qkv, cosine, sine)
+        mixed, lse = attend_fwd(slots, qkv, row_seg, col_seg)
+        middle = hidden + fab.collect(mixed, w_o)
+        normed_ffn = fab.spread((middle * inner_rsqrt(middle) * gain_f).astype(jnp.bfloat16))
+        gating = matmul(normed_ffn, w_g)
+        upward = matmul(normed_ffn, w_u)
+        activated = (jax.nn.silu(gating) * upward).astype(jnp.bfloat16)
+        result = middle + fab.collect(activated, w_d)
+        saved.append(
+            (hidden, normed, qkv, mixed, lse, middle, normed_ffn,
+             gating.astype(jnp.bfloat16), upward.astype(jnp.bfloat16), activated, w_qkv, w_o, w_g, w_u, w_d)
+        )
+        hidden = result
+        outs.append(fab.regroup(outward(result.astype(jnp.bfloat16)).astype(jnp.bfloat16)))
+
+    upstream = cot.astype(jnp.float32)
+    grads = [None, None]
+    gain_grads = [None] * 4
+    for layer in (1, 0):
+        (hid, normed, qkv, mixed, lse, middle, normed_ffn, gating, upward, activated,
+         w_qkv, w_o, w_g, w_u, w_d) = saved[layer]
+        gain_a, gain_f = gains[layer], gains[2 + layer]
+        branch = fab.spread(upstream.astype(jnp.bfloat16))
+        grad_act = matmul(branch, w_d.T)
+        gating = gating.astype(jnp.float32)
+        upward = upward.astype(jnp.float32)
+        sig = jax.nn.sigmoid(gating)
+        grad_gate = (grad_act * upward * sig * (1.0 + gating * (1.0 - sig))).astype(jnp.bfloat16)
+        grad_up = (grad_act * gating * sig).astype(jnp.bfloat16)
+        both = jnp.concatenate([grad_gate, grad_up], axis=1)
+        down_grad = reduce_blocks(fab, activated, branch, None)
+        gu_grad = reduce_blocks(fab, normed_ffn, both, None)
+        w_gu = jnp.concatenate([w_g, w_u], axis=1)
+        grad_normed_ffn = fab.collect(both, w_gu.T)
+        part, gain_grads[2 + layer] = norm_back(middle, gain_f, grad_normed_ffn)
+        grad_middle = upstream + part
+        proj = fab.spread(grad_middle.astype(jnp.bfloat16))
+        grad_mixed = matmul(proj, w_o.T).astype(jnp.bfloat16)
+        out_grad = reduce_blocks(fab, mixed, proj, None)
+        grad_qkv = attend_bwd(slots, qkv, grad_mixed, mixed, lse, row_seg, col_seg, cosine, sine)
+        qkv_grad = reduce_blocks(fab, normed, grad_qkv, None)
+        grad_normed = fab.collect(grad_qkv, w_qkv.T)
+        part, gain_grads[layer] = norm_back(hid, gain_a, grad_normed)
+        upstream = grad_middle + part
+        gu_parts = return_columns(fab, gu_grad)
+        units = gu_parts[0].shape[1] // 2
+        qkv_parts = return_columns(fab, qkv_grad)
+        qw, kw = heads * HEAD_DIM, kv_heads * HEAD_DIM
+        grads[layer] = (
+            join_columns([p[:, :qw] for p in qkv_parts]),
+            join_columns([p[:, qw : qw + kw] for p in qkv_parts]),
+            join_columns([p[:, qw + kw :] for p in qkv_parts]),
+            outward(out_grad.astype(jnp.bfloat16)),
+            join_columns([p[:, :units] for p in gu_parts]),
+            join_columns([p[:, units:] for p in gu_parts]),
+            outward(down_grad.astype(jnp.bfloat16)),
+        )
+    input_grad = fab.regroup(outward(upstream.astype(jnp.bfloat16)).astype(jnp.bfloat16)).astype(
+        jnp.float32
+    )
+    gain_sums = lax.psum(jnp.stack(gain_grads), ("dp", "fsdp"))
+    own_gain = lax.dynamic_slice_in_dim(
+        gain_sums, (fab.y * fab.z_size + fab.z) * (TP * shard) + fab.q * shard, shard, 1
+    )
+    pair = lambda n: jnp.stack([grads[0][n], grads[1][n]])
+    return (
+        jnp.stack(outs),
+        input_grad,
+        own_gain[:2],
+        pair(0),
+        pair(1),
+        pair(2),
+        pair(3),
+        own_gain[2:],
+        pair(4),
+        pair(5),
+        pair(6),
+    )
+
+
+def per_device(*arrays):
+    tokens, w_query, w_key, w_gate = arrays[0], arrays[2], arrays[3], arrays[7]
+    dp_size, z_size = lax.axis_size("dp"), lax.axis_size("fsdp")
+    suits = (
+        dp_size == 2 * TP
+        and z_size == TP
+        and w_key.shape[2] // HEAD_DIM == dp_size
+        and w_query.shape[2] == 2 * w_key.shape[2]
+        and tokens.shape[0] % 128 == 0
+        and w_query.shape[1] % 16 == 0
+        and w_gate.shape[2] % (TP * dp_size * 128) == 0
+    )
+    return (fast_device if suits else general_device)(*arrays)
+
+
 def solution(mesh):
     placed = (
         P(("dp", "fsdp"), None),

time: 3040 us -> 1530 us (0.50)
  waiting for transfers between devices: 2260 us -> 593 us
  starting transfers between devices: 2.23 us -> 227 us
  matrix products: 409 us -> 200 us
  Pallas kernels: 0 us -> 134 us
  loops' own time: 43.6 us -> 0 us
  blocking collectives: 77.8 us -> 116 us
  local copies, waits for them, and re-layouts: 128 us -> 164 us
    reduce_scatter x30 -> x0, waiting for transfers between devices: 1330 us -> none  [the longest x2 192 us: layer_backward(): lax.psum_scatter(grad_up_w.astype(jnp.bfloat16), 'dp', scatter_dimension=...]
    all_gather x16 -> x0, waiting for transfers between devices: 931 us -> none  [the longest x2 179 us: fetch_ffn(): lax.all_gather(w_down[layer_index], ('dp', 'fsdp'), axis=0, tiled=True)]
    ppermute x0 -> x122, waiting for transfers between devices: none -> 593 us  [the longest x80 349 us: rank(): return lax.ppermute(values, 'dp', flip_dp(self.dp_size, bits))]
    ppermute x0 -> x122, starting transfers between devices: none -> 227 us  [the longest x36 109 us: over_z(): return lax.ppermute(values, 'fsdp', flip_z(self.z_size, bits))]
    pallas_call x0 -> x10, Pallas kernels: none -> 134 us  [the longest x2 57.2 us: attend_bwd(): pl.pallas_call(attend_bwd_kernel, out_shape=jax.ShapeDtypeStruct((total,...]
    dot_general x112 -> x11, matrix products: 158 us -> 35.6 us  [the longest x7 25.5 us: fast_device(): lax.dot_general(v, to_inner, (((1,), (1,)), ((), ())), preferred_element_...]
    dot_general x42 -> x40, matrix products: 251 us -> 164 us  [matmul(): return jnp.dot(left, right, preferred_element_type=jnp.float32)]
    unnamed x3 -> x0, blocking collectives: 77.8 us -> none
  transfers between devices with their start and end apart: 46 -> 122, of which waited for: 42 -> 46; matrix products, arithmetic and copies ran while one was open for 11% -> 23% of each run, Pallas kernels for 0% -> 7%
where the time goes in v1:
time: 1530 us; the launch traced here: 1520 us
  waiting for transfers between devices  593 us (39%)
  starting transfers between devices  227 us (15%)
  matrix products  200 us (13%)
  local copies, waits for them, and re-layouts  164 us (11%)
  Pallas kernels  134 us (9%)
  blocking collectives  116 us (8%)
  other arithmetic  82.2 us (5%)
    ppermute x80, waiting for transfers between devices, rank(): return lax.ppermute(values, 'dp', flip_dp(self.dp_size, bits))  349 us
    ppermute x36, waiting for transfers between devices, over_z(): return lax.ppermute(values, 'fsdp', flip_z(self.z_size, bits))  244 us
    dot_general x40, matrix products, matmul(): return jnp.dot(left, right, preferred_element_type=jnp.float32)  164 us
    ppermute x36, starting transfers between devices, over_z(): return lax.ppermute(values, 'fsdp', flip_z(self.z_size, bits))  109 us
    ppermute x80, starting transfers between devices, rank(): return lax.ppermute(values, 'dp', flip_dp(self.dp_size, bits))  101 us
    all_gather x1, blocking collectives, fast_device(): lax.all_gather(jnp.concatenate([gain_attn, gain_ffn], axis=0), ('dp', 'fs...  65.2 us
    pallas_call x2, Pallas kernels, attend_bwd(): pl.pallas_call(attend_bwd_kernel, out_shape=jax.ShapeDtypeStruct((total,...  57.2 us
    unnamed x380, local copies, waits for them, and re-layouts  55.2 us
  transfers between devices with their start and end apart: 122, of which 46 were waited for; matrix products, arithmetic and copies ran while one was open for 23% of the time, Pallas kernels for 7%

profile of v1, /device:TPU:0, one launch (start us, length us, event | category | flops | bytes accessed | tf_op | source)
XLA Modules:
  0.0 1520.7 jit_solution(3948975355495365792)
XLA Ops:
  38.0 14.9 dynamic-slice_reduce_fusion
  61.0 65.2 %all-gather.1 = bf16[32,4,48]{2,1,0:T(4,128)(2,1)S(1)} all-gather(bf16[1,4,48]{2,1,0:T(4,128)(2,1)S(1)} %maximum_bitcast_fusion), channel_id=2, replica_groups=mesh['dp'=8,'fsdp'=4] {'dp','fsdp'}, dimensions={0}, use_global_device_ids=true | all-gather | bytes 12672 | tf_op jit(solution)/shard_map/all_gather | solution.py:851
  139.4 7.2 concatenate.157.cos_ref
  147.6 7.3 concatenate.158.sin_ref
  168.0 26.1 %collective-permute-start.48 = (bf16[48,2048]{1,0:T(8,128)(2,1)S(1)}, bf16[48,2048]{1,0:T(8,128)(2,1)S(1)}, u32[]{:S(2)}, u32[]{:S(2)}) collective-permute-start(bf16[48,2048]{1,0:T(8,128)(2,1)S(1)} %copy-done.104), channel_id=1, source_target_pairs={{0,8},{4,12},{8,0},{12,4},{16,24},{20,28},{24,16},{28,20},{1,9},{5... | collective-permute-start | bytes 589832 | tf_op jit(solution)/shard_map/ppermute | solution.py:710
  204.4 8.7 collective-permute-done.6
  234.9 7.8 collective-permute-done.11
  251.3 7.0 shard_map.203
  268.8 14.1 shard_map.205
  299.5 42.4 %collective-permute-done.21 = bf16[288,2048]{1,0:T(8,128)(2,1)} collective-permute-done((bf16[288,2048]{1,0:T(8,128)(2,1)}, bf16[288,2048]{1,0:T(8,128)(2,1)}, u32[]{:S(2)}, u32[]{:S(2)}) %collective-permute-start.21) | collective-permute-done | bytes 1179680 | tf_op jit(solution)/shard_map/ppermute | solution.py:722
  342.4 27.9 %collective-permute-done.22 = bf16[288,2048]{1,0:T(8,128)(2,1)} collective-permute-done((bf16[288,2048]{1,0:T(8,128)(2,1)}, bf16[288,2048]{1,0:T(8,128)(2,1)}, u32[]{:S(2)}, u32[]{:S(2)}) %collective-permute-start.22) | collective-permute-done | bytes 1179680 | tf_op jit(solution)/shard_map/ppermute | solution.py:722
  381.1 12.5 collective-permute-done.16
  400.5 21.8 %collective-permute-done.27 = bf16[288,2048]{1,0:T(8,128)(2,1)S(1)} collective-permute-done((bf16[288,2048]{1,0:T(8,128)(2,1)}, bf16[288,2048]{1,0:T(8,128)(2,1)S(1)}, u32[]{:S(2)}, u32[]{:S(2)}) %collective-permute-start.27) | collective-permute-done | bytes 1179680 | tf_op jit(solution)/shard_map/ppermute | solution.py:710
  423.4 10.3 shard_map.206
  439.9 8.4 multiply_convert_fusion.1
  451.4 7.4 collective-permute-start.60
  472.4 23.0 %collective-permute-done.29 = bf16[256,1536]{1,0:T(8,128)(2,1)S(1)} collective-permute-done((bf16[256,1536]{1,0:T(8,128)(2,1)S(1)}, bf16[256,1536]{1,0:T(8,128)(2,1)S(1)}, u32[]{:S(2)}, u32[]{:S(2)}) %collective-permute-start.29) | collective-permute-done | bytes 786464 | tf_op jit(solution)/shard_map/ppermute | solution.py:710
  502.5 12.3 collective-permute-done.31
  577.9 14.1 shard_map.209
  599.6 25.0 %collective-permute-done.51 = bf16[288,2048]{1,0:T(8,128)(2,1)} collective-permute-done((bf16[288,2048]{1,0:T(8,128)(2,1)}, bf16[288,2048]{1,0:T(8,128)(2,1)}, u32[]{:S(2)}, u32[]{:S(2)}) %collective-permute-start.51) | collective-permute-done | bytes 1179680 | tf_op jit(solution)/shard_map/ppermute | solution.py:722
  636.9 16.8 %collective-permute-done.54 = bf16[288,2048]{1,0:T(8,128)(2,1)S(1)} collective-permute-done((bf16[288,2048]{1,0:T(8,128)(2,1)}, bf16[288,2048]{1,0:T(8,128)(2,1)S(1)}, u32[]{:S(2)}, u32[]{:S(2)}) %collective-permute-start.54) | collective-permute-done | bytes 1179680 | tf_op jit(solution)/shard_map/ppermute | solution.py:710
  656.9 22.0 %collective-permute-done.55 = bf16[288,2048]{1,0:T(8,128)(2,1)S(1)} collective-permute-done((bf16[288,2048]{1,0:T(8,128)(2,1)}, bf16[288,2048]{1,0:T(8,128)(2,1)S(1)}, u32[]{:S(2)}, u32[]{:S(2)}) %collective-permute-start.55) | collective-permute-done | bytes 1179680 | tf_op jit(solution)/shard_map/ppermute | solution.py:710
  680.1 18.3 %collective-permute-done.56 = bf16[288,2048]{1,0:T(8,128)(2,1)S(1)} collective-permute-done((bf16[288,2048]{1,0:T(8,128)(2,1)}, bf16[288,2048]{1,0:T(8,128)(2,1)S(1)}, u32[]{:S(2)}, u32[]{:S(2)}) %collective-permute-start.56) | collective-permute-done | bytes 1179680 | tf_op jit(solution)/shard_map/ppermute | solution.py:710
  699.5 10.2 shard_map.210
  737.5 10.4 fusion.29
  758.1 7.5 convolution_convert_fusion
  777.5 16.1 %collective-permute-done.118 = bf16[512,1536]{1,0:T(8,128)(2,1)} collective-permute-done((bf16[512,1536]{1,0:T(8,128)(2,1)S(1)}, bf16[512,1536]{1,0:T(8,128)(2,1)}, u32[]{:S(2)}, u32[]{:S(2)}) %collective-permute-start.118) | collective-permute-done | bytes 1572896 | tf_op jit(solution)/shard_map/ppermute | solution.py:710
  809.7 50.9 %collective-permute-done.107 = bf16[768,2048]{1,0:T(8,128)(2,1)} collective-permute-done((bf16[768,2048]{1,0:T(8,128)(2,1)}, bf16[768,2048]{1,0:T(8,128)(2,1)}, u32[]{:S(2)}, u32[]{:S(2)}) %collective-permute-start.107) | collective-permute-done | bytes 3145760 | tf_op jit(solution)/shard_map/ppermute | solution.py:710
  869.5 10.3 collective-permute-done.65
  900.9 14.4 collective-permute-done.108
  917.3 21.7 %collective-permute-done.109 = bf16[192,2048]{1,0:T(8,128)(2,1)S(1)} collective-permute-done((bf16[192,2048]{1,0:T(8,128)(2,1)S(1)}, bf16[192,2048]{1,0:T(8,128)(2,1)S(1)}, u32[]{:S(2)}, u32[]{:S(2)}) %collective-permute-start.109) | collective-permute-done | bytes 786464 | tf_op jit(solution)/shard_map/ppermute | solution.py:722
  942.3 28.4 %shard_map.211 = bf16[1024,768]{1,0:T(8,128)(2,1)} custom-call(s32[4]{0:T(128)} %copy-done.15, bf16[1024,768]{1,0:T(8,128)(2,1)} %copy-done.6, bf16[1024,384]{1,0:T(8,128)(2,1)} %convolution_convert_fusion.15.grad_ref, bf16[1024,384]{1,0:T(8,128)(2,1)} %copy-done.10, f32[4,256,4]{2,1,0:T(8,128)} %copy-done.17, s32[4,256,1]{2,1,0:T(8,128)} %copy-done.12, ...), custom_call_target="tpu_custom_call" | custom-call | flops 4026531840 | bytes 9437184 | tf_op jit(solution)/shard_map/pallas_call | solution.py:606
  974.5 17.9 %collective-permute-start.111 = (bf16[48,2048]{1,0:T(8,128)(2,1)S(1)}, bf16[48,2048]{1,0:T(8,128)(2,1)S(1)}, u32[]{:S(2)}, u32[]{:S(2)}) collective-permute-start(bf16[48,2048]{1,0:T(8,128)(2,1)S(1)} %get-tuple-element.139), channel_id=1, source_target_pairs={{0,12},{4,8},{8,4},{12,0},{16,28},{20,24},{24,20},{28,16},{1,13},{... | collective-permute-start | bytes 589832 | tf_op jit(solution)/shard_map/ppermute | solution.py:710
  1037.5 18.3 %collective-permute-done.85 = bf16[768,768]{1,0:T(8,128)(2,1)S(1)} collective-permute-done((bf16[768,768]{1,0:T(8,128)(2,1)S(1)}, bf16[768,768]{1,0:T(8,128)(2,1)S(1)}, u32[]{:S(2)}, u32[]{:S(2)}) %collective-permute-start.85) | collective-permute-done | bytes 1179680 | tf_op jit(solution)/shard_map/ppermute | solution.py:710
  1057.4 17.1 %collective-permute-start.86 = (bf16[192,768]{1,0:T(8,128)(2,1)S(1)}, bf16[192,768]{1,0:T(8,128)(2,1)S(1)}, u32[]{:S(2)}, u32[]{:S(2)}) collective-permute-start(bf16[192,768]{1,0:T(8,128)(2,1)S(1)} %get-tuple-element.131), channel_id=1, source_target_pairs={{0,1},{1,0},{2,3},{3,2},{4,5},{5,4},{6,7},{7,6},{8,9},{9,8},{10,11... | collective-permute-start | bytes 884744 | tf_op jit(solution)/shard_map/ppermute | solution.py:722
  1086.6 15.2 %collective-permute-done.87 = bf16[192,768]{1,0:T(8,128)(2,1)S(1)} collective-permute-done((bf16[192,768]{1,0:T(8,128)(2,1)S(1)}, bf16[192,768]{1,0:T(8,128)(2,1)S(1)}, u32[]{:S(2)}, u32[]{:S(2)}) %collective-permute-start.87) | collective-permute-done | bytes 294944 | tf_op jit(solution)/shard_map/ppermute | solution.py:722
  1116.0 9.5 fusion.37
  1139.2 13.3 collective-permute-done.114
  1176.2 12.3 collective-permute-done.116
  1193.0 26.6 %collective-permute-done.100 = bf16[768,2048]{1,0:T(8,128)(2,1)} collective-permute-done((bf16[768,2048]{1,0:T(8,128)(2,1)}, bf16[768,2048]{1,0:T(8,128)(2,1)}, u32[]{:S(2)}, u32[]{:S(2)}) %collective-permute-start.100) | collective-permute-done | bytes 3145760 | tf_op jit(solution)/shard_map/ppermute | solution.py:710
  1234.5 26.7 %collective-permute-done.101 = bf16[192,2048]{1,0:T(8,128)(2,1)S(1)} collective-permute-done((bf16[192,2048]{1,0:T(8,128)(2,1)S(1)}, bf16[192,2048]{1,0:T(8,128)(2,1)S(1)}, u32[]{:S(2)}, u32[]{:S(2)}) %collective-permute-start.101) | collective-permute-done | bytes 786464 | tf_op jit(solution)/shard_map/ppermute | solution.py:722
  1261.2 21.1 %collective-permute-done.102 = bf16[192,2048]{1,0:T(8,128)(2,1)S(1)} collective-permute-done((bf16[192,2048]{1,0:T(8,128)(2,1)S(1)}, bf16[192,2048]{1,0:T(8,128)(2,1)S(1)}, u32[]{:S(2)}, u32[]{:S(2)}) %collective-permute-start.102) | collective-permute-done | bytes 786464 | tf_op jit(solution)/shard_map/ppermute | solution.py:722
  1323.9 28.8 %shard_map.212 = bf16[1024,768]{1,0:T(8,128)(2,1)} custom-call(s32[4]{0:T(128)} %copy-done.15, bf16[1024,768]{1,0:T(8,128)(2,1)} %copy-done.5, bf16[1024,384]{1,0:T(8,128)(2,1)} %convolution_convert_fusion.14.grad_ref, bf16[1024,384]{1,0:T(8,128)(2,1)} %copy-done.7, f32[4,256,4]{2,1,0:T(8,128)} %copy-done.16, s32[4,256,1]{2,1,0:T(8,128)} %copy-done.12, ...), custom_call_target="tpu_custom_call" | custom-call | flops 4026531840 | bytes 9437184 | tf_op jit(solution)/shard_map/pallas_call | solution.py:606
  1363.7 16.0 %collective-permute-start.93 = (bf16[48,1536]{1,0:T(8,128)(2,1)S(1)}, bf16[48,1536]{1,0:T(8,128)(2,1)S(1)}, u32[]{:S(2)}, u32[]{:S(2)}) collective-permute-start(bf16[48,1536]{1,0:T(8,128)(2,1)S(1)} %get-tuple-element.156), channel_id=1, source_target_pairs={{0,1},{1,0},{2,3},{3,2},{4,5},{5,4},{6,7},{7,6},{8,9},{9,8},{10,11... | collective-permute-start | bytes 442376 | tf_op jit(solution)/shard_map/ppermute | solution.py:722
  1387.8 16.0 %collective-permute-start.79 = (bf16[192,768]{1,0:T(8,128)(2,1)S(1)}, bf16[192,768]{1,0:T(8,128)(2,1)S(1)}, u32[]{:S(2)}, u32[]{:S(2)}) collective-permute-start(bf16[192,768]{1,0:T(8,128)(2,1)S(1)} %get-tuple-element.128), channel_id=1, source_target_pairs={{0,1},{1,0},{2,3},{3,2},{4,5},{5,4},{6,7},{7,6},{8,9},{9,8},{10,11... | collective-permute-start | bytes 884744 | tf_op jit(solution)/shard_map/ppermute | solution.py:722
  1415.4 11.9 collective-permute-done.80
  1448.1 10.1 collective-permute-done.76
  1467.9 50.6 %psum.7 = f32[4,1536]{1,0:T(4,128)S(1)} all-reduce(f32[4,1536]{1,0:T(4,128)S(1)} %pad_maximum_fusion.49), channel_id=1, replica_groups=mesh['dp'=8,'fsdp'=4] {'dp','fsdp'}, use_global_device_ids=true, to_apply=%region_16.17 | all-reduce | flops 6144 | bytes 49152 | tf_op jit(solution)/shard_map/psum | solution.py:953
  (932 shorter events, 614.0 us)
Async XLA Ops:
  10.5 185.8 %collective-permute-start.18 = (bf16[48,2048]{1,0:T(8,128)(2,1)}, bf16[48,2048]{1,0:T(8,128)(2,1)S(1)}, u32[]{:S(2)}, u32[]{:S(2)}) collective-permute-start(bf16[48,2048]{1,0:T(8,128)(2,1)} %pad_maximum_fusion.29), channel_id=1, source_target_pairs={{0,12},{4,8},{8,4},{12,0},{16,28},{20,24},{24,20},{28,16},{1,13},{... | collective-permute-start | bytes 589832 | tf_op jit(solution)/shard_map/ppermute | solution.py:710
  13.5 183.0 %collective-permute-start.19 = (bf16[48,2048]{1,0:T(8,128)(2,1)}, bf16[48,2048]{1,0:T(8,128)(2,1)}, u32[]{:S(2)}, u32[]{:S(2)}) collective-permute-start(bf16[48,2048]{1,0:T(8,128)(2,1)} %pad_maximum_fusion.30), channel_id=1, source_target_pairs={{0,8},{4,12},{8,0},{12,4},{16,24},{20,28},{24,16},{28,20},{1,9},{5... | collective-permute-start | bytes 589832 | tf_op jit(solution)/shard_map/ppermute | solution.py:710
  14.1 117.8 %collective-permute-start.13 = (s32[1,4]{1,0:T(1,128)}, s32[1,4]{1,0:T(1,128)}, u32[]{:S(2)}, u32[]{:S(2)}) collective-permute-start(s32[1,4]{1,0:T(1,128)} %param.22), channel_id=1, source_target_pairs={{0,0},{1,8},{2,4},{3,12},{4,2},{5,10},{6,6},{7,14},{8,1},{9,9},{10... | collective-permute-start | bytes 56 | tf_op jit(solution)/shard_map/ppermute | solution.py:725
  23.6 131.3 %collective-permute-start.35 = (bf16[48,768]{1,0:T(8,128)(2,1)}, bf16[48,768]{1,0:T(8,128)(2,1)S(1)}, u32[]{:S(2)}, u32[]{:S(2)}) collective-permute-start(bf16[48,768]{1,0:T(8,128)(2,1)} %pad_maximum_fusion.47), channel_id=1, source_target_pairs={{0,4},{4,0},{8,12},{12,8},{16,20},{20,16},{24,28},{28,24},{1,5},{5... | collective-permute-start | bytes 221192 | tf_op jit(solution)/shard_map/ppermute | solution.py:710
  27.4 127.6 %collective-permute-start.34 = (bf16[48,768]{1,0:T(8,128)(2,1)}, bf16[48,768]{1,0:T(8,128)(2,1)S(1)}, u32[]{:S(2)}, u32[]{:S(2)}) collective-permute-start(bf16[48,768]{1,0:T(8,128)(2,1)} %pad_maximum_fusion.46), channel_id=1, source_target_pairs={{0,8},{4,12},{8,0},{12,4},{16,24},{20,28},{24,16},{28,20},{1,9},{5... | collective-permute-start | bytes 221192 | tf_op jit(solution)/shard_map/ppermute | solution.py:710
  157.8 38.8 %collective-permute-start.20 = (bf16[48,2048]{1,0:T(8,128)(2,1)}, bf16[48,2048]{1,0:T(8,128)(2,1)S(1)}, u32[]{:S(2)}, u32[]{:S(2)}) collective-permute-start(bf16[48,2048]{1,0:T(8,128)(2,1)} %pad_maximum_fusion.31), channel_id=1, source_target_pairs={{0,4},{4,0},{8,12},{12,8},{16,20},{20,16},{24,28},{28,24},{1,5},{5... | collective-permute-start | bytes 589832 | tf_op jit(solution)/shard_map/ppermute | solution.py:710
  289.1 52.7 %collective-permute-start.21 = (bf16[288,2048]{1,0:T(8,128)(2,1)}, bf16[288,2048]{1,0:T(8,128)(2,1)}, u32[]{:S(2)}, u32[]{:S(2)}) collective-permute-start(bf16[288,2048]{1,0:T(8,128)(2,1)} %maximum_dynamic-update-slice_fusion.2), channel_id=1, source_target_pairs={{0,1},{1,0},{2,3},{3,2},{4,5},{5,4},{6,7},{7,6},{8,9},{9,8},{10,11... | collective-permute-start | bytes 3538952 | tf_op jit(solution)/shard_map/ppermute | solution.py:722
  289.7 80.6 %collective-permute-start.22 = (bf16[288,2048]{1,0:T(8,128)(2,1)}, bf16[288,2048]{1,0:T(8,128)(2,1)}, u32[]{:S(2)}, u32[]{:S(2)}) collective-permute-start(bf16[288,2048]{1,0:T(8,128)(2,1)} %maximum_dynamic-update-slice_fusion.2), channel_id=1, source_target_pairs={{0,2},{1,3},{2,0},{3,1},{4,6},{5,7},{6,4},{7,5},{8,10},{9,11},{10,... | collective-permute-start | bytes 3538952 | tf_op jit(solution)/shard_map/ppermute | solution.py:722
  289.7 81.1 %collective-permute-start.23 = (bf16[288,2048]{1,0:T(8,128)(2,1)}, bf16[288,2048]{1,0:T(8,128)(2,1)}, u32[]{:S(2)}, u32[]{:S(2)}) collective-permute-start(bf16[288,2048]{1,0:T(8,128)(2,1)} %maximum_dynamic-update-slice_fusion.2), channel_id=1, source_target_pairs={{0,3},{1,2},{2,1},{3,0},{4,7},{5,6},{6,5},{7,4},{8,11},{9,10},{10,... | collective-permute-start | bytes 3538952 | tf_op jit(solution)/shard_map/ppermute | solution.py:722
  293.6 101.3 %collective-permute-start.24 = (bf16[288,2048]{1,0:T(8,128)(2,1)}, bf16[288,2048]{1,0:T(8,128)(2,1)S(1)}, u32[]{:S(2)}, u32[]{:S(2)}) collective-permute-start(bf16[288,2048]{1,0:T(8,128)(2,1)} %maximum_dynamic-update-slice_fusion.2), channel_id=1, source_target_pairs={{0,16},{4,20},{8,24},{12,28},{16,0},{20,4},{24,8},{28,12},{1,17},{... | collective-permute-start | bytes 3538952 | tf_op jit(solution)/shard_map/ppermute | solution.py:710
  296.9 77.9 %collective-permute-start.15 = (bf16[256,1536]{1,0:T(8,128)(2,1)S(1)}, bf16[256,1536]{1,0:T(8,128)(2,1)S(1)}, u32[]{:S(2)}, u32[]{:S(2)}) collective-permute-start(bf16[256,1536]{1,0:T(8,128)(2,1)S(1)} %slice.703), channel_id=1, source_target_pairs={{0,8},{4,12},{8,0},{12,4},{16,24},{20,28},{24,16},{28,20},{1,9},{5... | collective-permute-start | bytes 2359304 | tf_op jit(solution)/shard_map/ppermute | solution.py:710
  341.9 54.2 %collective-permute-start.25 = (bf16[288,2048]{1,0:T(8,128)(2,1)}, bf16[288,2048]{1,0:T(8,128)(2,1)S(1)}, u32[]{:S(2)}, u32[]{:S(2)}) collective-permute-start(bf16[288,2048]{1,0:T(8,128)(2,1)} %collective-permute-done.21), channel_id=1, source_target_pairs={{0,16},{4,20},{8,24},{12,28},{16,0},{20,4},{24,8},{28,12},{1,17},{... | collective-permute-start | bytes 3538952 | tf_op jit(solution)/shard_map/ppermute | solution.py:710
  370.8 51.5 %collective-permute-start.27 = (bf16[288,2048]{1,0:T(8,128)(2,1)}, bf16[288,2048]{1,0:T(8,128)(2,1)S(1)}, u32[]{:S(2)}, u32[]{:S(2)}) collective-permute-start(bf16[288,2048]{1,0:T(8,128)(2,1)} %collective-permute-done.23), channel_id=1, source_target_pairs={{0,16},{4,20},{8,24},{12,28},{16,0},{20,4},{24,8},{28,12},{1,17},{... | collective-permute-start | bytes 3538952 | tf_op jit(solution)/shard_map/ppermute | solution.py:710
  394.9 38.9 %collective-permute-start.17 = (bf16[512,1536]{1,0:T(8,128)(2,1)}, bf16[512,1536]{1,0:T(8,128)(2,1)}, u32[]{:S(2)}, u32[]{:S(2)}) collective-permute-start(bf16[512,1536]{1,0:T(8,128)(2,1)} %pad_maximum_fusion.15), channel_id=1, source_target_pairs={{0,4},{4,0},{8,12},{12,8},{16,20},{20,16},{24,28},{28,24},{1,5},{5... | collective-permute-start | bytes 4718600 | tf_op jit(solution)/shard_map/ppermute | solution.py:710
  451.4 141.6 %collective-permute-start.60 = (bf16[256,1536]{1,0:T(8,128)(2,1)}, bf16[256,1536]{1,0:T(8,128)(2,1)}, u32[]{:S(2)}, u32[]{:S(2)}) collective-permute-start(bf16[256,1536]{1,0:T(8,128)(2,1)} %param.23), channel_id=1, source_target_pairs={{0,0},{1,8},{2,4},{3,12},{4,2},{5,10},{6,6},{7,14},{8,1},{9,9},{10... | collective-permute-start | bytes 2359304 | tf_op jit(solution)/shard_map/ppermute | solution.py:725
  459.0 58.6 %collective-permute-start.36 = (bf16[288,768]{1,0:T(8,128)(2,1)}, bf16[288,768]{1,0:T(8,128)(2,1)S(1)}, u32[]{:S(2)}, u32[]{:S(2)}) collective-permute-start(bf16[288,768]{1,0:T(8,128)(2,1)} %get-tuple-element.176), channel_id=1, source_target_pairs={{0,1},{1,0},{2,3},{3,2},{4,5},{5,4},{6,7},{7,6},{8,9},{9,8},{10,11... | collective-permute-start | bytes 1327112 | tf_op jit(solution)/shard_map/ppermute | solution.py:722
  459.1 59.4 %collective-permute-start.37 = (bf16[288,768]{1,0:T(8,128)(2,1)}, bf16[288,768]{1,0:T(8,128)(2,1)S(1)}, u32[]{:S(2)}, u32[]{:S(2)}) collective-permute-start(bf16[288,768]{1,0:T(8,128)(2,1)} %get-tuple-element.176), channel_id=1, source_target_pairs={{0,2},{1,3},{2,0},{3,1},{4,6},{5,7},{6,4},{7,5},{8,10},{9,11},{10,... | collective-permute-start | bytes 1327112 | tf_op jit(solution)/shard_map/ppermute | solution.py:722
  459.2 61.2 %collective-permute-start.38 = (bf16[288,768]{1,0:T(8,128)(2,1)}, bf16[288,768]{1,0:T(8,128)(2,1)S(1)}, u32[]{:S(2)}, u32[]{:S(2)}) collective-permute-start(bf16[288,768]{1,0:T(8,128)(2,1)} %get-tuple-element.176), channel_id=1, source_target_pairs={{0,3},{1,2},{2,1},{3,0},{4,7},{5,6},{6,5},{7,4},{8,11},{9,10},{10,... | collective-permute-start | bytes 1327112 | tf_op jit(solution)/shard_map/ppermute | solution.py:722
  517.6 47.8 %collective-permute-start.32 = (bf16[512,1536]{1,0:T(8,128)(2,1)}, bf16[512,1536]{1,0:T(8,128)(2,1)}, u32[]{:S(2)}, u32[]{:S(2)}) collective-permute-start(bf16[512,1536]{1,0:T(8,128)(2,1)} %pad_maximum_fusion.16), channel_id=1, source_target_pairs={{0,4},{4,0},{8,12},{12,8},{16,20},{20,16},{24,28},{28,24},{1,5},{5... | collective-permute-start | bytes 4718600 | tf_op jit(solution)/shard_map/ppermute | solution.py:710
  518.5 77.9 %collective-permute-start.50 = (bf16[288,2048]{1,0:T(8,128)(2,1)}, bf16[288,2048]{1,0:T(8,128)(2,1)}, u32[]{:S(2)}, u32[]{:S(2)}) collective-permute-start(bf16[288,2048]{1,0:T(8,128)(2,1)} %maximum_dynamic-update-slice_fusion.3), channel_id=1, source_target_pairs={{0,1},{1,0},{2,3},{3,2},{4,5},{5,4},{6,7},{7,6},{8,9},{9,8},{10,11... | collective-permute-start | bytes 3538952 | tf_op jit(solution)/shard_map/ppermute | solution.py:722
  546.2 78.4 %collective-permute-start.51 = (bf16[288,2048]{1,0:T(8,128)(2,1)}, bf16[288,2048]{1,0:T(8,128)(2,1)}, u32[]{:S(2)}, u32[]{:S(2)}) collective-permute-start(bf16[288,2048]{1,0:T(8,128)(2,1)} %maximum_dynamic-update-slice_fusion.3), channel_id=1, source_target_pairs={{0,2},{1,3},{2,0},{3,1},{4,6},{5,7},{6,4},{7,5},{8,10},{9,11},{10,... | collective-permute-start | bytes 3538952 | tf_op jit(solution)/shard_map/ppermute | solution.py:722
  553.5 74.6 %collective-permute-start.52 = (bf16[288,2048]{1,0:T(8,128)(2,1)}, bf16[288,2048]{1,0:T(8,128)(2,1)}, u32[]{:S(2)}, u32[]{:S(2)}) collective-permute-start(bf16[288,2048]{1,0:T(8,128)(2,1)} %maximum_dynamic-update-slice_fusion.3), channel_id=1, source_target_pairs={{0,3},{1,2},{2,1},{3,0},{4,7},{5,6},{6,5},{7,4},{8,11},{9,10},{10,... | collective-permute-start | bytes 3538952 | tf_op jit(solution)/shard_map/ppermute | solution.py:722
  565.5 68.1 %collective-permute-start.53 = (bf16[288,2048]{1,0:T(8,128)(2,1)}, bf16[288,2048]{1,0:T(8,128)(2,1)S(1)}, u32[]{:S(2)}, u32[]{:S(2)}) collective-permute-start(bf16[288,2048]{1,0:T(8,128)(2,1)} %maximum_dynamic-update-slice_fusion.3), channel_id=1, source_target_pairs={{0,16},{4,20},{8,24},{12,28},{16,0},{20,4},{24,8},{28,12},{1,17},{... | collective-permute-start | bytes 3538952 | tf_op jit(solution)/shard_map/ppermute | solution.py:710
  593.0 38.4 %collective-permute-start.43 = (bf16[512,1536]{1,0:T(8,128)(2,1)S(1)}, bf16[512,1536]{1,0:T(8,128)(2,1)S(1)}, u32[]{:S(2)}, u32[]{:S(2)}) collective-permute-start(bf16[512,1536]{1,0:T(8,128)(2,1)S(1)} %convolution_convert_fusion.9), channel_id=1, source_target_pairs={{0,4},{4,0},{8,12},{12,8},{16,20},{20,16},{24,28},{28,24},{1,5},{5... | collective-permute-start | bytes 4718600 | tf_op jit(solution)/shard_map/ppermute | solution.py:710
  596.5 39.2 %collective-permute-start.61 = (bf16[256,1536]{1,0:T(8,128)(2,1)S(1)}, bf16[256,1536]{1,0:T(8,128)(2,1)S(1)}, u32[]{:S(2)}, u32[]{:S(2)}) collective-permute-start(bf16[256,1536]{1,0:T(8,128)(2,1)S(1)} %fusion.50), channel_id=1, source_target_pairs={{0,8},{4,12},{8,0},{12,4},{16,24},{20,28},{24,16},{28,20},{1,9},{5... | collective-permute-start | bytes 2359304 | tf_op jit(solution)/shard_map/ppermute | solution.py:710
  628.1 50.9 %collective-permute-start.55 = (bf16[288,2048]{1,0:T(8,128)(2,1)}, bf16[288,2048]{1,0:T(8,128)(2,1)S(1)}, u32[]{:S(2)}, u32[]{:S(2)}) collective-permute-start(bf16[288,2048]{1,0:T(8,128)(2,1)} %collective-permute-done.51), channel_id=1, source_target_pairs={{0,16},{4,20},{8,24},{12,28},{16,0},{20,4},{24,8},{28,12},{1,17},{... | collective-permute-start | bytes 3538952 | tf_op jit(solution)/shard_map/ppermute | solution.py:710
  631.5 66.9 %collective-permute-start.56 = (bf16[288,2048]{1,0:T(8,128)(2,1)}, bf16[288,2048]{1,0:T(8,128)(2,1)S(1)}, u32[]{:S(2)}, u32[]{:S(2)}) collective-permute-start(bf16[288,2048]{1,0:T(8,128)(2,1)} %collective-permute-done.52), channel_id=1, source_target_pairs={{0,16},{4,20},{8,24},{12,28},{16,0},{20,4},{24,8},{28,12},{1,17},{... | collective-permute-start | bytes 3538952 | tf_op jit(solution)/shard_map/ppermute | solution.py:710
  636.9 100.6 %collective-permute-start.62 = (bf16[512,1536]{1,0:T(8,128)(2,1)}, bf16[512,1536]{1,0:T(8,128)(2,1)}, u32[]{:S(2)}, u32[]{:S(2)}) collective-permute-start(bf16[512,1536]{1,0:T(8,128)(2,1)} %pad_maximum_fusion.19), channel_id=1, source_target_pairs={{0,4},{4,0},{8,12},{12,8},{16,20},{20,16},{24,28},{28,24},{1,5},{5... | collective-permute-start | bytes 4718600 | tf_op jit(solution)/shard_map/ppermute | solution.py:710
  656.5 53.2 %collective-permute-start.45 = (bf16[256,1536]{1,0:T(8,128)(2,1)S(1)}, bf16[256,1536]{1,0:T(8,128)(2,1)}, u32[]{:S(2)}, u32[]{:S(2)}) collective-permute-start(bf16[256,1536]{1,0:T(8,128)(2,1)S(1)} %multiply_convert_fusion.2), channel_id=1, source_target_pairs={{0,8},{4,12},{8,0},{12,4},{16,24},{20,28},{24,16},{28,20},{1,9},{5... | collective-permute-start | bytes 2359304 | tf_op jit(solution)/shard_map/ppermute | solution.py:710
  765.5 95.1 %collective-permute-start.107 = (bf16[768,2048]{1,0:T(8,128)(2,1)}, bf16[768,2048]{1,0:T(8,128)(2,1)}, u32[]{:S(2)}, u32[]{:S(2)}) collective-permute-start(bf16[768,2048]{1,0:T(8,128)(2,1)} %convolution_convert_fusion), channel_id=1, source_target_pairs={{0,16},{4,20},{8,24},{12,28},{16,0},{20,4},{24,8},{28,12},{1,17},{... | collective-permute-start | bytes 9437192 | tf_op jit(solution)/shard_map/ppermute | solution.py:710
  797.4 85.8 %collective-permute-start.119 = (bf16[128,1536]{1,0:T(8,128)(2,1)S(1)}, bf16[128,1536]{1,0:T(8,128)(2,1)}, u32[]{:S(2)}, u32[]{:S(2)}) collective-permute-start(bf16[128,1536]{1,0:T(8,128)(2,1)S(1)} %get-tuple-element.117), channel_id=1, source_target_pairs={{0,1},{1,0},{2,3},{3,2},{4,5},{5,4},{6,7},{7,6},{8,9},{9,8},{10,11... | collective-permute-start | bytes 1179656 | tf_op jit(solution)/shard_map/ppermute | solution.py:722
  800.8 85.9 %collective-permute-start.120 = (bf16[128,1536]{1,0:T(8,128)(2,1)S(1)}, bf16[128,1536]{1,0:T(8,128)(2,1)}, u32[]{:S(2)}, u32[]{:S(2)}) collective-permute-start(bf16[128,1536]{1,0:T(8,128)(2,1)S(1)} %get-tuple-element.119), channel_id=1, source_target_pairs={{0,2},{1,3},{2,0},{3,1},{4,6},{5,7},{6,4},{7,5},{8,10},{9,11},{10,... | collective-permute-start | bytes 1179656 | tf_op jit(solution)/shard_map/ppermute | solution.py:722
  804.2 82.6 %collective-permute-start.121 = (bf16[128,1536]{1,0:T(8,128)(2,1)S(1)}, bf16[128,1536]{1,0:T(8,128)(2,1)}, u32[]{:S(2)}, u32[]{:S(2)}) collective-permute-start(bf16[128,1536]{1,0:T(8,128)(2,1)S(1)} %get-tuple-element.118), channel_id=1, source_target_pairs={{0,3},{1,2},{2,1},{3,0},{4,7},{5,6},{6,5},{7,4},{8,11},{9,10},{10,... | collective-permute-start | bytes 1179656 | tf_op jit(solution)/shard_map/ppermute | solution.py:722
  806.2 88.7 %collective-permute-start.58 = (bf16[256,1536]{1,0:T(8,128)(2,1)S(1)}, bf16[256,1536]{1,0:T(8,128)(2,1)}, u32[]{:S(2)}, u32[]{:S(2)}) collective-permute-start(bf16[256,1536]{1,0:T(8,128)(2,1)S(1)} %slice.700), channel_id=1, source_target_pairs={{0,8},{4,12},{8,0},{12,4},{16,24},{20,28},{24,16},{28,20},{1,9},{5... | collective-permute-start | bytes 2359304 | tf_op jit(solution)/shard_map/ppermute | solution.py:710
  883.2 55.8 %collective-permute-start.109 = (bf16[192,2048]{1,0:T(8,128)(2,1)S(1)}, bf16[192,2048]{1,0:T(8,128)(2,1)S(1)}, u32[]{:S(2)}, u32[]{:S(2)}) collective-permute-start(bf16[192,2048]{1,0:T(8,128)(2,1)S(1)} %get-tuple-element.113), channel_id=1, source_target_pairs={{0,2},{1,3},{2,0},{3,1},{4,6},{5,7},{6,4},{7,5},{8,10},{9,11},{10,... | collective-permute-start | bytes 2359304 | tf_op jit(solution)/shard_map/ppermute | solution.py:722
  886.7 52.3 %collective-permute-start.110 = (bf16[192,2048]{1,0:T(8,128)(2,1)S(1)}, bf16[192,2048]{1,0:T(8,128)(2,1)S(1)}, u32[]{:S(2)}, u32[]{:S(2)}) collective-permute-start(bf16[192,2048]{1,0:T(8,128)(2,1)S(1)} %get-tuple-element.112), channel_id=1, source_target_pairs={{0,3},{1,2},{2,1},{3,0},{4,7},{5,6},{6,5},{7,4},{8,11},{9,10},{10,... | collective-permute-start | bytes 2359304 | tf_op jit(solution)/shard_map/ppermute | solution.py:722
  886.8 52.8 %collective-permute-start.66 = (bf16[512,1536]{1,0:T(8,128)(2,1)S(1)}, bf16[512,1536]{1,0:T(8,128)(2,1)S(1)}, u32[]{:S(2)}, u32[]{:S(2)}) collective-permute-start(bf16[512,1536]{1,0:T(8,128)(2,1)S(1)} %pad_maximum_fusion.20), channel_id=1, source_target_pairs={{0,4},{4,0},{8,12},{12,8},{16,20},{20,16},{24,28},{28,24},{1,5},{5... | collective-permute-start | bytes 4718600 | tf_op jit(solution)/shard_map/ppermute | solution.py:710
  894.9 97.4 %collective-permute-start.30 = (bf16[256,1536]{1,0:T(8,128)(2,1)}, bf16[256,1536]{1,0:T(8,128)(2,1)S(1)}, u32[]{:S(2)}, u32[]{:S(2)}) collective-permute-start(bf16[256,1536]{1,0:T(8,128)(2,1)} %fusion.44), channel_id=1, source_target_pairs={{0,0},{1,8},{2,4},{3,12},{4,2},{5,10},{6,6},{7,14},{8,1},{9,9},{10... | collective-permute-start | bytes 2359304 | tf_op jit(solution)/shard_map/ppermute | solution.py:725
  915.4 77.1 %collective-permute-start.59 = (bf16[256,1536]{1,0:T(8,128)(2,1)}, bf16[256,1536]{1,0:T(8,128)(2,1)S(1)}, u32[]{:S(2)}, u32[]{:S(2)}) collective-permute-start(bf16[256,1536]{1,0:T(8,128)(2,1)} %fusion.45), channel_id=1, source_target_pairs={{0,0},{1,8},{2,4},{3,12},{4,2},{5,10},{6,6},{7,14},{8,1},{9,9},{10... | collective-permute-start | bytes 2359304 | tf_op jit(solution)/shard_map/ppermute | solution.py:725
  1034.9 42.9 %collective-permute-start.69 = (bf16[256,1536]{1,0:T(8,128)(2,1)S(1)}, bf16[256,1536]{1,0:T(8,128)(2,1)S(1)}, u32[]{:S(2)}, u32[]{:S(2)}) collective-permute-start(bf16[256,1536]{1,0:T(8,128)(2,1)S(1)} %get-tuple-element.91), channel_id=1, source_target_pairs={{0,8},{4,12},{8,0},{12,4},{16,24},{20,28},{24,16},{28,20},{1,9},{5... | collective-permute-start | bytes 2359304 | tf_op jit(solution)/shard_map/ppermute | solution.py:710
  1037.0 41.1 %collective-permute-start.96 = (bf16[192,1536]{1,0:T(8,128)(2,1)S(1)}, bf16[192,1536]{1,0:T(8,128)(2,1)S(1)}, u32[]{:S(2)}, u32[]{:S(2)}) collective-permute-start(bf16[192,1536]{1,0:T(8,128)(2,1)S(1)} %convolution_convert_fusion.12), channel_id=1, source_target_pairs={{0,16},{4,20},{8,24},{12,28},{16,0},{20,4},{24,8},{28,12},{1,17},{... | collective-permute-start | bytes 1769480 | tf_op jit(solution)/shard_map/ppermute | solution.py:710
  1138.3 81.3 %collective-permute-start.100 = (bf16[768,2048]{1,0:T(8,128)(2,1)}, bf16[768,2048]{1,0:T(8,128)(2,1)}, u32[]{:S(2)}, u32[]{:S(2)}) collective-permute-start(bf16[768,2048]{1,0:T(8,128)(2,1)} %convolution_convert_fusion.1), channel_id=1, source_target_pairs={{0,16},{4,20},{8,24},{12,28},{16,0},{20,4},{24,8},{28,12},{1,17},{... | collective-permute-start | bytes 9437192 | tf_op jit(solution)/shard_map/ppermute | solution.py:710
  1227.3 55.1 %collective-permute-start.102 = (bf16[192,2048]{1,0:T(8,128)(2,1)S(1)}, bf16[192,2048]{1,0:T(8,128)(2,1)S(1)}, u32[]{:S(2)}, u32[]{:S(2)}) collective-permute-start(bf16[192,2048]{1,0:T(8,128)(2,1)S(1)} %get-tuple-element.110), channel_id=1, source_target_pairs={{0,2},{1,3},{2,0},{3,1},{4,6},{5,7},{6,4},{7,5},{8,10},{9,11},{10,... | collective-permute-start | bytes 2359304 | tf_op jit(solution)/shard_map/ppermute | solution.py:722
  1230.0 52.3 %collective-permute-start.103 = (bf16[192,2048]{1,0:T(8,128)(2,1)S(1)}, bf16[192,2048]{1,0:T(8,128)(2,1)S(1)}, u32[]{:S(2)}, u32[]{:S(2)}) collective-permute-start(bf16[192,2048]{1,0:T(8,128)(2,1)S(1)} %get-tuple-element.109), channel_id=1, source_target_pairs={{0,3},{1,2},{2,1},{3,0},{4,7},{5,6},{6,5},{7,4},{8,11},{9,10},{10,... | collective-permute-start | bytes 2359304 | tf_op jit(solution)/shard_map/ppermute | solution.py:722
  1232.2 52.7 %collective-permute-start.73 = (bf16[256,1536]{1,0:T(8,128)(2,1)S(1)}, bf16[256,1536]{1,0:T(8,128)(2,1)S(1)}, u32[]{:S(2)}, u32[]{:S(2)}) collective-permute-start(bf16[256,1536]{1,0:T(8,128)(2,1)S(1)} %get-tuple-element.89), channel_id=1, source_target_pairs={{0,8},{4,12},{8,0},{12,4},{16,24},{20,28},{24,16},{28,20},{1,9},{5... | collective-permute-start | bytes 2359304 | tf_op jit(solution)/shard_map/ppermute | solution.py:710
  1319.6 41.5 %collective-permute-start.92 = (bf16[192,1536]{1,0:T(8,128)(2,1)}, bf16[192,1536]{1,0:T(8,128)(2,1)}, u32[]{:S(2)}, u32[]{:S(2)}) collective-permute-start(bf16[192,1536]{1,0:T(8,128)(2,1)} %convolution_convert_fusion.13), channel_id=1, source_target_pairs={{0,16},{4,20},{8,24},{12,28},{16,0},{20,4},{24,8},{28,12},{1,17},{... | collective-permute-start | bytes 1769480 | tf_op jit(solution)/shard_map/ppermute | solution.py:710
  1363.7 41.1 %collective-permute-start.93 = (bf16[48,1536]{1,0:T(8,128)(2,1)S(1)}, bf16[48,1536]{1,0:T(8,128)(2,1)S(1)}, u32[]{:S(2)}, u32[]{:S(2)}) collective-permute-start(bf16[48,1536]{1,0:T(8,128)(2,1)S(1)} %get-tuple-element.156), channel_id=1, source_target_pairs={{0,1},{1,0},{2,3},{3,2},{4,5},{5,4},{6,7},{7,6},{8,9},{9,8},{10,11... | collective-permute-start | bytes 442376 | tf_op jit(solution)/shard_map/ppermute | solution.py:722
  1465.2 53.9 %collective-permute-start.77 = (bf16[256,1536]{1,0:T(8,128)(2,1)}, bf16[256,1536]{1,0:T(8,128)(2,1)S(1)}, u32[]{:S(2)}, u32[]{:S(2)}) collective-permute-start(bf16[256,1536]{1,0:T(8,128)(2,1)} %fusion.47), channel_id=1, source_target_pairs={{0,0},{1,8},{2,4},{3,12},{4,2},{5,10},{6,6},{7,14},{8,1},{9,9},{10... | collective-permute-start | bytes 2359304 | tf_op jit(solution)/shard_map/ppermute | solution.py:725
  (239 other events, 5743.1 us)

commit v2 on v1

--- a/solution.py
+++ b/solution.py
@@ -804,6 +804,426 @@
     return lax.rsqrt(jnp.mean(values * values, axis=-1, keepdims=True) + EPSILON)
 
 
+MESH = pl.DeviceIdType.MESH
+VMEM_LIMIT = 61 * 2**20
+ANYWHERE = pl.BlockSpec(memory_space=pl.ANY)
+IN_VMEM = pl.BlockSpec(memory_space=pltpu.VMEM)
+
+
+class Net:
+    def __init__(self, send_sems, recv_sems, local_sems):
+        dp, z = lax.axis_index("dp"), lax.axis_index("fsdp")
+        self.z = z
+        self.q = lax.rem(dp, TP)
+        self.y = lax.div(dp, TP)
+        self.r = self.y * TP + z
+        core = dp + 1 - 2 * lax.rem(dp, 2)
+        across = dp + 2 - 4 * lax.rem(lax.div(dp, 2), 2)
+        both = core + 2 - 4 * lax.rem(lax.div(dp, 2), 2)
+        other = dp + TP - 2 * TP * lax.div(dp, TP)
+        self.peer = {
+            "core": (core, z),
+            "x": (across, z),
+            "both": (both, z),
+            "y": (other, z),
+            "z1": (dp, flip_index(z, 1)),
+            "z2": (dp, flip_index(z, 2)),
+            "z3": (dp, flip_index(z, 3)),
+        }
+        self.send_sems, self.recv_sems, self.local_sems = send_sems, recv_sems, local_sems
+        self.n_remote = self.n_local = 0
+        self.flying = []
+        self.leaving = []
+
+    def greet(self, names):
+        barrier = pltpu.get_barrier_semaphore()
+        for name in names:
+            pl.semaphore_signal(barrier, inc=1, device_id=self.peer[name], device_id_type=MESH)
+        pl.semaphore_wait(barrier, len(names))
+
+    def remote(self, src, dst, name):
+        n = self.n_remote
+        self.n_remote += 1
+        copy = pltpu.make_async_remote_copy(
+            src_ref=src,
+            dst_ref=dst,
+            send_sem=self.send_sems.at[n],
+            recv_sem=self.recv_sems.at[n],
+            device_id=self.peer[name],
+            device_id_type=MESH,
+        )
+        copy.start()
+        return copy
+
+    def local(self, src, dst):
+        n = self.n_local
+        self.n_local += 1
+        copy = pltpu.make_async_copy(src, dst, self.local_sems.at[n])
+        copy.start()
+        return copy
+
+    def keep(self, src, dst):
+        self.leaving.append(self.local(src, dst))
+
+    def finish(self):
+        for copy in self.flying + self.leaving:
+            copy.wait()
+        self.flying, self.leaving = [], []
+
+    def advance(self, moves):
+        for copy in self.flying:
+            copy.wait()
+        self.flying = []
+        for kind, ref, low, count in moves:
+            if kind == "z":
+                part = ref.at[self.r, pl.ds(low, count)]
+                for k in (2, 3, 1):
+                    self.flying.append(self.remote(part, part, f"z{k}"))
+            else:
+                part = ref.at[pl.ds(self.y * TP, TP), pl.ds(low, count)]
+                self.flying.append(self.remote(part, part, "y"))
+
+
+def flip_index(value, bits):
+    low = lax.rem(value, 2)
+    high = lax.div(value, 2)
+    if bits & 1:
+        low = 1 - low
+    if bits & 2:
+        high = 1 - high
+    return high * 2 + low
+
+
+def mixed_index(static, dynamic):
+    return flip_index(dynamic, static)
+
+
+def swap_index(value):
+    return lax.rem(value, 2) * 2 + lax.div(value, 2)
+
+
+def sems(remote, local):
+    return [
+        pltpu.SemaphoreType.DMA((max(remote, 1),)),
+        pltpu.SemaphoreType.DMA((max(remote, 1),)),
+        pltpu.SemaphoreType.DMA((max(local, 1),)),
+    ]
+
+
+def start_kernel(
+    qkv_pack, gu_pack, out_own, down_own, gain_tile, cot,
+    g_qkv0, g_qkv1, g_gu0, g_gu1, g_out0, g_out1, g_down0, g_down1, g_gain, branch,
+    spread_buf, send_sems, recv_sems, local_sems,
+):
+    net = Net(send_sems, recv_sems, local_sems)
+    shard = qkv_pack.shape[2]
+    bring = net.local(cot, spread_buf.at[0])
+    net.greet(("core", "x", "both", "y", "z1", "z2", "z3"))
+    mine = pl.ds(pl.multiple_of(net.q * shard, shard), shard)
+    r = net.r
+
+    def columns(pack, layer, target):
+        copies = []
+        for name, bits in (("both", 3), ("x", 2), ("core", 1)):
+            copies.append(
+                net.remote(pack.at[layer, flip_index(net.q, bits)], target.at[r, mine], name)
+            )
+        copies.append(net.local(pack.at[layer, net.q], target.at[r, mine]))
+        return copies
+
+    first = columns(qkv_pack, 0, g_qkv0)
+    for name in ("both", "x", "core"):
+        first.append(net.remote(gain_tile, g_gain.at[r, net.q], name))
+    first.append(net.local(gain_tile, g_gain.at[r, net.q]))
+    placed = [
+        net.local(out_own.at[0], g_out0.at[r]),
+        net.local(out_own.at[1], g_out1.at[r]),
+        net.local(down_own.at[0], g_down0.at[r]),
+        net.local(down_own.at[1], g_down1.at[r]),
+    ]
+    out_first = [net.remote(out_own.at[0], g_out0.at[r], f"z{k}") for k in (2, 3, 1)]
+    for copy in first:
+        copy.wait()
+    net.flying = []
+    net.advance((("z", g_qkv0, 0, g_qkv0.shape[1]), ("z", g_gain, 0, TP)))
+    second = columns(gu_pack, 0, g_gu0) + columns(qkv_pack, 1, g_qkv1) + columns(gu_pack, 1, g_gu1)
+    bring.wait()
+    over_x = net.remote(spread_buf.at[0], spread_buf.at[1], "x")
+    over_core = net.remote(spread_buf.at[0], spread_buf.at[2], "core")
+    for copy in out_first + placed:
+        copy.wait()
+    net.advance(
+        (
+            ("y", g_qkv0, 0, g_qkv0.shape[1]),
+            ("y", g_gain, 0, TP),
+            ("y", g_out0, 0, g_out0.shape[1]),
+            ("z", g_down0, 0, g_down0.shape[1]),
+        )
+    )
+    over_x.wait()
+    forward = net.remote(spread_buf.at[1], spread_buf.at[3], "core")
+    over_core.wait()
+    forward.wait()
+    net.keep(spread_buf, branch)
+    for copy in second:
+        copy.wait()
+    net.finish()
+
+
+def start_exchange(qkv_pack, gu_pack, out_own, down_own, gain_tile, cot):
+    bf = jnp.bfloat16
+    block, depth = cot.shape
+    shard, qkv_width = qkv_pack.shape[2:]
+    units = gu_pack.shape[3]
+    outs = []
+    for rows, width in (
+        (TP * shard, qkv_width),
+        (TP * shard, units),
+        (shard, depth),
+        (down_own.shape[1], depth),
+    ):
+        outs += [jax.ShapeDtypeStruct((2 * TP, rows, width), bf)] * 2
+    outs.append(jax.ShapeDtypeStruct((2 * TP, TP) + gain_tile.shape, jnp.float32))
+    outs.append(jax.ShapeDtypeStruct((TP, block, depth), bf))
+    return pl.pallas_call(
+        start_kernel,
+        out_shape=outs,
+        in_specs=[ANYWHERE] * 6,
+        out_specs=[ANYWHERE] * 10,
+        scratch_shapes=[pltpu.VMEM((TP, block, depth), bf)] + sems(40, 24),
+        compiler_params=pltpu.CompilerParams(
+            collective_id=1, has_side_effects=True, vmem_limit_bytes=VMEM_LIMIT
+        ),
+        cost_estimate=pl.CostEstimate(flops=0, bytes_accessed=300 * 2**20, transcendentals=0),
+    )(qkv_pack, gu_pack, out_own, down_own, gain_tile, cot)
+
+
+def attend_rows(net, block):
+    base = swap_index(net.q)
+    return [pl.ds(pl.multiple_of(mixed_index(b, base) * block, block), block) for b in range(TP)]
+
+
+def attend_forward_block(net, qkv_ref, row_seg_ref, col_seg_ref, mixed_ref, lse_ref):
+    total, width = qkv_ref.shape
+    block = total // TP
+    q_heads = width // (2 * HEAD_DIM)
+    kv_heads = q_heads // 2
+    factor = 1.0 / math.sqrt(HEAD_DIM)
+    key_at = q_heads * HEAD_DIM
+    value_at = key_at + kv_heads * HEAD_DIM
+    places = attend_rows(net, block)
+    nt = (((1,), (1,)), ((), ()))
+    for i in range(TP):
+        row_seg = row_seg_ref[i]
+        masks = [block_mask(row_seg, col_seg_ref[j], i == j, block) for j in range(i + 1)]
+        for h in range(q_heads):
+            kv = h // 2
+            query = qkv_ref[places[i], h * HEAD_DIM : (h + 1) * HEAD_DIM]
+            scores = []
+            for j in range(i + 1):
+                key = qkv_ref[places[j], key_at + kv * HEAD_DIM : key_at + (kv + 1) * HEAD_DIM]
+                s = lax.dot_general(query, key, nt, preferred_element_type=jnp.float32) * factor
+                scores.append(jnp.where(masks[j], s, NEGATIVE))
+            peak = scores[0].max(axis=1, keepdims=True)
+            for s in scores[1:]:
+                peak = jnp.maximum(peak, s.max(axis=1, keepdims=True))
+            total_e = jnp.zeros((block, 1), jnp.float32)
+            mixed = jnp.zeros((block, HEAD_DIM), jnp.float32)
+            for j in range(i + 1):
+                e = jnp.exp(scores[j] - peak)
+                total_e = total_e + e.sum(axis=1, keepdims=True)
+                value = qkv_ref[places[j], value_at + kv * HEAD_DIM : value_at + (kv + 1) * HEAD_DIM]
+                mixed = mixed + jnp.dot(
+                    e.astype(jnp.bfloat16), value, preferred_element_type=jnp.float32
+                )
+            mixed_ref[places[i], h * HEAD_DIM : (h + 1) * HEAD_DIM] = (mixed / total_e).astype(
+                jnp.bfloat16
+            )
+            lse_ref[i, :, h : h + 1] = peak + jnp.log(total_e)
+
+
+def normalize(values, gain_row):
+    scale = lax.rsqrt(jnp.mean(values * values, axis=-1, keepdims=True) + EPSILON)
+    return (values * scale * gain_row).astype(jnp.bfloat16)
+
+
+def spread_begin(net, buf):
+    return (net.remote(buf.at[0], buf.at[1], "x"), net.remote(buf.at[0], buf.at[2], "core"))
+
+
+def spread_each(net, buf, begun, work):
+    over_x, over_core = begun
+    work(0)
+    over_core.wait()
+    work(2)
+    over_x.wait()
+    forward = net.remote(buf.at[1], buf.at[3], "core")
+    work(1)
+    forward.wait()
+    work(3)
+
+
+def collect(net, part, far_out, far_in, pass_out, pass_in):
+    low = lambda v: v.astype(jnp.bfloat16)
+    far_out[0] = low(part(3))
+    first = net.remote(far_out.at[0], far_in.at[0], "core")
+    near = part(1)
+    first.wait()
+    pass_out[...] = low(near + far_in[0].astype(jnp.float32))
+    passed = net.remote(pass_out, pass_in, "x")
+    far_out[1] = low(part(2))
+    second = net.remote(far_out.at[1], far_in.at[1], "core")
+    own = part(0)
+    second.wait()
+    own = own + far_in[1].astype(jnp.float32)
+    passed.wait()
+    return own + pass_in[...].astype(jnp.float32)
+
+
+def forward_kernel(programs, n_moving, *refs):
+    x_own, gain_a, gain_f, cos_ref, sin_ref, row_seg, col_seg = refs[:7]
+    refs = refs[7 + n_moving :]
+    moving, refs = refs[:n_moving], refs[n_moving:]
+    (x_next, middle_ref, lse_ref, rows_out, qkv_out, mixed_out, ffn_rows_out, gate_out, up_out, act_out) = refs[:10]
+    (rows, ffn_rows, w_qkv, w_o, w_gu, w_d, qkv, mixed, gate, up, act,
+     far_out, far_in, pass_out, pass_in, send_sems, recv_sems, local_sems) = refs[10:]
+    net = Net(send_sems, recv_sems, local_sems)
+    steps = [[(kind, moving[n], low, count) for kind, n, low, count in step] for step in programs]
+    block, depth = x_own.shape
+    load_qkv = net.local(moving[0], w_qkv)
+    load_o = net.local(moving[1], w_o)
+    net.greet(("core", "x", "y", "z1", "z2", "z3"))
+    net.advance(steps[0])
+    rows[0] = normalize(x_own[...], gain_a[...])
+    begun = spread_begin(net, rows)
+    load_qkv.wait()
+
+    def project(s):
+        raw = jnp.dot(
+            rows[s], w_qkv[...].reshape(depth, -1), preferred_element_type=jnp.float32
+        )
+        at = slice(s * block, (s + 1) * block)
+        turned = raw * cos_ref[at, :] + head_partner(raw, HEAD_DIM // 2) * sin_ref[at, :]
+        qkv[at, :] = turned.astype(jnp.bfloat16)
+
+    spread_each(net, rows, begun, project)
+    net.keep(rows, rows_out)
+    net.keep(qkv, qkv_out)
+    net.advance(steps[1])
+    load_d = net.local(moving[3], w_d)
+    attend_forward_block(net, qkv, row_seg, col_seg, mixed, lse_ref)
+    net.keep(mixed, mixed_out)
+    load_o.wait()
+
+    def out_part(s):
+        return jnp.dot(
+            mixed[s * block : (s + 1) * block, :],
+            w_o[...].reshape(-1, depth),
+            preferred_element_type=jnp.float32,
+        )
+
+    middle = x_own[...] + collect(
+        net, out_part, far_out, far_in.at[0], pass_out, pass_in.at[0]
+    )
+    middle_ref[...] = middle
+    net.advance(steps[2])
+    ffn_rows[0] = normalize(middle, gain_f[...])
+    begun = spread_begin(net, ffn_rows)
+    net.advance(steps[3])
+    load_gu = net.local(moving[2], w_gu)
+    load_d.wait()
+    load_gu.wait()
+    units = act.shape[2]
+
+    def expand(s):
+        value = ffn_rows[s]
+        gating = jnp.dot(
+            value, w_gu[:, :, :units].reshape(depth, units), preferred_element_type=jnp.float32
+        )
+        upward = jnp.dot(
+            value, w_gu[:, :, units:].reshape(depth, units), preferred_element_type=jnp.float32
+        )
+        gate[s] = gating.astype(jnp.bfloat16)
+        up[s] = upward.astype(jnp.bfloat16)
+        act[s] = (gating * jax.nn.sigmoid(gating) * upward).astype(jnp.bfloat16)
+
+    spread_each(net, ffn_rows, begun, expand)
+    net.keep(ffn_rows, ffn_rows_out)
+    net.keep(gate, gate_out)
+    net.keep(up, up_out)
+    net.keep(act, act_out)
+
+    def down_part(s):
+        return jnp.dot(act[s], w_d[...].reshape(-1, depth), preferred_element_type=jnp.float32)
+
+    x_next[...] = middle_ref[...] + collect(
+        net, down_part, far_out, far_in.at[1], pass_out, pass_in.at[1]
+    )
+    net.finish()
+
+
+def forward_layer(programs, cid, x_own, gain_a, gain_f, cosine, sine, row_seg, col_seg, moving):
+    bf, f32 = jnp.bfloat16, jnp.float32
+    block, depth = x_own.shape
+    total, qkv_width = cosine.shape
+    units = moving[2].shape[2] // 2
+    q_heads = qkv_width // (2 * HEAD_DIM)
+    shape = jax.ShapeDtypeStruct
+    outs = [shape(m.shape, m.dtype) for m in moving] + [
+        shape((block, depth), f32),
+        shape((block, depth), f32),
+        shape((TP, block, q_heads), f32),
+        shape((TP, block, depth), bf),
+        shape((total, qkv_width), bf),
+        shape((total, qkv_width // 2), bf),
+        shape((TP, block, depth), bf),
+        shape((TP, block, units), bf),
+        shape((TP, block, units), bf),
+        shape((TP, block, units), bf),
+    ]
+    n = len(moving)
+    scratch = [
+        pltpu.VMEM((TP, block, depth), bf),
+        pltpu.VMEM((TP, block, depth), bf),
+        pltpu.VMEM(moving[0].shape, bf),
+        pltpu.VMEM(moving[1].shape, bf),
+        pltpu.VMEM(moving[2].shape, bf),
+        pltpu.VMEM(moving[3].shape, bf),
+        pltpu.VMEM((total, qkv_width), bf),
+        pltpu.VMEM((total, qkv_width // 2), bf),
+        pltpu.VMEM((TP, block, units), bf),
+        pltpu.VMEM((TP, block, units), bf),
+        pltpu.VMEM((TP, block, units), bf),
+        pltpu.VMEM((2, block, depth), bf),
+        pltpu.VMEM((2, 2, block, depth), bf),
+        pltpu.VMEM((block, depth), bf),
+        pltpu.VMEM((2, block, depth), bf),
+    ] + sems(64, 24)
+    return pl.pallas_call(
+        functools.partial(forward_kernel, programs, n),
+        out_shape=outs,
+        in_specs=[IN_VMEM] * 7 + [ANYWHERE] * n,
+        out_specs=[ANYWHERE] * n + [IN_VMEM] * 3 + [ANYWHERE] * 7,
+        scratch_shapes=scratch,
+        input_output_aliases={7 + i: i for i in range(n)},
+        compiler_params=pltpu.CompilerParams(
+            collective_id=cid, has_side_effects=True, vmem_limit_bytes=VMEM_LIMIT
+        ),
+        cost_estimate=pl.CostEstimate(
+            flops=16 * 10**9, bytes_accessed=400 * 2**20, transcendentals=10**7
+        ),
+    )(x_own, gain_a, gain_f, cosine, sine, row_seg, col_seg, *moving)
+
+
+def column_pack(weights):
+    parts = []
+    for weight in weights:
+        layers, rows, width = weight.shape
+        view = weight.reshape(layers, rows, 2, TP, width // (2 * TP))
+        parts.append(view.transpose(0, 3, 1, 2, 4).reshape(layers, TP, rows, width // TP))
+    return jnp.concatenate(parts, axis=3)
+
+
 def fast_device(
     tokens, gain_attn, w_query, w_key, w_value, w_out, gain_ffn, w_gate, w_up, w_down, lengths, cotangent
 ):
@@ -826,37 +1246,13 @@
 
     out_in = inward(w_out.reshape(-1, depth)).reshape(w_out.shape)
     down_in = inward(w_down.reshape(-1, depth)).reshape(w_down.shape)
-    attn_own, ffn_own = [], []
-    for layer in range(2):
-        pieces = [
-            jnp.concatenate([column_pieces(fab, w, layer, k) for w in (w_query, w_key, w_value)], axis=1)
-            for k in range(TP)
-        ]
-        cols = exchange_columns(fab, pieces)
-        width = cols[0].shape[1]
-        own_out = out_in[layer]
-        attn_own.append(jnp.concatenate(cols + [own_out[:, :width], own_out[:, width:]], axis=0))
-        pieces = [
-            jnp.concatenate([column_pieces(fab, w, layer, k) for w in (w_gate, w_up)], axis=1)
-            for k in range(TP)
-        ]
-        cols = exchange_columns(fab, pieces)
-        units = cols[0].shape[1] // 2
-        dn = down_in[layer]
-        dr = dn.shape[0]
-        wide = jnp.concatenate([dn[: dr // 2, :units], dn[dr // 2 :, :units]], axis=1)
-        rest = jnp.concatenate([dn[s * dr // 4 : (s + 1) * dr // 4, units:] for s in range(4)], axis=1)
-        ffn_own.append(jnp.concatenate(cols + [wide, rest], axis=0))
-
-    gains = lax.all_gather(
-        jnp.concatenate([gain_attn, gain_ffn], axis=0), ("dp", "fsdp"), axis=0, tiled=False
-    )
-    gains = gains.reshape(2, TP, fab.z_size, 4, shard).transpose(3, 0, 2, 1, 4).reshape(4, depth)
-    gains = gains.astype(jnp.float32)
-
+    gain_tile = jnp.pad(
+        jnp.concatenate([gain_attn, gain_ffn], axis=0).astype(jnp.float32), ((0, 4), (0, 128 - shard))
+    )
     hidden = inward(fab.regroup(tokens)).astype(jnp.float32)
     cot = inward(fab.regroup(cotangent))
     lengths_row = fab.regroup(lengths)[0]
+    gains = None
 
     segment, position = layout(lengths_row, group_tok)
     base = halves_swapped(fab.q)
@@ -882,28 +1278,47 @@
         axis=1,
     )
 
-    places = jnp.arange(8, dtype=jnp.int32)
-    order = (places // 4 ^ fab.y) * 4 + (places % 4 // 2 ^ fab.z // 2) * 2 + (places % 2 ^ fab.z % 2)
-    saved, outs = [], []
-    for layer in range(2):
-        w_qkv, w_o = place_attn(order, gather_chunks(fab, attn_own[layer]), depth)
-        w_g, w_u, w_d = place_ffn(order, gather_chunks(fab, ffn_own[layer]), depth)
-        gain_a, gain_f = gains[layer], gains[2 + layer]
-        normed = fab.spread((hidden * inner_rsqrt(hidden) * gain_a).astype(jnp.bfloat16))
-        qkv = project_qkv(normed, w_qkv, cosine, sine)
-        mixed, lse = attend_fwd(slots, qkv, row_seg, col_seg)
-        middle = hidden + fab.collect(mixed, w_o)
-        normed_ffn = fab.spread((middle * inner_rsqrt(middle) * gain_f).astype(jnp.bfloat16))
-        gating = matmul(normed_ffn, w_g)
-        upward = matmul(normed_ffn, w_u)
-        activated = (jax.nn.silu(gating) * upward).astype(jnp.bfloat16)
-        result = middle + fab.collect(activated, w_d)
+    (g_qkv0, g_qkv1, g_gu0, g_gu1, g_out0, g_out1, g_down0, g_down1, g_gain, branch) = start_exchange(
+        column_pack((w_query, w_key, w_value)), column_pack((w_gate, w_up)), out_in, down_in, gain_tile, cot
+    )
+    gains = jnp.transpose(g_gain[:, :, :4, :shard], (2, 0, 1, 3)).reshape(4, 1, depth)
+    cols, drows, srows = TP * shard, g_down0.shape[1], shard
+    half = cols // 2
+    programs0 = (
+        (("y", 3, 0, drows), ("z", 2, 0, half)),
+        (("y", 2, 0, half), ("z", 2, half, half)),
+        (("y", 2, half, half), ("z", 4, 0, cols), ("z", 5, 0, srows)),
+        (("y", 4, 0, cols), ("y", 5, 0, srows), ("z", 7, 0, drows)),
+    )
+    programs1 = (
+        (("y", 3, 0, drows), ("z", 2, 0, half)),
+        (("y", 2, 0, half), ("z", 2, half, half)),
+        (("y", 2, half, half),),
+        (),
+    )
+    res = forward_layer(
+        programs0, 2, hidden, gains[0], gains[2], cosine, sine, row_seg, col_seg,
+        (g_qkv0, g_out0, g_gu0, g_down0, g_qkv1, g_out1, g_gu1, g_down1),
+    )
+    weights0, moving1, acts0 = res[:4], res[4:8], res[8:]
+    res = forward_layer(
+        programs1, 3, acts0[0], gains[1], gains[3], cosine, sine, row_seg, col_seg, moving1
+    )
+    weights1, acts1 = res[:4], res[4:]
+    outs = [
+        fab.regroup(outward(a[0].astype(jnp.bfloat16)).astype(jnp.bfloat16)) for a in (acts0, acts1)
+    ]
+    saved = []
+    for hid, weights, acts in ((hidden, weights0, acts0), (acts0[0], weights1, acts1)):
+        (x_next, middle, lse, normed, qkv, mixed, normed_ffn, gating, upward, activated) = acts
+        flat = lambda v: v.reshape(-1, v.shape[-1])
+        w_qkv, w_o, w_gu, w_d = (flat(w) for w in weights)
+        units = w_gu.shape[1] // 2
         saved.append(
-            (hidden, normed, qkv, mixed, lse, middle, normed_ffn,
-             gating.astype(jnp.bfloat16), upward.astype(jnp.bfloat16), activated, w_qkv, w_o, w_g, w_u, w_d)
-        )
-        hidden = result
-        outs.append(fab.regroup(outward(result.astype(jnp.bfloat16)).astype(jnp.bfloat16)))
+            (hid, flat(normed), qkv, mixed, lse, middle, flat(normed_ffn), flat(gating), flat(upward),
+             flat(activated), w_qkv, w_o, w_gu[:, :units], w_gu[:, units:], w_d)
+        )
+    gains = gains[:, 0]
 
     upstream = cot.astype(jnp.float32)
     grads = [None, None]
@@ -912,7 +1327,7 @@
         (hid, normed, qkv, mixed, lse, middle, normed_ffn, gating, upward, activated,
          w_qkv, w_o, w_g, w_u, w_d) = saved[layer]
         gain_a, gain_f = gains[layer], gains[2 + layer]
-        branch = fab.spread(upstream.astype(jnp.bfloat16))
+        branch = branch.reshape(-1, depth) if layer == 1 else fab.spread(upstream.astype(jnp.bfloat16))
         grad_act = matmul(branch, w_d.T)
         gating = gating.astype(jnp.float32)
         upward = upward.astype(jnp.float32)

time: 1530 us -> 1280 us (0.84)
  waiting for transfers between devices: 593 us -> 256 us
  Pallas kernels: 134 us -> 466 us
  starting transfers between devices: 227 us -> 161 us
  blocking collectives: 116 us -> 50.7 us
  matrix products: 200 us -> 152 us
  local copies, waits for them, and re-layouts: 164 us -> 126 us
  other arithmetic: 82.2 us -> 55.1 us
    pallas_call x8 -> x3, Pallas kernels: 76.8 us -> 409 us  [the longest x2 320 us: forward_layer(): pl.pallas_call(functools.partial(forward_kernel, programs, n), out_shape=...]
    ppermute x80 -> x34, waiting for transfers between devices: 349 us -> 118 us  [rank(): return lax.ppermute(values, 'dp', flip_dp(self.dp_size, bits))]
    ppermute x36 -> x24, waiting for transfers between devices: 244 us -> 137 us  [over_z(): return lax.ppermute(values, 'fsdp', flip_z(self.z_size, bits))]
    ppermute x80 -> x34, starting transfers between devices: 101 us -> 21.3 us  [rank(): return lax.ppermute(values, 'dp', flip_dp(self.dp_size, bits))]
    all_gather x1 -> x0, blocking collectives: 65.2 us -> none  [fast_device(): lax.all_gather(jnp.concatenate([gain_attn, gain_ffn], axis=0), ('dp', 'fs...]
    dot_general x40 -> x28, matrix products: 164 us -> 114 us  [matmul(): return jnp.dot(left, right, preferred_element_type=jnp.float32)]
    unnamed x380 -> x197, local copies, waits for them, and re-layouts: 55.2 us -> 9.16 us
    dynamic_slice x10 -> x0, local copies, waits for them, and re-layouts: 30.1 us -> none  [column_pieces(): lax.dynamic_index_in_dim(view, chosen, 2, keepdims=False)]
  transfers between devices with their start and end apart: 122 -> 64, of which waited for: 46 -> 23; matrix products, arithmetic and copies ran while one was open for 23% -> 21% of each run, Pallas kernels for 7% -> 12%
where the time goes in v2:
time: 1280 us; the launch traced here: 1270 us
  Pallas kernels  466 us (36%)
  waiting for transfers between devices  256 us (20%)
  starting transfers between devices  161 us (13%)
  matrix products  152 us (12%)
  local copies, waits for them, and re-layouts  126 us (10%)
  other arithmetic  55.1 us (4%)
  blocking collectives  50.7 us (4%)
    pallas_call x2, Pallas kernels, forward_layer(): pl.pallas_call(functools.partial(forward_kernel, programs, n), out_shape=...  320 us
    ppermute x24, waiting for transfers between devices, over_z(): return lax.ppermute(values, 'fsdp', flip_z(self.z_size, bits))  137 us
    ppermute x34, waiting for transfers between devices, rank(): return lax.ppermute(values, 'dp', flip_dp(self.dp_size, bits))  118 us
    dot_general x28, matrix products, matmul(): return jnp.dot(left, right, preferred_element_type=jnp.float32)  114 us
    ppermute x24, starting transfers between devices, over_z(): return lax.ppermute(values, 'fsdp', flip_z(self.z_size, bits))  106 us
    pallas_call x1, Pallas kernels, start_exchange(): pl.pallas_call(start_kernel, out_shape=outs, in_specs=[ANYWHERE] * 6, out...  89.7 us
    pallas_call x2, Pallas kernels, attend_bwd(): pl.pallas_call(attend_bwd_kernel, out_shape=jax.ShapeDtypeStruct((total,...  56.9 us
    psum x1, blocking collectives, fast_device(): gain_sums = lax.psum(jnp.stack(gain_grads), ('dp', 'fsdp'))  50.7 us
  transfers between devices with their start and end apart: 64, of which 23 were waited for; matrix products, arithmetic and copies ran while one was open for 21% of the time, Pallas kernels for 12%

profile of v2, /device:TPU:0, one launch (start us, length us, event | category | flops | bytes accessed | tf_op | source)
XLA Modules:
  0.0 1269.5 jit_solution(16637452347938135240)
XLA Ops:
  2.1 7.4 collective-permute-start.1
  9.5 7.4 collective-permute-start
  37.3 6.1 concatenate.47.refs_3_.cos_ref
  43.5 6.1 concatenate.48.refs_4_.sin_ref
  53.7 89.7 %shard_map.203 = (bf16[8,192,768]{2,1,0:T(8,128)(2,1)}, bf16[8,192,768]{2,1,0:T(8,128)(2,1)}, bf16[8,192,2048]{2,1,0:T(8,128)(2,1)}, bf16[8,192,2048]{2,1,0:T(8,...) custom-call(bf16[2,4,48,768]{3,2,1,0:T(8,128)(2,1)} %pad_maximum_fus, ...), custom_call_target="tpu_custom_call" | custom-call | bytes 314572800 | tf_op jit(solution)/shard_map/pallas_call | solution.py:988
  151.6 155.3 %shard_map.204 = (bf16[8,192,768]{2,1,0:T(8,128)(2,1)}, bf16[8,48,1536]{2,1,0:T(8,128)(2,1)}, bf16[8,192,2048]{2,1,0:T(8,128)(2,1)}, bf16[8,128,1536]{2,1,0:T(8,...) custom-call(f32[256,1536]{1,0:T(8,128)} %get-tuple-element.215.refs_, ...), custom_call_target="tpu_custom_call", output_to_operand_aliasing={{0}: (7, {}), {1}: (8, {}), {2}: (9, {}), {3}: (10, {}), {4... | custom-call | flops 16000000000 | bytes 419430400 | tf_op jit(solution)/shard_map/pallas_call | solution.py:1202
  306.9 164.4 %shard_map.205 = (bf16[8,192,768]{2,1,0:T(8,128)(2,1)}, bf16[8,48,1536]{2,1,0:T(8,128)(2,1)}, bf16[8,192,2048]{2,1,0:T(8,128)(2,1)}, bf16[8,128,1536]{2,1,0:T(8,...) custom-call(f32[256,1536]{1,0:T(8,128)} %get-tuple-element.62.refs_0, ...), custom_call_target="tpu_custom_call", output_to_operand_aliasing={{0}: (7, {}), {1}: (8, {}), {2}: (9, {}), {3}: (10, {})} | custom-call | flops 16000000000 | bytes 419430400 | tf_op jit(solution)/shard_map/pallas_call | solution.py:1202
  471.3 6.5 bitcast_convert_fusion.1
  477.8 5.3 copy.103
  483.1 5.5 copy.104
  488.6 9.9 multiply_convert_fusion.2
  498.6 4.9 convolution_convert_fusion.7
  509.1 8.1 convolution_convert_fusion
  521.9 5.0 convert_add_fusion.3
  530.5 7.4 collective-permute-start.4
  537.9 7.4 collective-permute-start.3
  545.9 4.6 bitcast_convert_fusion
  550.5 8.7 collective-permute-done.6
  564.6 5.4 copy.108
  570.0 5.3 copy.109
  580.0 17.4 %collective-permute-done.7 = bf16[256,1536]{1,0:T(8,128)(2,1)S(1)} collective-permute-done((bf16[256,1536]{1,0:T(8,128)(2,1)S(1)}, bf16[256,1536]{1,0:T(8,128)(2,1)S(1)}, u32[]{:S(2)}, u32[]{:S(2)}) %collective-permute-start.7) | collective-permute-done | bytes 786464 | tf_op jit(solution)/shard_map/ppermute | solution.py:710
  597.6 14.2 %collective-permute-done.49 = bf16[768,2048]{1,0:T(8,128)(2,1)} collective-permute-done((bf16[768,2048]{1,0:T(8,128)(2,1)}, bf16[768,2048]{1,0:T(8,128)(2,1)}, u32[]{:S(2)}, u32[]{:S(2)}) %collective-permute-start.49) | collective-permute-done | bytes 3145760 | tf_op jit(solution)/shard_map/ppermute | solution.py:710
  611.9 6.2 add_convert_fusion
  618.3 11.8 collective-permute-start.50
  637.1 27.2 %collective-permute-done.50 = bf16[192,2048]{1,0:T(8,128)(2,1)S(1)} collective-permute-done((bf16[192,2048]{1,0:T(8,128)(2,1)S(1)}, bf16[192,2048]{1,0:T(8,128)(2,1)S(1)}, u32[]{:S(2)}, u32[]{:S(2)}) %collective-permute-start.50) | collective-permute-done | bytes 786464 | tf_op jit(solution)/shard_map/ppermute | solution.py:722
  664.2 21.0 %collective-permute-done.51 = bf16[192,2048]{1,0:T(8,128)(2,1)S(1)} collective-permute-done((bf16[192,2048]{1,0:T(8,128)(2,1)S(1)}, bf16[192,2048]{1,0:T(8,128)(2,1)S(1)}, u32[]{:S(2)}, u32[]{:S(2)}) %collective-permute-start.51) | collective-permute-done | bytes 786464 | tf_op jit(solution)/shard_map/ppermute | solution.py:722
  690.5 28.1 %shard_map.206 = bf16[1024,768]{1,0:T(8,128)(2,1)} custom-call(s32[4]{0:T(128)} %get-tuple-element.116.slot_ref, bf16[1024,768]{1,0:T(8,128)(2,1)} %get-tuple-element.74.qkv_ref, bf16[1024,384]{1,0:T(8,128)(2,1)} %convolution_convert_fusion.11.grad_ref, bf16[1024,384]{1,0:T(8,128)(2,1)} %get-tuple-element.76.mixed_ref, ...), custom_call_target="tpu_custom_call" | custom-call | flops 4026531840 | bytes 9437184 | tf_op jit(solution)/shard_map/pallas_call | solution.py:606
  727.5 4.9 fusion.37
  771.3 19.7 %collective-permute-done.27 = bf16[768,768]{1,0:T(8,128)(2,1)S(1)} collective-permute-done((bf16[768,768]{1,0:T(8,128)(2,1)S(1)}, bf16[768,768]{1,0:T(8,128)(2,1)S(1)}, u32[]{:S(2)}, u32[]{:S(2)}) %collective-permute-start.27) | collective-permute-done | bytes 1179680 | tf_op jit(solution)/shard_map/ppermute | solution.py:710
  792.6 32.4 %collective-permute-start.28 = (bf16[192,768]{1,0:T(8,128)(2,1)S(1)}, bf16[192,768]{1,0:T(8,128)(2,1)S(1)}, u32[]{:S(2)}, u32[]{:S(2)}) collective-permute-start(bf16[192,768]{1,0:T(8,128)(2,1)S(1)} %get-tuple-element.144), channel_id=1, source_target_pairs={{0,1},{1,0},{2,3},{3,2},{4,5},{5,4},{6,7},{7,6},{8,9},{9,8},{10,11... | collective-permute-start | bytes 884744 | tf_op jit(solution)/shard_map/ppermute | solution.py:722
  828.5 7.2 collective-permute-start.39
  836.3 15.9 %collective-permute-done.29 = bf16[192,768]{1,0:T(8,128)(2,1)S(1)} collective-permute-done((bf16[192,768]{1,0:T(8,128)(2,1)S(1)}, bf16[192,768]{1,0:T(8,128)(2,1)S(1)}, u32[]{:S(2)}, u32[]{:S(2)}) %collective-permute-start.29) | collective-permute-done | bytes 294944 | tf_op jit(solution)/shard_map/ppermute | solution.py:722
  855.2 6.7 collective-permute-done.40
  869.5 7.1 multiply_convert_fusion
  876.7 5.2 convolution_convert_fusion.5
  883.1 7.2 convolution_convert_fusion.1
  891.2 13.6 %collective-permute-done.56 = bf16[512,1536]{1,0:T(8,128)(2,1)} collective-permute-done((bf16[512,1536]{1,0:T(8,128)(2,1)S(1)}, bf16[512,1536]{1,0:T(8,128)(2,1)}, u32[]{:S(2)}, u32[]{:S(2)}) %collective-permute-start.56) | collective-permute-done | bytes 1572896 | tf_op jit(solution)/shard_map/ppermute | solution.py:710
  955.8 16.0 %collective-permute-done.42 = bf16[768,2048]{1,0:T(8,128)(2,1)} collective-permute-done((bf16[768,2048]{1,0:T(8,128)(2,1)}, bf16[768,2048]{1,0:T(8,128)(2,1)}, u32[]{:S(2)}, u32[]{:S(2)}) %collective-permute-start.42) | collective-permute-done | bytes 3145760 | tf_op jit(solution)/shard_map/ppermute | solution.py:710
  971.8 6.0 add_convert_fusion.1
  986.2 26.7 %collective-permute-done.43 = bf16[192,2048]{1,0:T(8,128)(2,1)S(1)} collective-permute-done((bf16[192,2048]{1,0:T(8,128)(2,1)S(1)}, bf16[192,2048]{1,0:T(8,128)(2,1)S(1)}, u32[]{:S(2)}, u32[]{:S(2)}) %collective-permute-start.43) | collective-permute-done | bytes 786464 | tf_op jit(solution)/shard_map/ppermute | solution.py:722
  1013.0 21.3 %collective-permute-done.44 = bf16[192,2048]{1,0:T(8,128)(2,1)S(1)} collective-permute-done((bf16[192,2048]{1,0:T(8,128)(2,1)S(1)}, bf16[192,2048]{1,0:T(8,128)(2,1)S(1)}, u32[]{:S(2)}, u32[]{:S(2)}) %collective-permute-start.44) | collective-permute-done | bytes 786464 | tf_op jit(solution)/shard_map/ppermute | solution.py:722
  1037.1 5.0 collective-permute-done.46
  1075.3 28.8 %shard_map.207 = bf16[1024,768]{1,0:T(8,128)(2,1)} custom-call(s32[4]{0:T(128)} %get-tuple-element.116.slot_ref, bf16[1024,768]{1,0:T(8,128)(2,1)} %get-tuple-element.84.qkv_ref, bf16[1024,384]{1,0:T(8,128)(2,1)} %convolution_convert_fusion.10.grad_ref, bf16[1024,384]{1,0:T(8,128)(2,1)} %get-tuple-element.86.mixed_ref, ...), custom_call_target="tpu_custom_call" | custom-call | flops 4026531840 | bytes 9437184 | tf_op jit(solution)/shard_map/pallas_call | solution.py:606
  1115.1 15.3 %collective-permute-start.35 = (bf16[48,1536]{1,0:T(8,128)(2,1)S(1)}, bf16[48,1536]{1,0:T(8,128)(2,1)S(1)}, u32[]{:S(2)}, u32[]{:S(2)}) collective-permute-start(bf16[48,1536]{1,0:T(8,128)(2,1)S(1)} %get-tuple-element.153), channel_id=1, source_target_pairs={{0,1},{1,0},{2,3},{3,2},{4,5},{5,4},{6,7},{7,6},{8,9},{9,8},{10,11... | collective-permute-start | bytes 442376 | tf_op jit(solution)/shard_map/ppermute | solution.py:722
  1139.0 15.4 %collective-permute-start.21 = (bf16[192,768]{1,0:T(8,128)(2,1)S(1)}, bf16[192,768]{1,0:T(8,128)(2,1)S(1)}, u32[]{:S(2)}, u32[]{:S(2)}) collective-permute-start(bf16[192,768]{1,0:T(8,128)(2,1)S(1)} %get-tuple-element.141), channel_id=1, source_target_pairs={{0,1},{1,0},{2,3},{3,2},{4,5},{5,4},{6,7},{7,6},{8,9},{9,8},{10,11... | collective-permute-start | bytes 884744 | tf_op jit(solution)/shard_map/ppermute | solution.py:722
  1165.2 12.6 collective-permute-done.22
  1198.9 9.4 collective-permute-done.18
  1216.5 50.7 %psum.7 = f32[4,1536]{1,0:T(4,128)S(1)} all-reduce(f32[4,1536]{1,0:T(4,128)S(1)} %pad_maximum_fusion.31), channel_id=1, replica_groups=mesh['dp'=8,'fsdp'=4] {'dp','fsdp'}, use_global_device_ids=true, to_apply=%region_16.17 | all-reduce | flops 6144 | bytes 49152 | tf_op jit(solution)/shard_map/psum | solution.py:1368
  (535 shorter events, 292.4 us)
Async XLA Ops:
  0.7 31.1 %collective-permute-start.2 = (s32[1,4]{1,0:T(1,128)}, s32[1,4]{1,0:T(1,128)S(1)}, u32[]{:S(2)}, u32[]{:S(2)}) collective-permute-start(s32[1,4]{1,0:T(1,128)} %param.22), channel_id=1, source_target_pairs={{0,0},{1,8},{2,4},{3,12},{4,2},{5,10},{6,6},{7,14},{8,1},{9,9},{10... | collective-permute-start | bytes 56 | tf_op jit(solution)/shard_map/ppermute | solution.py:725
  2.1 47.5 %collective-permute-start.1 = (bf16[256,1536]{1,0:T(8,128)(2,1)}, bf16[256,1536]{1,0:T(8,128)(2,1)}, u32[]{:S(2)}, u32[]{:S(2)}) collective-permute-start(bf16[256,1536]{1,0:T(8,128)(2,1)} %param.23), channel_id=1, source_target_pairs={{0,0},{1,8},{2,4},{3,12},{4,2},{5,10},{6,6},{7,14},{8,1},{9,9},{10... | collective-permute-start | bytes 2359304 | tf_op jit(solution)/shard_map/ppermute | solution.py:725
  9.5 137.8 %collective-permute-start = (bf16[256,1536]{1,0:T(8,128)(2,1)}, bf16[256,1536]{1,0:T(8,128)(2,1)}, u32[]{:S(2)}, u32[]{:S(2)}) collective-permute-start(bf16[256,1536]{1,0:T(8,128)(2,1)} %param.12), channel_id=1, source_target_pairs={{0,0},{1,8},{2,4},{3,12},{4,2},{5,10},{6,6},{7,14},{8,1},{9,9},{10... | collective-permute-start | bytes 2359304 | tf_op jit(solution)/shard_map/ppermute | solution.py:725
  506.7 125.9 %collective-permute-start.60 = (bf16[512,1536]{1,0:T(8,128)(2,1)}, bf16[512,1536]{1,0:T(8,128)(2,1)}, u32[]{:S(2)}, u32[]{:S(2)}) collective-permute-start(bf16[512,1536]{1,0:T(8,128)(2,1)} %convolution_convert_fusion.2), channel_id=1, source_target_pairs={{0,16},{4,20},{8,24},{12,28},{16,0},{20,4},{24,8},{28,12},{1,17},{... | collective-permute-start | bytes 4718600 | tf_op jit(solution)/shard_map/ppermute | solution.py:710
  517.2 94.6 %collective-permute-start.49 = (bf16[768,2048]{1,0:T(8,128)(2,1)}, bf16[768,2048]{1,0:T(8,128)(2,1)}, u32[]{:S(2)}, u32[]{:S(2)}) collective-permute-start(bf16[768,2048]{1,0:T(8,128)(2,1)} %convolution_convert_fusion), channel_id=1, source_target_pairs={{0,16},{4,20},{8,24},{12,28},{16,0},{20,4},{24,8},{28,12},{1,17},{... | collective-permute-start | bytes 9437192 | tf_op jit(solution)/shard_map/ppermute | solution.py:710
  527.0 32.2 %collective-permute-start.6 = (bf16[256,1536]{1,0:T(8,128)(2,1)S(1)}, bf16[256,1536]{1,0:T(8,128)(2,1)S(1)}, u32[]{:S(2)}, u32[]{:S(2)}) collective-permute-start(bf16[256,1536]{1,0:T(8,128)(2,1)S(1)} %slice.429), channel_id=1, source_target_pairs={{0,8},{4,12},{8,0},{12,4},{16,24},{20,28},{24,16},{28,20},{1,9},{5... | collective-permute-start | bytes 2359304 | tf_op jit(solution)/shard_map/ppermute | solution.py:710
  530.5 46.7 %collective-permute-start.4 = (bf16[256,1536]{1,0:T(8,128)(2,1)}, bf16[256,1536]{1,0:T(8,128)(2,1)}, u32[]{:S(2)}, u32[]{:S(2)}) collective-permute-start(bf16[256,1536]{1,0:T(8,128)(2,1)} %fusion.31), channel_id=1, source_target_pairs={{0,0},{1,8},{2,4},{3,12},{4,2},{5,10},{6,6},{7,14},{8,1},{9,9},{10... | collective-permute-start | bytes 2359304 | tf_op jit(solution)/shard_map/ppermute | solution.py:725
  537.9 39.3 %collective-permute-start.3 = (bf16[256,1536]{1,0:T(8,128)(2,1)}, bf16[256,1536]{1,0:T(8,128)(2,1)}, u32[]{:S(2)}, u32[]{:S(2)}) collective-permute-start(bf16[256,1536]{1,0:T(8,128)(2,1)} %fusion.30), channel_id=1, source_target_pairs={{0,0},{1,8},{2,4},{3,12},{4,2},{5,10},{6,6},{7,14},{8,1},{9,9},{10... | collective-permute-start | bytes 2359304 | tf_op jit(solution)/shard_map/ppermute | solution.py:725
  561.7 35.7 %collective-permute-start.7 = (bf16[256,1536]{1,0:T(8,128)(2,1)S(1)}, bf16[256,1536]{1,0:T(8,128)(2,1)S(1)}, u32[]{:S(2)}, u32[]{:S(2)}) collective-permute-start(bf16[256,1536]{1,0:T(8,128)(2,1)S(1)} %get-tuple-element.113), channel_id=1, source_target_pairs={{0,8},{4,12},{8,0},{12,4},{16,24},{20,28},{24,16},{28,20},{1,9},{5... | collective-permute-start | bytes 2359304 | tf_op jit(solution)/shard_map/ppermute | solution.py:710
  597.5 90.2 %collective-permute-start.8 = (bf16[512,1536]{1,0:T(8,128)(2,1)S(1)}, bf16[512,1536]{1,0:T(8,128)(2,1)S(1)}, u32[]{:S(2)}, u32[]{:S(2)}) collective-permute-start(bf16[512,1536]{1,0:T(8,128)(2,1)S(1)} %pad_maximum_fusion.15), channel_id=1, source_target_pairs={{0,4},{4,0},{8,12},{12,8},{16,20},{20,16},{24,28},{28,24},{1,5},{5... | collective-permute-start | bytes 4718600 | tf_op jit(solution)/shard_map/ppermute | solution.py:710
  618.3 45.9 %collective-permute-start.50 = (bf16[192,2048]{1,0:T(8,128)(2,1)S(1)}, bf16[192,2048]{1,0:T(8,128)(2,1)S(1)}, u32[]{:S(2)}, u32[]{:S(2)}) collective-permute-start(bf16[192,2048]{1,0:T(8,128)(2,1)S(1)} %get-tuple-element.124), channel_id=1, source_target_pairs={{0,1},{1,0},{2,3},{3,2},{4,5},{5,4},{6,7},{7,6},{8,9},{9,8},{10,11... | collective-permute-start | bytes 2359304 | tf_op jit(solution)/shard_map/ppermute | solution.py:722
  630.1 55.1 %collective-permute-start.51 = (bf16[192,2048]{1,0:T(8,128)(2,1)S(1)}, bf16[192,2048]{1,0:T(8,128)(2,1)S(1)}, u32[]{:S(2)}, u32[]{:S(2)}) collective-permute-start(bf16[192,2048]{1,0:T(8,128)(2,1)S(1)} %get-tuple-element.126), channel_id=1, source_target_pairs={{0,2},{1,3},{2,0},{3,1},{4,6},{5,7},{6,4},{7,5},{8,10},{9,11},{10,... | collective-permute-start | bytes 2359304 | tf_op jit(solution)/shard_map/ppermute | solution.py:722
  630.7 56.5 %collective-permute-start.52 = (bf16[192,2048]{1,0:T(8,128)(2,1)S(1)}, bf16[192,2048]{1,0:T(8,128)(2,1)S(1)}, u32[]{:S(2)}, u32[]{:S(2)}) collective-permute-start(bf16[192,2048]{1,0:T(8,128)(2,1)S(1)} %get-tuple-element.125), channel_id=1, source_target_pairs={{0,3},{1,2},{2,1},{3,0},{4,7},{5,6},{6,5},{7,4},{8,11},{9,10},{10,... | collective-permute-start | bytes 2359304 | tf_op jit(solution)/shard_map/ppermute | solution.py:722
  635.9 87.3 %collective-permute-start.61 = (bf16[128,1536]{1,0:T(8,128)(2,1)S(1)}, bf16[128,1536]{1,0:T(8,128)(2,1)}, u32[]{:S(2)}, u32[]{:S(2)}) collective-permute-start(bf16[128,1536]{1,0:T(8,128)(2,1)S(1)} %get-tuple-element.130), channel_id=1, source_target_pairs={{0,1},{1,0},{2,3},{3,2},{4,5},{5,4},{6,7},{7,6},{8,9},{9,8},{10,11... | collective-permute-start | bytes 1179656 | tf_op jit(solution)/shard_map/ppermute | solution.py:722
  664.2 63.2 %collective-permute-start.62 = (bf16[128,1536]{1,0:T(8,128)(2,1)S(1)}, bf16[128,1536]{1,0:T(8,128)(2,1)}, u32[]{:S(2)}, u32[]{:S(2)}) collective-permute-start(bf16[128,1536]{1,0:T(8,128)(2,1)S(1)} %get-tuple-element.132), channel_id=1, source_target_pairs={{0,2},{1,3},{2,0},{3,1},{4,6},{5,7},{6,4},{7,5},{8,10},{9,11},{10,... | collective-permute-start | bytes 1179656 | tf_op jit(solution)/shard_map/ppermute | solution.py:722
  685.2 42.2 %collective-permute-start.63 = (bf16[128,1536]{1,0:T(8,128)(2,1)S(1)}, bf16[128,1536]{1,0:T(8,128)(2,1)}, u32[]{:S(2)}, u32[]{:S(2)}) collective-permute-start(bf16[128,1536]{1,0:T(8,128)(2,1)S(1)} %get-tuple-element.131), channel_id=1, source_target_pairs={{0,3},{1,2},{2,1},{3,0},{4,7},{5,6},{6,5},{7,4},{8,11},{9,10},{10,... | collective-permute-start | bytes 1179656 | tf_op jit(solution)/shard_map/ppermute | solution.py:722
  762.0 29.0 %collective-permute-start.27 = (bf16[768,768]{1,0:T(8,128)(2,1)S(1)}, bf16[768,768]{1,0:T(8,128)(2,1)S(1)}, u32[]{:S(2)}, u32[]{:S(2)}) collective-permute-start(bf16[768,768]{1,0:T(8,128)(2,1)S(1)} %fusion.76), channel_id=1, source_target_pairs={{0,16},{4,20},{8,24},{12,28},{16,0},{20,4},{24,8},{28,12},{1,17},{... | collective-permute-start | bytes 3538952 | tf_op jit(solution)/shard_map/ppermute | solution.py:710
  768.8 58.5 %collective-permute-start.11 = (bf16[256,1536]{1,0:T(8,128)(2,1)S(1)}, bf16[256,1536]{1,0:T(8,128)(2,1)S(1)}, u32[]{:S(2)}, u32[]{:S(2)}) collective-permute-start(bf16[256,1536]{1,0:T(8,128)(2,1)S(1)} %get-tuple-element.111), channel_id=1, source_target_pairs={{0,8},{4,12},{8,0},{12,4},{16,24},{20,28},{24,16},{28,20},{1,9},{5... | collective-permute-start | bytes 2359304 | tf_op jit(solution)/shard_map/ppermute | solution.py:710
  770.6 56.9 %collective-permute-start.38 = (bf16[192,1536]{1,0:T(8,128)(2,1)S(1)}, bf16[192,1536]{1,0:T(8,128)(2,1)S(1)}, u32[]{:S(2)}, u32[]{:S(2)}) collective-permute-start(bf16[192,1536]{1,0:T(8,128)(2,1)S(1)} %convolution_convert_fusion.8), channel_id=1, source_target_pairs={{0,16},{4,20},{8,24},{12,28},{16,0},{20,4},{24,8},{28,12},{1,17},{... | collective-permute-start | bytes 1769480 | tf_op jit(solution)/shard_map/ppermute | solution.py:710
  792.6 43.2 %collective-permute-start.28 = (bf16[192,768]{1,0:T(8,128)(2,1)S(1)}, bf16[192,768]{1,0:T(8,128)(2,1)S(1)}, u32[]{:S(2)}, u32[]{:S(2)}) collective-permute-start(bf16[192,768]{1,0:T(8,128)(2,1)S(1)} %get-tuple-element.144), channel_id=1, source_target_pairs={{0,1},{1,0},{2,3},{3,2},{4,5},{5,4},{6,7},{7,6},{8,9},{9,8},{10,11... | collective-permute-start | bytes 884744 | tf_op jit(solution)/shard_map/ppermute | solution.py:722
  824.9 27.3 %collective-permute-start.29 = (bf16[192,768]{1,0:T(8,128)(2,1)S(1)}, bf16[192,768]{1,0:T(8,128)(2,1)S(1)}, u32[]{:S(2)}, u32[]{:S(2)}) collective-permute-start(bf16[192,768]{1,0:T(8,128)(2,1)S(1)} %get-tuple-element.146), channel_id=1, source_target_pairs={{0,2},{1,3},{2,0},{3,1},{4,6},{5,7},{6,4},{7,5},{8,10},{9,11},{10,... | collective-permute-start | bytes 884744 | tf_op jit(solution)/shard_map/ppermute | solution.py:722
  825.5 28.6 %collective-permute-start.30 = (bf16[192,768]{1,0:T(8,128)(2,1)S(1)}, bf16[192,768]{1,0:T(8,128)(2,1)S(1)}, u32[]{:S(2)}, u32[]{:S(2)}) collective-permute-start(bf16[192,768]{1,0:T(8,128)(2,1)S(1)} %get-tuple-element.145), channel_id=1, source_target_pairs={{0,3},{1,2},{2,1},{3,0},{4,7},{5,6},{6,5},{7,4},{8,11},{9,10},{10,... | collective-permute-start | bytes 884744 | tf_op jit(solution)/shard_map/ppermute | solution.py:722
  827.5 38.0 %collective-permute-start.12 = (bf16[512,1536]{1,0:T(8,128)(2,1)S(1)}, bf16[512,1536]{1,0:T(8,128)(2,1)S(1)}, u32[]{:S(2)}, u32[]{:S(2)}) collective-permute-start(bf16[512,1536]{1,0:T(8,128)(2,1)S(1)} %pad_maximum_fusion.16), channel_id=1, source_target_pairs={{0,4},{4,0},{8,12},{12,8},{16,20},{20,16},{24,28},{28,24},{1,5},{5... | collective-permute-start | bytes 4718600 | tf_op jit(solution)/shard_map/ppermute | solution.py:710
  828.5 25.9 %collective-permute-start.39 = (bf16[48,1536]{1,0:T(8,128)(2,1)S(1)}, bf16[48,1536]{1,0:T(8,128)(2,1)S(1)}, u32[]{:S(2)}, u32[]{:S(2)}) collective-permute-start(bf16[48,1536]{1,0:T(8,128)(2,1)S(1)} %get-tuple-element.156), channel_id=1, source_target_pairs={{0,1},{1,0},{2,3},{3,2},{4,5},{5,4},{6,7},{7,6},{8,9},{9,8},{10,11... | collective-permute-start | bytes 442376 | tf_op jit(solution)/shard_map/ppermute | solution.py:722
  835.8 26.2 %collective-permute-start.40 = (bf16[48,1536]{1,0:T(8,128)(2,1)S(1)}, bf16[48,1536]{1,0:T(8,128)(2,1)S(1)}, u32[]{:S(2)}, u32[]{:S(2)}) collective-permute-start(bf16[48,1536]{1,0:T(8,128)(2,1)S(1)} %get-tuple-element.158), channel_id=1, source_target_pairs={{0,2},{1,3},{2,0},{3,1},{4,6},{5,7},{6,4},{7,5},{8,10},{9,11},{10,... | collective-permute-start | bytes 442376 | tf_op jit(solution)/shard_map/ppermute | solution.py:722
  867.4 37.4 %collective-permute-start.56 = (bf16[512,1536]{1,0:T(8,128)(2,1)S(1)}, bf16[512,1536]{1,0:T(8,128)(2,1)}, u32[]{:S(2)}, u32[]{:S(2)}) collective-permute-start(bf16[512,1536]{1,0:T(8,128)(2,1)S(1)} %convolution_convert_fusion.3), channel_id=1, source_target_pairs={{0,16},{4,20},{8,24},{12,28},{16,0},{20,4},{24,8},{28,12},{1,17},{... | collective-permute-start | bytes 4718600 | tf_op jit(solution)/shard_map/ppermute | solution.py:710
  881.8 31.9 %collective-permute-start.13 = (bf16[512,1536]{1,0:T(8,128)(2,1)S(1)}, bf16[512,1536]{1,0:T(8,128)(2,1)S(1)}, u32[]{:S(2)}, u32[]{:S(2)}) collective-permute-start(bf16[512,1536]{1,0:T(8,128)(2,1)S(1)} %convolution_convert_fusion.5), channel_id=1, source_target_pairs={{0,4},{4,0},{8,12},{12,8},{16,20},{20,16},{24,28},{28,24},{1,5},{5... | collective-permute-start | bytes 4718600 | tf_op jit(solution)/shard_map/ppermute | solution.py:710
  890.3 81.5 %collective-permute-start.42 = (bf16[768,2048]{1,0:T(8,128)(2,1)}, bf16[768,2048]{1,0:T(8,128)(2,1)}, u32[]{:S(2)}, u32[]{:S(2)}) collective-permute-start(bf16[768,2048]{1,0:T(8,128)(2,1)} %convolution_convert_fusion.1), channel_id=1, source_target_pairs={{0,16},{4,20},{8,24},{12,28},{16,0},{20,4},{24,8},{28,12},{1,17},{... | collective-permute-start | bytes 9437192 | tf_op jit(solution)/shard_map/ppermute | solution.py:710
  909.1 42.1 %collective-permute-start.57 = (bf16[128,1536]{1,0:T(8,128)(2,1)}, bf16[128,1536]{1,0:T(8,128)(2,1)}, u32[]{:S(2)}, u32[]{:S(2)}) collective-permute-start(bf16[128,1536]{1,0:T(8,128)(2,1)} %get-tuple-element.127), channel_id=1, source_target_pairs={{0,1},{1,0},{2,3},{3,2},{4,5},{5,4},{6,7},{7,6},{8,9},{9,8},{10,11... | collective-permute-start | bytes 1179656 | tf_op jit(solution)/shard_map/ppermute | solution.py:722
  911.4 39.9 %collective-permute-start.58 = (bf16[128,1536]{1,0:T(8,128)(2,1)}, bf16[128,1536]{1,0:T(8,128)(2,1)}, u32[]{:S(2)}, u32[]{:S(2)}) collective-permute-start(bf16[128,1536]{1,0:T(8,128)(2,1)} %get-tuple-element.129), channel_id=1, source_target_pairs={{0,2},{1,3},{2,0},{3,1},{4,6},{5,7},{6,4},{7,5},{8,10},{9,11},{10,... | collective-permute-start | bytes 1179656 | tf_op jit(solution)/shard_map/ppermute | solution.py:722
  911.9 39.4 %collective-permute-start.59 = (bf16[128,1536]{1,0:T(8,128)(2,1)}, bf16[128,1536]{1,0:T(8,128)(2,1)}, u32[]{:S(2)}, u32[]{:S(2)}) collective-permute-start(bf16[128,1536]{1,0:T(8,128)(2,1)} %get-tuple-element.128), channel_id=1, source_target_pairs={{0,3},{1,2},{2,1},{3,0},{4,7},{5,6},{6,5},{7,4},{8,11},{9,10},{10,... | collective-permute-start | bytes 1179656 | tf_op jit(solution)/shard_map/ppermute | solution.py:722
  919.0 36.2 %collective-permute-start.14 = (bf16[256,1536]{1,0:T(8,128)(2,1)S(1)}, bf16[256,1536]{1,0:T(8,128)(2,1)S(1)}, u32[]{:S(2)}, u32[]{:S(2)}) collective-permute-start(bf16[256,1536]{1,0:T(8,128)(2,1)S(1)} %slice.427), channel_id=1, source_target_pairs={{0,8},{4,12},{8,0},{12,4},{16,24},{20,28},{24,16},{28,20},{1,9},{5... | collective-permute-start | bytes 2359304 | tf_op jit(solution)/shard_map/ppermute | solution.py:710
  978.1 34.8 %collective-permute-start.43 = (bf16[192,2048]{1,0:T(8,128)(2,1)S(1)}, bf16[192,2048]{1,0:T(8,128)(2,1)S(1)}, u32[]{:S(2)}, u32[]{:S(2)}) collective-permute-start(bf16[192,2048]{1,0:T(8,128)(2,1)S(1)} %get-tuple-element.121), channel_id=1, source_target_pairs={{0,1},{1,0},{2,3},{3,2},{4,5},{5,4},{6,7},{7,6},{8,9},{9,8},{10,11... | collective-permute-start | bytes 2359304 | tf_op jit(solution)/shard_map/ppermute | solution.py:722
  979.2 55.1 %collective-permute-start.44 = (bf16[192,2048]{1,0:T(8,128)(2,1)S(1)}, bf16[192,2048]{1,0:T(8,128)(2,1)S(1)}, u32[]{:S(2)}, u32[]{:S(2)}) collective-permute-start(bf16[192,2048]{1,0:T(8,128)(2,1)S(1)} %get-tuple-element.123), channel_id=1, source_target_pairs={{0,2},{1,3},{2,0},{3,1},{4,6},{5,7},{6,4},{7,5},{8,10},{9,11},{10,... | collective-permute-start | bytes 2359304 | tf_op jit(solution)/shard_map/ppermute | solution.py:722
  980.7 53.5 %collective-permute-start.45 = (bf16[192,2048]{1,0:T(8,128)(2,1)S(1)}, bf16[192,2048]{1,0:T(8,128)(2,1)S(1)}, u32[]{:S(2)}, u32[]{:S(2)}) collective-permute-start(bf16[192,2048]{1,0:T(8,128)(2,1)S(1)} %get-tuple-element.122), channel_id=1, source_target_pairs={{0,3},{1,2},{2,1},{3,0},{4,7},{5,6},{6,5},{7,4},{8,11},{9,10},{10,... | collective-permute-start | bytes 2359304 | tf_op jit(solution)/shard_map/ppermute | solution.py:722
  984.3 52.5 %collective-permute-start.15 = (bf16[256,1536]{1,0:T(8,128)(2,1)S(1)}, bf16[256,1536]{1,0:T(8,128)(2,1)S(1)}, u32[]{:S(2)}, u32[]{:S(2)}) collective-permute-start(bf16[256,1536]{1,0:T(8,128)(2,1)S(1)} %get-tuple-element.109), channel_id=1, source_target_pairs={{0,8},{4,12},{8,0},{12,4},{16,24},{20,28},{24,16},{28,20},{1,9},{5... | collective-permute-start | bytes 2359304 | tf_op jit(solution)/shard_map/ppermute | solution.py:710
  1036.9 30.1 %collective-permute-start.16 = (bf16[512,1536]{1,0:T(8,128)(2,1)S(1)}, bf16[512,1536]{1,0:T(8,128)(2,1)}, u32[]{:S(2)}, u32[]{:S(2)}) collective-permute-start(bf16[512,1536]{1,0:T(8,128)(2,1)S(1)} %pad_maximum_fusion.17), channel_id=1, source_target_pairs={{0,4},{4,0},{8,12},{12,8},{16,20},{20,16},{24,28},{28,24},{1,5},{5... | collective-permute-start | bytes 4718600 | tf_op jit(solution)/shard_map/ppermute | solution.py:710
  1070.9 41.5 %collective-permute-start.34 = (bf16[192,1536]{1,0:T(8,128)(2,1)}, bf16[192,1536]{1,0:T(8,128)(2,1)S(1)}, u32[]{:S(2)}, u32[]{:S(2)}) collective-permute-start(bf16[192,1536]{1,0:T(8,128)(2,1)} %convolution_convert_fusion.9), channel_id=1, source_target_pairs={{0,16},{4,20},{8,24},{12,28},{16,0},{20,4},{24,8},{28,12},{1,17},{... | collective-permute-start | bytes 1769480 | tf_op jit(solution)/shard_map/ppermute | solution.py:710
  1108.1 28.0 %collective-permute-start.20 = (bf16[768,768]{1,0:T(8,128)(2,1)}, bf16[768,768]{1,0:T(8,128)(2,1)}, u32[]{:S(2)}, u32[]{:S(2)}) collective-permute-start(bf16[768,768]{1,0:T(8,128)(2,1)} %fusion.73), channel_id=1, source_target_pairs={{0,16},{4,20},{8,24},{12,28},{16,0},{20,4},{24,8},{28,12},{1,17},{... | collective-permute-start | bytes 3538952 | tf_op jit(solution)/shard_map/ppermute | solution.py:710
  1115.1 39.7 %collective-permute-start.35 = (bf16[48,1536]{1,0:T(8,128)(2,1)S(1)}, bf16[48,1536]{1,0:T(8,128)(2,1)S(1)}, u32[]{:S(2)}, u32[]{:S(2)}) collective-permute-start(bf16[48,1536]{1,0:T(8,128)(2,1)S(1)} %get-tuple-element.153), channel_id=1, source_target_pairs={{0,1},{1,0},{2,3},{3,2},{4,5},{5,4},{6,7},{7,6},{8,9},{9,8},{10,11... | collective-permute-start | bytes 442376 | tf_op jit(solution)/shard_map/ppermute | solution.py:722
  1130.4 29.0 %collective-permute-start.36 = (bf16[48,1536]{1,0:T(8,128)(2,1)S(1)}, bf16[48,1536]{1,0:T(8,128)(2,1)S(1)}, u32[]{:S(2)}, u32[]{:S(2)}) collective-permute-start(bf16[48,1536]{1,0:T(8,128)(2,1)S(1)} %get-tuple-element.155), channel_id=1, source_target_pairs={{0,2},{1,3},{2,0},{3,1},{4,6},{5,7},{6,4},{7,5},{8,10},{9,11},{10,... | collective-permute-start | bytes 442376 | tf_op jit(solution)/shard_map/ppermute | solution.py:722
  1131.0 28.5 %collective-permute-start.37 = (bf16[48,1536]{1,0:T(8,128)(2,1)S(1)}, bf16[48,1536]{1,0:T(8,128)(2,1)S(1)}, u32[]{:S(2)}, u32[]{:S(2)}) collective-permute-start(bf16[48,1536]{1,0:T(8,128)(2,1)S(1)} %get-tuple-element.154), channel_id=1, source_target_pairs={{0,3},{1,2},{2,1},{3,0},{4,7},{5,6},{6,5},{7,4},{8,11},{9,10},{10,... | collective-permute-start | bytes 442376 | tf_op jit(solution)/shard_map/ppermute | solution.py:722
  1139.0 26.2 %collective-permute-start.21 = (bf16[192,768]{1,0:T(8,128)(2,1)S(1)}, bf16[192,768]{1,0:T(8,128)(2,1)S(1)}, u32[]{:S(2)}, u32[]{:S(2)}) collective-permute-start(bf16[192,768]{1,0:T(8,128)(2,1)S(1)} %get-tuple-element.141), channel_id=1, source_target_pairs={{0,1},{1,0},{2,3},{3,2},{4,5},{5,4},{6,7},{7,6},{8,9},{9,8},{10,11... | collective-permute-start | bytes 884744 | tf_op jit(solution)/shard_map/ppermute | solution.py:722
  1154.3 23.5 %collective-permute-start.22 = (bf16[192,768]{1,0:T(8,128)(2,1)S(1)}, bf16[192,768]{1,0:T(8,128)(2,1)S(1)}, u32[]{:S(2)}, u32[]{:S(2)}) collective-permute-start(bf16[192,768]{1,0:T(8,128)(2,1)S(1)} %get-tuple-element.143), channel_id=1, source_target_pairs={{0,2},{1,3},{2,0},{3,1},{4,6},{5,7},{6,4},{7,5},{8,10},{9,11},{10,... | collective-permute-start | bytes 884744 | tf_op jit(solution)/shard_map/ppermute | solution.py:722
  1154.8 23.0 %collective-permute-start.23 = (bf16[192,768]{1,0:T(8,128)(2,1)S(1)}, bf16[192,768]{1,0:T(8,128)(2,1)S(1)}, u32[]{:S(2)}, u32[]{:S(2)}) collective-permute-start(bf16[192,768]{1,0:T(8,128)(2,1)S(1)} %get-tuple-element.142), channel_id=1, source_target_pairs={{0,3},{1,2},{2,1},{3,0},{4,7},{5,6},{6,5},{7,4},{8,11},{9,10},{10,... | collective-permute-start | bytes 884744 | tf_op jit(solution)/shard_map/ppermute | solution.py:722
  1159.5 24.4 %collective-permute-start.17 = (bf16[512,1536]{1,0:T(8,128)(2,1)}, bf16[512,1536]{1,0:T(8,128)(2,1)}, u32[]{:S(2)}, u32[]{:S(2)}) collective-permute-start(bf16[512,1536]{1,0:T(8,128)(2,1)} %convolution_convert_fusion.4), channel_id=1, source_target_pairs={{0,4},{4,0},{8,12},{12,8},{16,20},{20,16},{24,28},{28,24},{1,5},{5... | collective-permute-start | bytes 4718600 | tf_op jit(solution)/shard_map/ppermute | solution.py:710
  1188.7 19.6 %collective-permute-start.18 = (bf16[256,1536]{1,0:T(8,128)(2,1)S(1)}, bf16[256,1536]{1,0:T(8,128)(2,1)S(1)}, u32[]{:S(2)}, u32[]{:S(2)}) collective-permute-start(bf16[256,1536]{1,0:T(8,128)(2,1)S(1)} %slice.426), channel_id=1, source_target_pairs={{0,8},{4,12},{8,0},{12,4},{16,24},{20,28},{24,16},{28,20},{1,9},{5... | collective-permute-start | bytes 2359304 | tf_op jit(solution)/shard_map/ppermute | solution.py:710
  1213.8 54.1 %collective-permute-start.19 = (bf16[256,1536]{1,0:T(8,128)(2,1)}, bf16[256,1536]{1,0:T(8,128)(2,1)S(1)}, u32[]{:S(2)}, u32[]{:S(2)}) collective-permute-start(bf16[256,1536]{1,0:T(8,128)(2,1)} %fusion.32), channel_id=1, source_target_pairs={{0,0},{1,8},{2,4},{3,12},{4,2},{5,10},{6,6},{7,14},{8,1},{9,9},{10... | collective-permute-start | bytes 2359304 | tf_op jit(solution)/shard_map/ppermute | solution.py:725
  (114 other events, 1958.4 us)

commit v3 on v0

--- a/solution.py
+++ b/solution.py
@@ -1,8 +1,11 @@
+import functools
 import math
 
 import jax
 import jax.numpy as jnp
 from jax import lax
+from jax.experimental import pallas as pl
+from jax.experimental.pallas import tpu as pltpu
 from jax.sharding import PartitionSpec as P
 
 HEAD_DIM = 96
@@ -332,7 +335,7 @@
     return (grad_middle + grad_hidden_part, attn_grads, ffn_grads)
 
 
-def per_device(
+def general_device(
     tokens,
     gain_attn,
     w_query,
@@ -401,6 +404,1206 @@
     )
 
 
+TP = 4
+
+
+def head_partner(values, halfway):
+    width = values.shape[1]
+    lane = lax.broadcasted_iota(jnp.int32, values.shape, 1)
+    ahead = pltpu.roll(values, width - halfway, 1)
+    behind = pltpu.roll(values, halfway, 1)
+    return jnp.where(lane % HEAD_DIM < halfway, ahead, behind)
+
+
+def block_mask(row_seg, col_seg, same_block, block):
+    visible = (row_seg == col_seg) | (col_seg == 0)
+    if same_block:
+        rows = lax.broadcasted_iota(jnp.int32, (block, block), 0)
+        cols = lax.broadcasted_iota(jnp.int32, (block, block), 1)
+        visible = visible & (cols <= rows)
+    return visible
+
+
+MESH = pl.DeviceIdType.MESH
+VMEM_LIMIT = 61 * 2**20
+ANYWHERE = pl.BlockSpec(memory_space=pl.ANY)
+IN_VMEM = pl.BlockSpec(memory_space=pltpu.VMEM)
+
+
+class Net:
+    def __init__(self, send_sems, recv_sems, local_sems):
+        dp, z = lax.axis_index("dp"), lax.axis_index("fsdp")
+        self.z = z
+        self.q = lax.rem(dp, TP)
+        self.y = lax.div(dp, TP)
+        self.r = self.y * TP + z
+        core = dp + 1 - 2 * lax.rem(dp, 2)
+        across = dp + 2 - 4 * lax.rem(lax.div(dp, 2), 2)
+        both = core + 2 - 4 * lax.rem(lax.div(dp, 2), 2)
+        other = dp + TP - 2 * TP * lax.div(dp, TP)
+        self.peer = {
+            "core": (core, z),
+            "x": (across, z),
+            "both": (both, z),
+            "y": (other, z),
+            "z1": (dp, flip_index(z, 1)),
+            "z2": (dp, flip_index(z, 2)),
+            "z3": (dp, flip_index(z, 3)),
+        }
+        x, c = lax.div(self.q, 2), lax.rem(self.q, 2)
+        high, low = lax.div(z, 2), lax.rem(z, 2)
+        twisted = x + low - 2 * x * low
+        self.peer["group"] = (self.y * TP + 2 * twisted + high, 2 * c + x)
+        self.peer["home"] = (self.y * TP + 2 * low + high, 2 * c + twisted)
+        self.alone = (self.peer["group"][0] == dp) & (self.peer["group"][1] == z)
+        self.base = 2 * c + twisted
+        self.send_sems, self.recv_sems, self.local_sems = send_sems, recv_sems, local_sems
+        self.n_remote = self.n_local = 0
+        self.flying = []
+        self.leaving = []
+        self.inner, self.outer = {}, {}
+
+    def greet(self, names, regroup=None):
+        barrier = pltpu.get_barrier_semaphore()
+        for name in names:
+            pl.semaphore_signal(barrier, inc=1, device_id=self.peer[name], device_id_type=MESH)
+        if regroup is None:
+            pl.semaphore_wait(barrier, len(names))
+            return
+        sender = self.peer["home" if regroup == "group" else "group"]
+
+        @pl.when(jnp.logical_not(self.alone))
+        def _():
+            pl.semaphore_signal(barrier, inc=1, device_id=sender, device_id_type=MESH)
+            pl.semaphore_wait(barrier, len(names) + 1)
+
+        @pl.when(self.alone)
+        def _():
+            pl.semaphore_wait(barrier, len(names))
+
+    def remote(self, src, dst, name):
+        n = self.n_remote
+        self.n_remote += 1
+        copy = pltpu.make_async_remote_copy(
+            src_ref=src,
+            dst_ref=dst,
+            send_sem=self.send_sems.at[n],
+            recv_sem=self.recv_sems.at[n],
+            device_id=self.peer[name],
+            device_id_type=MESH,
+        )
+        copy.start()
+        return copy
+
+    def regroup(self, src, dst, name):
+        n, k = self.n_remote, self.n_local
+        self.n_remote += 1
+        self.n_local += 1
+        away = pltpu.make_async_remote_copy(
+            src_ref=src,
+            dst_ref=dst,
+            send_sem=self.send_sems.at[n],
+            recv_sem=self.recv_sems.at[n],
+            device_id=self.peer[name],
+            device_id_type=MESH,
+        )
+        here = pltpu.make_async_copy(src, dst, self.local_sems.at[k])
+        copy = EitherCopy(self.alone, here, away)
+        copy.start()
+        return copy
+
+    def local(self, src, dst):
+        n = self.n_local
+        self.n_local += 1
+        copy = pltpu.make_async_copy(src, dst, self.local_sems.at[n])
+        copy.start()
+        return copy
+
+    def keep(self, src, dst):
+        self.leaving.append(self.local(src, dst))
+
+    def finish(self):
+        for copies in (*self.inner.values(), *self.outer.values(), self.flying, self.leaving):
+            for copy in copies:
+                copy.wait()
+        self.inner, self.outer = {}, {}
+        self.flying, self.leaving = [], []
+
+    def arrived(self, ref):
+        for pending in (self.inner, self.outer):
+            for key in [k for k in pending if k[0] == id(ref)]:
+                for copy in pending.pop(key):
+                    copy.wait()
+
+    def advance(self, moves):
+        for stage, ref, low, count in moves:
+            key = (id(ref), low)
+            for copy in self.inner.pop(key, []):
+                copy.wait()
+            part = lambda bits: ref.at[self.y, pl.ds(low, count), flip_index(self.z, bits)]
+            if stage == 1:
+                sent = ((0, "z2"), (0, "z1"), (0, "y"))
+            elif stage == 2:
+                sent = ((2, "z1"), (1, "y"), (2, "y"))
+            else:
+                sent = ((3, "y"),)
+            for bits, name in sent:
+                pending = self.outer if name == "y" else self.inner
+                pending.setdefault(key, []).append(self.remote(part(bits), part(bits), name))
+
+
+class EitherCopy:
+    def __init__(self, alone, here, away):
+        self.alone, self.here, self.away = alone, here, away
+
+    def start(self):
+        pl.when(self.alone)(self.here.start)
+        pl.when(jnp.logical_not(self.alone))(self.away.start)
+
+    def wait(self):
+        pl.when(self.alone)(self.here.wait)
+        pl.when(jnp.logical_not(self.alone))(self.away.wait)
+
+
+def flip_index(value, bits):
+    low = lax.rem(value, 2)
+    high = lax.div(value, 2)
+    if bits & 1:
+        low = 1 - low
+    if bits & 2:
+        high = 1 - high
+    return high * 2 + low
+
+
+def mixed_index(static, dynamic):
+    return flip_index(dynamic, static)
+
+
+def swap_index(value):
+    return lax.rem(value, 2) * 2 + lax.div(value, 2)
+
+
+def sems(remote, local):
+    return [
+        pltpu.SemaphoreType.DMA((max(remote, 1),)),
+        pltpu.SemaphoreType.DMA((max(remote, 1),)),
+        pltpu.SemaphoreType.DMA((max(local, 1),)),
+    ]
+
+
+PEERS = ("core", "x", "both", "y", "z1", "z2", "z3")
+RANK_PEERS = (("core", 1), ("x", 2), ("both", 3))
+
+
+def segments(lengths_ref, conts, group_tok, places):
+    one = [lengths_ref[0:1, c : c + 1] for c in range(conts)]
+    prompt = group_tok - sum(one)
+    begin = prompt
+    segment = jnp.zeros(places.shape, jnp.int32)
+    begins = jnp.zeros(places.shape, jnp.int32)
+    for c in range(conts):
+        inside = places >= begin
+        segment = segment + inside.astype(jnp.int32)
+        begins = jnp.where(inside, jnp.maximum(begins, begin), begins)
+        begin = begin + one[c]
+    position = jnp.where(segment > 0, places - begins + prompt, places)
+    return segment, position
+
+
+def block_segments(lengths_ref, conts, block, index, row):
+    shape = (block, 1) if row else (1, block)
+    places = index * block + lax.broadcasted_iota(jnp.int32, shape, 0 if row else 1)
+    return segments(lengths_ref, conts, TP * block, places)[0]
+
+
+def start_kernel(
+    conts, qkv_pack, w_gate, w_up, out_own, down_own, gain_tile, tokens, lengths, frequency, spread_cos, spread_sin,
+    tok_out, cos_ref, sin_ref, len_out,
+    g_qkv0, g_qkv1, g_gu0, g_gu1, g_out0, g_out1, g_down0, g_down1, g_gain,
+    tok_buf, len_buf, send_sems, recv_sems, local_sems,
+):
+    net = Net(send_sems, recv_sems, local_sems)
+    net.greet(PEERS, "group")
+    bring = [net.regroup(lengths, len_buf, "group"), net.regroup(tokens, tok_buf, "group")]
+    y, q, z = net.y, net.q, net.z
+    step = w_gate.shape[2] // (2 * TP)
+
+    def qkv_columns(layer, target):
+        copies = [
+            net.remote(qkv_pack.at[layer, flip_index(q, bits)], target.at[y, q, z], name)
+            for name, bits in RANK_PEERS
+        ]
+        return copies + [net.local(qkv_pack.at[layer, q], target.at[y, q, z])]
+
+    def gu_columns(layer, target):
+        copies = []
+        for name, bits in RANK_PEERS + ((None, 0),):
+            for n, weight in enumerate((w_gate, w_up)):
+                for half in range(2):
+                    at = pl.multiple_of((half * TP + flip_index(q, bits)) * step, step)
+                    src = weight.at[layer, :, pl.ds(at, step)]
+                    dst = target.at[y, q, z, :, pl.ds((2 * n + half) * step, step)]
+                    copies.append(net.local(src, dst) if name is None else net.remote(src, dst, name))
+        return copies
+
+    first = qkv_columns(0, g_qkv0)
+    first += [net.remote(gain_tile, g_gain.at[y, q, z], name) for name, _ in RANK_PEERS]
+    first.append(net.local(gain_tile, g_gain.at[y, q, z]))
+    placed = [
+        net.local(out_own.at[0], g_out0.at[y, 0, z]),
+        net.local(down_own.at[0], g_down0.at[y, 0, z]),
+        net.local(out_own.at[1], g_out1.at[y, 0, z]),
+        net.local(down_own.at[1], g_down1.at[y, 0, z]),
+    ]
+    second = gu_columns(0, g_gu0)
+    placed[0].wait()
+    net.advance(((1, g_out0, 0, 1),))
+    for copy in first:
+        copy.wait()
+    net.advance(((1, g_qkv0, 0, TP), (1, g_gain, 0, TP)))
+    placed[1].wait()
+    net.advance(((1, g_down0, 0, 1),))
+    second += qkv_columns(1, g_qkv1) + gu_columns(1, g_gu1)
+    bring[0].wait()
+    block = tok_buf.shape[0]
+    len_out[...] = len_buf[...]
+    def table(s):
+        places = mixed_index(s, net.base) * block + lax.broadcasted_iota(jnp.int32, (block, 1), 0)
+        position = segments(len_buf, conts, TP * block, places)[1]
+        angles = position.astype(jnp.float32) * frequency[...]
+        at = slice(s * block, (s + 1) * block)
+        for table_ref, values, lanes in (
+            (cos_ref, jnp.cos(angles), spread_cos), (sin_ref, jnp.sin(angles), spread_sin)
+        ):
+            table_ref[at, :] = jnp.dot(
+                values, lanes[...], precision=lax.Precision.HIGHEST, preferred_element_type=jnp.float32
+            )
+
+    table(0)
+    net.advance(((2, g_out0, 0, 1), (2, g_qkv0, 0, TP), (2, g_gain, 0, TP)))
+    table(1)
+    net.advance(((3, g_out0, 0, 1), (3, g_qkv0, 0, TP), (3, g_gain, 0, TP), (2, g_down0, 0, 1)))
+    table(2)
+    table(3)
+    bring[1].wait()
+    tok_out[...] = tok_buf[...].astype(jnp.float32)
+    for copy in placed[2:]:
+        copy.wait()
+    for copy in second:
+        copy.wait()
+    net.finish()
+
+
+def start_exchange(conts, qkv_pack, w_gate, w_up, out_own, down_own, gain_tile, tokens, lengths, frequency, spread_cos, spread_sin):
+    bf, f32 = jnp.bfloat16, jnp.float32
+    shape = jax.ShapeDtypeStruct
+    block, depth = tokens.shape
+    shard, qkv_width = qkv_pack.shape[2:]
+    units = w_gate.shape[2] // TP * 2
+    outs = [
+        shape((block, depth), f32),
+        shape((TP * block, spread_cos.shape[1]), f32),
+        shape((TP * block, spread_cos.shape[1]), f32),
+        shape(lengths.shape, lengths.dtype),
+    ]
+    for ranks, rows, width in (
+        (TP, shard, qkv_width),
+        (TP, shard, units),
+        (1, shard, depth),
+        (1, down_own.shape[1], depth),
+    ):
+        outs += [shape((2, ranks, TP, rows, width), bf)] * 2
+    outs.append(shape((2, TP, TP) + gain_tile.shape, f32))
+    return pl.pallas_call(
+        functools.partial(start_kernel, conts),
+        out_shape=outs,
+        in_specs=[IN_VMEM] * 11,
+        out_specs=[IN_VMEM] * 4 + [ANYWHERE] * 9,
+        scratch_shapes=[
+            pltpu.VMEM((block, depth), bf),
+            pltpu.VMEM(lengths.shape, lengths.dtype),
+        ] + sems(80, 24),
+        compiler_params=pltpu.CompilerParams(
+            collective_id=1, has_side_effects=True, vmem_limit_bytes=VMEM_LIMIT
+        ),
+        cost_estimate=pl.CostEstimate(flops=0, bytes_accessed=300 * 2**20, transcendentals=0),
+    )(qkv_pack, w_gate, w_up, out_own, down_own, gain_tile, tokens, lengths, frequency, spread_cos, spread_sin)
+
+
+def attend_rows(net, block):
+    return [
+        pl.ds(pl.multiple_of(mixed_index(b, net.base) * block, block), block) for b in range(TP)
+    ]
+
+
+def attend_forward_block(net, qkv_ref, len_ref, conts, mixed_ref, lse_ref):
+    total, width = qkv_ref.shape
+    block = total // TP
+    q_heads = width // (2 * HEAD_DIM)
+    kv_heads = q_heads // 2
+    factor = 1.0 / math.sqrt(HEAD_DIM)
+    key_at = q_heads * HEAD_DIM
+    value_at = key_at + kv_heads * HEAD_DIM
+    places = attend_rows(net, block)
+    nt = (((1,), (1,)), ((), ()))
+    for i in range(TP):
+        row_seg = block_segments(len_ref, conts, block, i, True)
+        masks = [
+            block_mask(row_seg, block_segments(len_ref, conts, block, j, False), i == j, block)
+            for j in range(i + 1)
+        ]
+        for h in range(q_heads):
+            kv = h // 2
+            query = qkv_ref[places[i], h * HEAD_DIM : (h + 1) * HEAD_DIM]
+            scores = []
+            for j in range(i + 1):
+                key = qkv_ref[places[j], key_at + kv * HEAD_DIM : key_at + (kv + 1) * HEAD_DIM]
+                s = lax.dot_general(query, key, nt, preferred_element_type=jnp.float32) * factor
+                scores.append(jnp.where(masks[j], s, NEGATIVE))
+            peak = scores[0].max(axis=1, keepdims=True)
+            for s in scores[1:]:
+                peak = jnp.maximum(peak, s.max(axis=1, keepdims=True))
+            total_e = jnp.zeros((block, 1), jnp.float32)
+            mixed = jnp.zeros((block, HEAD_DIM), jnp.float32)
+            for j in range(i + 1):
+                e = jnp.exp(scores[j] - peak)
+                total_e = total_e + e.sum(axis=1, keepdims=True)
+                value = qkv_ref[places[j], value_at + kv * HEAD_DIM : value_at + (kv + 1) * HEAD_DIM]
+                mixed = mixed + jnp.dot(
+                    e.astype(jnp.bfloat16), value, preferred_element_type=jnp.float32
+                )
+            mixed_ref[places[i], h * HEAD_DIM : (h + 1) * HEAD_DIM] = (mixed / total_e).astype(
+                jnp.bfloat16
+            )
+            lse_ref[i, :, h : h + 1] = peak + jnp.log(total_e)
+
+
+def normalize(values, gain_row):
+    scale = lax.rsqrt(jnp.mean(values * values, axis=-1, keepdims=True) + EPSILON)
+    return (values * scale * gain_row).astype(jnp.bfloat16)
+
+
+def spread_begin(net, buf):
+    return (net.remote(buf.at[0], buf.at[1], "x"), net.remote(buf.at[0], buf.at[2], "core"))
+
+
+def spread_each(net, buf, begun, work):
+    over_x, over_core = begun
+    work(0)
+    over_core.wait()
+    work(2)
+    over_x.wait()
+    forward = net.remote(buf.at[1], buf.at[3], "core")
+    work(1)
+    forward.wait()
+    work(3)
+
+
+def collect(net, part, far_out, far_in, pass_out, pass_in):
+    low = lambda v: v.astype(jnp.bfloat16)
+    far_out[0] = low(part(3))
+    first = net.remote(far_out.at[0], far_in.at[0], "core")
+    near = part(1)
+    first.wait()
+    pass_out[...] = low(near + far_in[0].astype(jnp.float32))
+    passed = net.remote(pass_out, pass_in, "x")
+    far_out[1] = low(part(2))
+    second = net.remote(far_out.at[1], far_in.at[1], "core")
+    own = part(0)
+    second.wait()
+    own = own + far_in[1].astype(jnp.float32)
+    passed.wait()
+    return own + pass_in[...].astype(jnp.float32)
+
+
+def forward_kernel(programs, has_cot, conts, n_moving, *refs):
+    x_own, gain_a, gain_f, cos_ref, sin_ref, lengths = refs[:6]
+    refs = refs[6:]
+    if has_cot:
+        cot, refs = refs[0], refs[1:]
+    refs = refs[n_moving:]
+    moving, refs = refs[:n_moving], refs[n_moving:]
+    (x_next, middle_ref, lse_ref, x_low, rows_out, qkv_out, mixed_out, ffn_rows_out, gate_out, up_out, act_out) = refs[:11]
+    refs = refs[11:]
+    if has_cot:
+        branch_out, refs, branch = refs[0], refs[1:-1], refs[-1]
+    (rows, ffn_rows, w_qkv, w_o, w_gu, w_d, qkv, mixed, gate, up, act,
+     far_out, far_in, pass_out, pass_in, send_sems, recv_sems, local_sems) = refs
+    net = Net(send_sems, recv_sems, local_sems)
+    steps = [[(kind, moving[n], low, count) for kind, n, low, count in step] for step in programs]
+    block, depth = x_own.shape
+    load_qkv = net.local(moving[0], w_qkv)
+    load_o = net.local(moving[1], w_o)
+    net.greet(("core", "x", "y", "z1", "z2", "z3"), "group" if has_cot else None)
+    net.advance(steps[0])
+    if has_cot:
+        bring = net.regroup(cot, branch.at[0], "group")
+    rows[0] = normalize(x_own[...], gain_a[...])
+    begun = spread_begin(net, rows)
+    load_qkv.wait()
+
+    def project(s):
+        raw = jnp.dot(
+            rows[s], w_qkv[...].reshape(depth, -1), preferred_element_type=jnp.float32
+        )
+        at = slice(s * block, (s + 1) * block)
+        turned = raw * cos_ref[at, :] + head_partner(raw, HEAD_DIM // 2) * sin_ref[at, :]
+        qkv[at, :] = turned.astype(jnp.bfloat16)
+
+    spread_each(net, rows, begun, project)
+    net.keep(rows, rows_out)
+    net.keep(qkv, qkv_out)
+    net.advance(steps[1])
+    attend_forward_block(net, qkv, lengths, conts, mixed, lse_ref)
+    net.keep(mixed, mixed_out)
+    net.advance(steps[2])
+    load_o.wait()
+
+    def out_part(s):
+        return jnp.dot(
+            mixed[s * block : (s + 1) * block, :],
+            w_o[...].reshape(-1, depth),
+            preferred_element_type=jnp.float32,
+        )
+
+    middle = x_own[...] + collect(
+        net, out_part, far_out, far_in.at[0], pass_out, pass_in.at[0]
+    )
+    middle_ref[...] = middle
+    net.advance(steps[3])
+    net.arrived(moving[3])
+    load_d = net.local(moving[3], w_d)
+    ffn_rows[0] = normalize(middle, gain_f[...])
+    begun = spread_begin(net, ffn_rows)
+    if has_cot:
+        bring.wait()
+        over_x, over_core = spread_begin(net, branch)
+    net.arrived(moving[2])
+    load_gu = net.local(moving[2], w_gu)
+    net.advance(steps[4])
+    load_d.wait()
+    load_gu.wait()
+    units = act.shape[2]
+
+    def expand(s):
+        value = ffn_rows[s]
+        gating = jnp.dot(
+            value, w_gu[:, :, :, :, :units].reshape(depth, units), preferred_element_type=jnp.float32
+        )
+        upward = jnp.dot(
+            value, w_gu[:, :, :, :, units:].reshape(depth, units), preferred_element_type=jnp.float32
+        )
+        gate[s] = gating.astype(jnp.bfloat16)
+        up[s] = upward.astype(jnp.bfloat16)
+        act[s] = (gating * jax.nn.sigmoid(gating) * upward).astype(jnp.bfloat16)
+
+    spread_each(net, ffn_rows, begun, expand)
+    if has_cot:
+        over_x.wait()
+        forward = net.remote(branch.at[1], branch.at[3], "core")
+    net.keep(ffn_rows, ffn_rows_out)
+    net.keep(gate, gate_out)
+    net.keep(up, up_out)
+    net.keep(act, act_out)
+
+    def down_part(s):
+        return jnp.dot(act[s], w_d[...].reshape(-1, depth), preferred_element_type=jnp.float32)
+
+    result = middle_ref[...] + collect_during(
+        net,
+        down_part,
+        (far_out, far_in.at[1], pass_out, pass_in.at[1]),
+        lambda: net.advance(steps[5]),
+    )
+    if has_cot:
+        over_core.wait()
+        forward.wait()
+        net.keep(branch, branch_out)
+    x_next[...] = result
+    x_low[...] = result.astype(jnp.bfloat16)
+    net.finish()
+
+
+def forward_layer(programs, cot, cid, conts, x_own, gain_a, gain_f, cosine, sine, lengths, moving):
+    bf, f32 = jnp.bfloat16, jnp.float32
+    block, depth = x_own.shape
+    total, qkv_width = cosine.shape
+    units = moving[2].shape[4] // 2
+    q_heads = qkv_width // (2 * HEAD_DIM)
+    shape = jax.ShapeDtypeStruct
+    outs = [shape(m.shape, m.dtype) for m in moving] + [
+        shape((block, depth), f32),
+        shape((block, depth), f32),
+        shape((TP, block, q_heads), f32),
+        shape((block, depth), bf),
+        shape((TP, block, depth), bf),
+        shape((total, qkv_width), bf),
+        shape((total, qkv_width // 2), bf),
+        shape((TP, block, depth), bf),
+        shape((TP, block, units), bf),
+        shape((TP, block, units), bf),
+        shape((TP, block, units), bf),
+    ]
+    n = len(moving)
+    given = [] if cot is None else [cot]
+    c = len(given)
+    outs += [shape((TP, block, depth), bf)] * c
+    scratch = [
+        pltpu.VMEM((TP, block, depth), bf),
+        pltpu.VMEM((TP, block, depth), bf),
+        pltpu.VMEM(moving[0].shape, bf),
+        pltpu.VMEM(moving[1].shape, bf),
+        pltpu.VMEM(moving[2].shape, bf),
+        pltpu.VMEM(moving[3].shape, bf),
+        pltpu.VMEM((total, qkv_width), bf),
+        pltpu.VMEM((total, qkv_width // 2), bf),
+        pltpu.VMEM((TP, block, units), bf),
+        pltpu.VMEM((TP, block, units), bf),
+        pltpu.VMEM((TP, block, units), bf),
+        pltpu.VMEM((2, block, depth), bf),
+        pltpu.VMEM((2, 2, block, depth), bf),
+        pltpu.VMEM((block, depth), bf),
+        pltpu.VMEM((2, block, depth), bf),
+    ] + sems(80, 24) + [pltpu.VMEM((TP, block, depth), bf)] * c
+    return pl.pallas_call(
+        functools.partial(forward_kernel, programs, bool(c), conts, n),
+        out_shape=outs,
+        in_specs=[IN_VMEM] * (6 + c) + [ANYWHERE] * n,
+        out_specs=[ANYWHERE] * n + [IN_VMEM] * 4 + [ANYWHERE] * (7 + c),
+        scratch_shapes=scratch,
+        input_output_aliases={6 + c + i: i for i in range(n)},
+        compiler_params=pltpu.CompilerParams(
+            collective_id=cid, has_side_effects=True, vmem_limit_bytes=VMEM_LIMIT
+        ),
+        cost_estimate=pl.CostEstimate(
+            flops=16 * 10**9, bytes_accessed=400 * 2**20, transcendentals=10**7
+        ),
+    )(x_own, gain_a, gain_f, cosine, sine, lengths, *given, *moving)
+
+
+def moved_shape(kind, source):
+    shape = source.shape
+    if kind in ("y", "whole_y"):
+        kept = shape
+    elif kind == "g":
+        kept = shape
+    elif kind == "zc":
+        kept = (3, shape[0]) + shape[2:]
+    elif kind in ("z", "t"):
+        kept = (3,) + shape[1:]
+    else:
+        kept = (3,) + shape
+    return jax.ShapeDtypeStruct(kept, source.dtype)
+
+
+def begin_move(net, kind, source, target):
+    if kind in ("y", "whole_y"):
+        return [net.remote(source, target, "y")]
+    if kind == "g":
+        return [net.regroup(source, target, "home")]
+    copies = []
+    for name, bits in RANK_PEERS:
+        if kind == "z":
+            copies.append(
+                net.remote(source.at[flip_index(net.z, bits)], target.at[bits - 1], f"z{bits}")
+            )
+        elif kind == "zc":
+            copies.append(
+                net.remote(source.at[:, flip_index(net.z, bits)], target.at[bits - 1], f"z{bits}")
+            )
+        elif kind == "whole_z":
+            copies.append(net.remote(source, target.at[bits - 1], f"z{bits}"))
+        elif kind == "t":
+            copies.append(
+                net.remote(source.at[flip_index(net.q, bits)], target.at[bits - 1], name)
+            )
+        else:
+            copies.append(net.remote(source, target.at[bits - 1], name))
+    return copies
+
+
+def begin_moves(net, kinds, sources, targets):
+    for kind, source, target in zip(kinds, sources, targets):
+        net.flying += begin_move(net, kind, source, target)
+
+
+def greet_all(net, kinds):
+    net.greet(PEERS, "home" if "g" in kinds else None)
+
+
+def move_kernel(kinds, *refs):
+    n = len(kinds)
+    net = Net(*refs[2 * n :])
+    greet_all(net, kinds)
+    begin_moves(net, kinds, refs[:n], refs[n : 2 * n])
+    net.finish()
+
+
+def run_moves(cid, moves):
+    kinds = tuple(kind for kind, _ in moves)
+    sources = [source for _, source in moves]
+    return pl.pallas_call(
+        functools.partial(move_kernel, kinds),
+        out_shape=[moved_shape(kind, source) for kind, source in moves],
+        in_specs=[ANYWHERE] * len(moves),
+        out_specs=[ANYWHERE] * len(moves),
+        scratch_shapes=sems(32, 4),
+        compiler_params=pltpu.CompilerParams(
+            collective_id=cid, has_side_effects=True, vmem_limit_bytes=VMEM_LIMIT
+        ),
+        cost_estimate=pl.CostEstimate(flops=0, bytes_accessed=200 * 2**20, transcendentals=0),
+    )(*sources)
+
+
+def norm_backward(values, gain_row, incoming):
+    inv = lax.rsqrt(jnp.mean(values * values, axis=-1, keepdims=True) + EPSILON)
+    weighted = incoming * gain_row
+    inner = jnp.mean(weighted * values, axis=-1, keepdims=True)
+    grad = inv * weighted - values * (inv * inv * inv * inner)
+    return grad, jnp.sum(incoming * values * inv, axis=0, keepdims=True)
+
+
+def collect_during(net, part, bufs, meanwhile):
+    far_out, far_in, pass_out, pass_in = bufs
+    low = lambda v: v.astype(jnp.bfloat16)
+    far_out[0] = low(part(3))
+    first = net.remote(far_out.at[0], far_in.at[0], "core")
+    near = part(1)
+    first.wait()
+    pass_out[...] = low(near + far_in[0].astype(jnp.float32))
+    passed = net.remote(pass_out, pass_in, "x")
+    far_out[1] = low(part(2))
+    second = net.remote(far_out.at[1], far_in.at[1], "core")
+    own = part(0)
+    second.wait()
+    own = own + far_in[1].astype(jnp.float32)
+    meanwhile()
+    passed.wait()
+    return own + pass_in[...].astype(jnp.float32)
+
+
+NT = (((1,), (1,)), ((), ()))
+TN = (((0,), (0,)), ((), ()))
+
+
+def dot_nt(left, right):
+    return lax.dot_general(left, right, NT, preferred_element_type=jnp.float32)
+
+
+def dot_tn(left, right):
+    return lax.dot_general(left, right, TN, preferred_element_type=jnp.float32)
+
+
+def ffn_backward_kernel(kinds, given, *refs):
+    n = len(kinds)
+    middle, gain, source_in = refs[:3]
+    acts, rows_in, gates, ups, mixed_in, wd_in, wgu_in, wo_in = refs[3:11]
+    refs = refs[11:]
+    sources, targets, refs = refs[:n], refs[n : 2 * n], refs[2 * n :]
+    (grad_middle, gain_grad, dmixed_out, d_own, d_got, gu_own, gu_other, o_own, o_other) = refs[:9]
+    (branch, proj, act, rows, gate, up, mixed, dmixed, w_d, w_gu, w_o, g_down, g_gu, g_out,
+     far_out, far_in, pass_out, pass_in, send_sems, recv_sems, local_sems) = refs[9:]
+    net = Net(send_sems, recv_sems, local_sems)
+    block, depth = middle.shape
+    units = act.shape[2]
+    total = TP * block
+    loads = {}
+    if given:
+        loads["branch"] = net.local(source_in, branch)
+    for name, src, dst in (
+        ("w_d", wd_in, w_d), ("gate", gates, gate), ("up", ups, up), ("act", acts, act),
+        ("w_gu", wgu_in, w_gu), ("rows", rows_in, rows), ("w_o", wo_in, w_o), ("mixed", mixed_in, mixed),
+    ):
+        loads[name] = net.local(src, dst)
+    greet_all(net, kinds)
+    begin_moves(net, kinds, sources, targets)
+    if given:
+        loads["branch"].wait()
+    else:
+        branch[0] = source_in[...].astype(jnp.bfloat16)
+        begun = spread_begin(net, branch)
+    loads["w_d"].wait()
+    loads["gate"].wait()
+    loads["up"].wait()
+
+    def through(s):
+        grad_act = dot_nt(branch[s], w_d[...].reshape(units, depth))
+        gating = gate[s].astype(jnp.float32)
+        upward = up[s].astype(jnp.float32)
+        sig = jax.nn.sigmoid(gating)
+        shared = grad_act * sig
+        gate[s] = (shared * upward * (1.0 + gating * (1.0 - sig))).astype(jnp.bfloat16)
+        up[s] = (shared * gating).astype(jnp.bfloat16)
+
+    if given:
+        for s in (3, 1, 2, 0):
+            through(s)
+    else:
+        spread_each(net, branch, begun, through)
+    loads["act"].wait()
+    theirs, ours = 1 - net.y, net.y
+    drows, urows = g_down.shape[2], g_gu.shape[3]
+    dwide, uwide = 2 * drows, 2 * TP * urows
+
+    def down_half(side):
+        def tile(m, carry):
+            lanes = pl.ds(pl.multiple_of((side * 2 + m) * dwide, dwide), dwide)
+            grad = dot_tn(act[:, :, lanes].reshape(total, dwide), branch[...].reshape(total, depth))
+            g_down[side, pl.ds(2 * m, 2)] = grad.astype(jnp.bfloat16).reshape(2, drows, depth)
+            return carry
+
+        lax.fori_loop(0, 2, tile, 0)
+
+    def gu_half(side):
+        def tile(m, carry):
+            lanes = pl.ds(pl.multiple_of((side * 2 + m) * uwide, uwide), uwide)
+            left = rows[:, :, lanes].reshape(total, uwide)
+            for ref, at in ((gate, 0), (up, units)):
+                grad = dot_tn(left, ref[...].reshape(total, units)).astype(jnp.bfloat16)
+                g_gu[side, pl.ds(2 * m, 2), :, :, at : at + units] = grad.reshape(2, TP, urows, units)
+            return carry
+
+        lax.fori_loop(0, 2, tile, 0)
+
+    down_half(theirs)
+    net.flying.append(net.remote(g_down.at[theirs], d_got, "y"))
+    loads["w_gu"].wait()
+    loads["rows"].wait()
+
+    def back(s):
+        return dot_nt(gate[s], w_gu[:, :, :, :, :units].reshape(depth, units)) + dot_nt(
+            up[s], w_gu[:, :, :, :, units:].reshape(depth, units)
+        )
+
+    def meanwhile():
+        gu_half(theirs)
+        net.keep(g_gu.at[theirs], gu_other)
+        gu_half(ours)
+        net.keep(g_gu.at[ours], gu_own)
+        down_half(ours)
+        net.keep(g_down.at[ours], d_own)
+
+    incoming = collect_during(net, back, (far_out, far_in, pass_out, pass_in), meanwhile)
+    part, gain_part = norm_backward(middle[...], gain[...], incoming)
+    gain_grad[...] = gain_part
+    grad_mid = (branch[0].astype(jnp.float32) if given else source_in[...]) + part
+    grad_middle[...] = grad_mid
+    proj[0] = grad_mid.astype(jnp.bfloat16)
+    begun = spread_begin(net, proj)
+    loads["w_o"].wait()
+    loads["mixed"].wait()
+
+    def mix_back(s):
+        dmixed[s * block : (s + 1) * block, :] = dot_nt(
+            proj[s], w_o[...].reshape(-1, depth)
+        ).astype(jnp.bfloat16)
+
+    spread_each(net, proj, begun, mix_back)
+    net.keep(dmixed, dmixed_out)
+    grad = dot_tn(mixed[...], proj[...].reshape(total, depth)).astype(jnp.bfloat16)
+    g_out[...] = grad.reshape(g_out.shape)
+    net.keep(g_out.at[ours], o_own)
+    net.keep(g_out.at[theirs], o_other)
+    net.finish()
+
+
+def ffn_backward(cid, moves, source, given, middle, gain, acts, rows, gates, ups, mixed, w_d, w_gu, w_o):
+    bf, f32 = jnp.bfloat16, jnp.float32
+    shape = jax.ShapeDtypeStruct
+    block, depth = middle.shape
+    units = gates.shape[2]
+    total, mixed_width = mixed.shape
+    kinds = tuple(kind for kind, _ in moves)
+    sources = [source for _, source in moves]
+    n = len(moves)
+    drows, urows, orows = w_d.shape[3], w_gu.shape[3], w_o.shape[3]
+    outs = [moved_shape(kind, source) for kind, source in moves] + [
+        shape((block, depth), f32),
+        shape((1, depth), f32),
+        shape((total, mixed_width), bf),
+        shape((TP, drows, depth), bf),
+        shape((TP, drows, depth), bf),
+        shape((TP, TP, urows, 2 * units), bf),
+        shape((TP, TP, urows, 2 * units), bf),
+        shape((TP, orows, depth), bf),
+        shape((TP, orows, depth), bf),
+    ]
+    scratch = [
+        pltpu.VMEM((TP, block, depth), bf),
+        pltpu.VMEM((TP, block, depth), bf),
+        pltpu.VMEM((TP, block, units), bf),
+        pltpu.VMEM((TP, block, depth), bf),
+        pltpu.VMEM((TP, block, units), bf),
+        pltpu.VMEM((TP, block, units), bf),
+        pltpu.VMEM((total, mixed_width), bf),
+        pltpu.VMEM((total, mixed_width), bf),
+        pltpu.VMEM(w_d.shape, bf),
+        pltpu.VMEM(w_gu.shape, bf),
+        pltpu.VMEM(w_o.shape, bf),
+        pltpu.VMEM((2, TP, drows, depth), bf),
+        pltpu.VMEM((2, TP, TP, urows, 2 * units), bf),
+        pltpu.VMEM((2, TP, orows, depth), bf),
+        pltpu.VMEM((2, block, depth), bf),
+        pltpu.VMEM((2, block, depth), bf),
+        pltpu.VMEM((block, depth), bf),
+        pltpu.VMEM((block, depth), bf),
+    ] + sems(48, 20)
+    operands = [middle, gain, source, acts, rows, gates, ups, mixed, w_d, w_gu, w_o]
+    return pl.pallas_call(
+        functools.partial(ffn_backward_kernel, kinds, given),
+        out_shape=outs,
+        in_specs=[IN_VMEM] * 2 + [ANYWHERE if given else IN_VMEM] + [ANYWHERE] * (8 + n),
+        out_specs=[ANYWHERE] * n + [IN_VMEM] * 2 + [ANYWHERE] * 7,
+        scratch_shapes=scratch,
+        compiler_params=pltpu.CompilerParams(
+            collective_id=cid, has_side_effects=True, vmem_limit_bytes=VMEM_LIMIT
+        ),
+        cost_estimate=pl.CostEstimate(
+            flops=24 * 10**9, bytes_accessed=200 * 2**20, transcendentals=10**6
+        ),
+    )(*operands, *sources)
+
+
+def attend_backward_block(net, qkv_ref, grad_ref, mixed_ref, lse_ref, len_ref, conts, acc_ref):
+    total, width = qkv_ref.shape
+    block = total // TP
+    q_heads = width // (2 * HEAD_DIM)
+    kv_heads = q_heads // 2
+    factor = 1.0 / math.sqrt(HEAD_DIM)
+    key_at = q_heads * HEAD_DIM
+    value_at = key_at + kv_heads * HEAD_DIM
+    places = attend_rows(net, block)
+    acc_ref[:, key_at:] = jnp.zeros((total, width - key_at), jnp.float32)
+    for i in range(TP):
+        row_seg = block_segments(len_ref, conts, block, i, True)
+        masks = [
+            block_mask(row_seg, block_segments(len_ref, conts, block, j, False), i == j, block)
+            for j in range(i + 1)
+        ]
+        for h in range(q_heads):
+            kv = h // 2
+            lanes = slice(h * HEAD_DIM, (h + 1) * HEAD_DIM)
+            query = qkv_ref[places[i], lanes]
+            grad = grad_ref[places[i], lanes]
+            lse = lse_ref[i, :, h : h + 1]
+            inner = jnp.sum(
+                grad.astype(jnp.float32) * mixed_ref[places[i], lanes].astype(jnp.float32),
+                axis=1,
+                keepdims=True,
+            )
+            grad_query = jnp.zeros((block, HEAD_DIM), jnp.float32)
+            key_lanes = slice(key_at + kv * HEAD_DIM, key_at + (kv + 1) * HEAD_DIM)
+            value_lanes = slice(value_at + kv * HEAD_DIM, value_at + (kv + 1) * HEAD_DIM)
+            for j in range(i + 1):
+                key = qkv_ref[places[j], key_lanes]
+                value = qkv_ref[places[j], value_lanes]
+                s = dot_nt(query, key) * factor
+                prob = jnp.where(masks[j], jnp.exp(s - lse), 0.0)
+                grad_prob = dot_nt(grad, value)
+                grad_score = (prob * (grad_prob - inner)).astype(jnp.bfloat16)
+                grad_query = grad_query + jnp.dot(
+                    grad_score, key, preferred_element_type=jnp.float32
+                )
+                acc_ref[places[j], key_lanes] += dot_tn(grad_score, query) * factor
+                acc_ref[places[j], value_lanes] += dot_tn(prob.astype(jnp.bfloat16), grad)
+            acc_ref[places[i], lanes] = grad_query * factor
+
+
+def attn_backward_kernel(kinds, conts, *refs):
+    n = len(kinds)
+    (grad_middle, hidden, gain, qkv, dmixed, mixed, lse, lengths, cos_ref, sin_ref) = refs[:10]
+    rows_in, w_in = refs[10:12]
+    sources, targets, refs = refs[12 : 12 + n], refs[12 + n : 12 + 2 * n], refs[12 + 2 * n :]
+    upstream, up_low, gain_grad, qkv_own, qkv_other = refs[:5]
+    (acc, dqkv, rows, w_qkv, g_qkv, far_out, far_in, pass_out, pass_in,
+     send_sems, recv_sems, local_sems) = refs[5:]
+    net = Net(send_sems, recv_sems, local_sems)
+    block, depth = hidden.shape
+    total = TP * block
+    load_rows = net.local(rows_in, rows)
+    load_w = net.local(w_in, w_qkv)
+    greet_all(net, kinds)
+    begin_moves(net, kinds, sources, targets)
+    attend_backward_block(net, qkv, dmixed, mixed, lse, lengths, conts, acc)
+    for s in range(TP):
+        at = slice(s * block, (s + 1) * block)
+        value = acc[at, :]
+        turned = value * cos_ref[at, :] - head_partner(value, HEAD_DIM // 2) * sin_ref[at, :]
+        dqkv[at, :] = turned.astype(jnp.bfloat16)
+    load_w.wait()
+    load_rows.wait()
+    urows = g_qkv.shape[2]
+    wide = 2 * TP * urows
+
+    def back(s):
+        return dot_nt(dqkv[s * block : (s + 1) * block, :], w_qkv[...].reshape(depth, -1))
+
+    def meanwhile():
+        def tile(m, carry):
+            lanes = pl.ds(pl.multiple_of(m * wide, wide), wide)
+            grad = dot_tn(rows[:, :, lanes].reshape(total, wide), dqkv[...])
+            g_qkv[pl.ds(2 * m, 2)] = grad.astype(jnp.bfloat16).reshape(2, TP, urows, -1)
+            return carry
+
+        lax.fori_loop(0, TP, tile, 0)
+        net.keep(g_qkv.at[pl.ds(net.y * TP, TP)], qkv_own)
+        net.keep(g_qkv.at[pl.ds((1 - net.y) * TP, TP)], qkv_other)
+
+    incoming = collect_during(net, back, (far_out, far_in, pass_out, pass_in), meanwhile)
+    part, gain_part = norm_backward(hidden[...], gain[...], incoming)
+    gain_grad[...] = gain_part
+    result = grad_middle[...] + part
+    upstream[...] = result
+    up_low[...] = result.astype(jnp.bfloat16)
+    net.finish()
+
+
+def attn_backward(
+    cid, moves, conts, grad_middle, hidden, gain, qkv, dmixed, mixed, lse, lengths, cosine, sine, rows, w_qkv
+):
+    bf, f32 = jnp.bfloat16, jnp.float32
+    shape = jax.ShapeDtypeStruct
+    block, depth = hidden.shape
+    total, width = qkv.shape
+    kinds = tuple(kind for kind, _ in moves)
+    sources = [source for _, source in moves]
+    n = len(moves)
+    urows = w_qkv.shape[3]
+    outs = [moved_shape(kind, source) for kind, source in moves] + [
+        shape((block, depth), f32),
+        shape((block, depth), bf),
+        shape((1, depth), f32),
+        shape((TP, TP, urows, width), bf),
+        shape((TP, TP, urows, width), bf),
+    ]
+    scratch = [
+        pltpu.VMEM((total, width), f32),
+        pltpu.VMEM((total, width), bf),
+        pltpu.VMEM((TP, block, depth), bf),
+        pltpu.VMEM(w_qkv.shape, bf),
+        pltpu.VMEM((2 * TP, TP, urows, width), bf),
+        pltpu.VMEM((2, block, depth), bf),
+        pltpu.VMEM((2, block, depth), bf),
+        pltpu.VMEM((block, depth), bf),
+        pltpu.VMEM((block, depth), bf),
+    ] + sems(48, 8)
+    return pl.pallas_call(
+        functools.partial(attn_backward_kernel, kinds, conts),
+        out_shape=outs,
+        in_specs=[IN_VMEM] * 10 + [ANYWHERE] * (2 + n),
+        out_specs=[ANYWHERE] * n + [IN_VMEM] * 3 + [ANYWHERE] * 2,
+        scratch_shapes=scratch,
+        compiler_params=pltpu.CompilerParams(
+            collective_id=cid, has_side_effects=True, vmem_limit_bytes=VMEM_LIMIT
+        ),
+        cost_estimate=pl.CostEstimate(
+            flops=16 * 10**9, bytes_accessed=200 * 2**20, transcendentals=10**7
+        ),
+    )(grad_middle, hidden, gain, qkv, dmixed, mixed, lse, lengths, cosine, sine, rows, w_qkv, *sources)
+
+
+def add_low(own, got):
+    return (own.astype(jnp.float32) + got.astype(jnp.float32)).astype(jnp.bfloat16)
+
+
+def z_total(summed, got, axis):
+    own = lax.dynamic_index_in_dim(summed, lax.axis_index("fsdp"), axis, keepdims=False)
+    return (own.astype(jnp.float32) + jnp.sum(got.astype(jnp.float32), axis=0)).astype(jnp.bfloat16)
+
+
+def end_kernel(step, qw, kw, *refs):
+    layers, refs = refs[:16], refs[16:]
+    x_outs, back, refs = refs[:2], refs[2], refs[3:]
+    out_x, out_back, out_q, out_k, out_v, out_o, out_g, out_u, out_d = refs
+    q = lax.rem(lax.axis_index("dp"), TP)
+    z = lax.axis_index("fsdp")
+    low, high = lax.rem(q, 2) == 1, lax.div(q, 2) == 1
+
+    def columns(blocks, got):
+        pieces = [blocks[q]] + [got[k] for k in range(3)]
+        a = [jnp.where(low, pieces[i ^ 1], pieces[i]) for i in range(4)]
+        return [jnp.where(high, a[i ^ 2], a[i]).astype(jnp.float32) for i in range(4)]
+
+    def lay(target, layer, pieces, at, width):
+        half = width // 2
+        for n, piece in enumerate(pieces):
+            for side in range(2):
+                to = (side * TP + n) * half
+                target[layer, :, to : to + half] = piece[:, at + side * half : at + (side + 1) * half]
+
+    for layer in range(2):
+        bqkv, tqkv, bgu, tgu, so, ro, sd, rd = layers[8 * layer : 8 * layer + 8]
+        pieces = columns(bqkv, tqkv)
+        lay(out_q, layer, pieces, 0, qw)
+        lay(out_k, layer, pieces, qw, kw)
+        lay(out_v, layer, pieces, qw + kw, kw)
+        pieces = columns(bgu, tgu)
+        lay(out_g, layer, pieces, 0, 2 * step)
+        lay(out_u, layer, pieces, 2 * step, 2 * step)
+        for summed, got, target in ((so, ro, out_o), (sd, rd, out_d)):
+            value = summed[z].astype(jnp.float32)
+            for k in range(3):
+                value = value + got[k].astype(jnp.float32)
+            target[layer] = value
+        out_x[layer] = x_outs[layer][...]
+    out_back[...] = back[...].astype(jnp.float32)
+
+
+def end_assembly(step, qw, kw, pieces, x_outs, back):
+    f32 = jnp.float32
+    shape = jax.ShapeDtypeStruct
+    block, depth = back.shape
+    rows = pieces[0].shape[1]
+    drows = pieces[6].shape[1]
+    outs = [
+        shape((2, block, depth), jnp.bfloat16),
+        shape((block, depth), f32),
+        shape((2, rows, TP * qw), f32),
+        shape((2, rows, TP * kw), f32),
+        shape((2, rows, TP * kw), f32),
+        shape((2, rows, depth), f32),
+        shape((2, rows, TP * 2 * step), f32),
+        shape((2, rows, TP * 2 * step), f32),
+        shape((2, drows, depth), f32),
+    ]
+    return pl.pallas_call(
+        functools.partial(end_kernel, step, qw, kw),
+        out_shape=outs,
+        in_specs=[IN_VMEM] * 19,
+        out_specs=[IN_VMEM] * 9,
+        compiler_params=pltpu.CompilerParams(vmem_limit_bytes=VMEM_LIMIT),
+    )(*pieces, *x_outs, back)
+
+
+def column_pack(weights):
+    parts = []
+    for weight in weights:
+        layers, rows, width = weight.shape
+        view = weight.reshape(layers, rows, 2, TP, width // (2 * TP))
+        parts.append(view.transpose(0, 3, 1, 2, 4).reshape(layers, TP, rows, width // TP))
+    return jnp.concatenate(parts, axis=3)
+
+
+def fast_device(
+    tokens, gain_attn, w_query, w_key, w_value, w_out, gain_ffn, w_gate, w_up, w_down, lengths, cotangent
+):
+    depth = tokens.shape[1]
+    shard = w_query.shape[1]
+    conts = lengths.shape[1]
+    halfway = HEAD_DIM // 2
+    qw, kw = w_query.shape[2] // TP, w_key.shape[2] // TP
+    step = w_gate.shape[2] // (2 * TP)
+    frequency = ROPE_BASE ** (-jnp.arange(halfway, dtype=jnp.float32) * 2.0 / HEAD_DIM)
+    lane = jnp.arange(128)[:, None]
+    column = jnp.arange(qw + 2 * kw)[None]
+    turned = column < qw + kw
+    frequency = jnp.pad(frequency, (0, 128 - halfway))[None]
+    picks = (lane == jnp.where(turned, column % halfway, halfway)).astype(jnp.float32)
+    signed = picks * jnp.where(turned, jnp.where(column % HEAD_DIM < halfway, -1.0, 1.0), 0.0)
+    gain_tile = jnp.pad(
+        jnp.concatenate([gain_attn, gain_ffn], axis=0).astype(jnp.float32), ((0, 4), (0, 128 - shard))
+    )
+    len_tile = jnp.pad(lengths, ((0, 7), (0, 128 - conts)))
+    (hidden, cosine, sine, lens, g_qkv0, g_qkv1, g_gu0, g_gu1, g_out0, g_out1, g_down0, g_down1, g_gain) = (
+        start_exchange(
+            conts, column_pack((w_query, w_key, w_value)), w_gate, w_up, w_out, w_down, gain_tile,
+            tokens, len_tile, frequency, picks, signed,
+        )
+    )
+    gains = jnp.transpose(g_gain[..., :4, :shard], (3, 0, 1, 2, 4)).reshape(4, 1, depth)
+    qkv, out, gu, down, qkv_next, out_next, gu_next, down_next = range(8)
+    programs0 = (
+        ((3, down, 0, 1), (1, gu, 0, 2), (1, gu, 2, 2)),
+        ((2, gu, 0, 2),),
+        ((2, gu, 2, 2), (3, gu, 0, 2)),
+        ((3, gu, 2, 2), (1, qkv_next, 0, 4), (1, out_next, 0, 1)),
+        ((2, qkv_next, 0, 4), (2, out_next, 0, 1), (1, down_next, 0, 1), (1, gu_next, 0, 2)),
+        ((3, qkv_next, 0, 4), (3, out_next, 0, 1), (2, down_next, 0, 1)),
+    )
+    programs1 = (
+        ((3, down, 0, 1), (2, gu, 0, 2), (1, gu, 2, 2)),
+        ((3, gu, 0, 2), (2, gu, 2, 2)),
+        (),
+        ((3, gu, 2, 2),),
+        (),
+        (),
+    )
+    tables = (cosine, sine, lens)
+    res = forward_layer(
+        programs0, cotangent, 2, conts, hidden, gains[0], gains[2], *tables,
+        (g_qkv0, g_out0, g_gu0, g_down0, g_qkv1, g_out1, g_gu1, g_down1),
+    )
+    weights0, moving1, acts0 = res[:4], res[4:8], res[8:]
+    (x1, mid0, lse0, low1, rows0, qkv0, mix0, frows0, gate0, up0, act0, branch) = acts0
+    res = forward_layer(programs1, None, 3, conts, x1, gains[1], gains[3], *tables, moving1)
+    weights1, acts1 = res[:4], res[4:]
+    (x2, mid1, lse1, low2, rows1, qkv1, mix1, frows1, gate1, up1, act1) = acts1
+
+    (low1_back, gmid1, ggf1, dmix1, d_own, d_got, gu_own, gu_other, o_own, o_other) = ffn_backward(
+        4, (("g", low1),), branch, True, mid1, gains[3], act1, frows1, gate1, up1, mix1,
+        weights1[3], weights1[2], weights1[1],
+    )
+    sd1 = add_low(d_own, d_got)
+    (gu_got, o_got, rd1, low2_back, up_1, _, gga1, qkv_own1, qkv_other1) = attn_backward(
+        5, (("y", gu_other), ("y", o_other), ("z", sd1), ("g", low2)), conts,
+        gmid1, x1, gains[1], qkv1, dmix1, mix1, lse1, lens, cosine, sine, rows1, weights1[0],
+    )
+    sgu1 = add_low(gu_own, gu_got)
+    so1 = add_low(o_own, o_got)
+    (qkv_got1, rgu1, ro1, gmid0, ggf0, dmix0, d_own0, d_got0, gu_own0, gu_other0, o_own0, o_other0) = ffn_backward(
+        6, (("y", qkv_other1), ("zc", sgu1), ("z", so1)), up_1, False, mid0, gains[2], act0, frows0, gate0, up0, mix0,
+        weights0[3], weights0[2], weights0[1],
+    )
+    sqkv1 = add_low(qkv_own1, qkv_got1)
+    sd0 = add_low(d_own0, d_got0)
+    bgu1 = z_total(sgu1, rgu1, 1)
+    (gu_got0, o_got0, rqkv1, rd0, tgu1, _, up_low, gga0, qkv_own0, qkv_other0) = attn_backward(
+        7, (("y", gu_other0), ("y", o_other0), ("zc", sqkv1), ("z", sd0), ("t", bgu1)), conts,
+        gmid0, hidden, gains[0], qkv0, dmix0, mix0, lse0, lens, cosine, sine, rows0, weights0[0],
+    )
+    sgu0 = add_low(gu_own0, gu_got0)
+    so0 = add_low(o_own0, o_got0)
+    bqkv1 = z_total(sqkv1, rqkv1, 1)
+    gain_part = jnp.concatenate([gga0, gga1, ggf0, ggf1, jnp.zeros((4, depth), jnp.float32)], axis=0)
+    (qkv_got0, rgu0, ro0, tqkv1, gain_t, back) = run_moves(
+        8,
+        (("y", qkv_other0), ("zc", sgu0), ("z", so0), ("t", bqkv1), ("whole_t", gain_part), ("g", up_low)),
+    )
+    sqkv0 = add_low(qkv_own0, qkv_got0)
+    bgu0 = z_total(sgu0, rgu0, 1)
+    gain_part = gain_part + jnp.sum(gain_t, axis=0)
+    (rqkv0, tgu0, gain_z) = run_moves(9, (("zc", sqkv0), ("t", bgu0), ("whole_z", gain_part)))
+    bqkv0 = z_total(sqkv0, rqkv0, 1)
+    gain_part = gain_part + jnp.sum(gain_z, axis=0)
+    (tqkv0, gain_y) = run_moves(10, (("t", bqkv0), ("whole_y", gain_part)))
+    gain_sums = (gain_part + gain_y)[:4]
+    device = lax.axis_index("dp") * lax.axis_size("fsdp") + lax.axis_index("fsdp")
+    own_gain = lax.dynamic_slice_in_dim(gain_sums, device * shard, shard, 1)
+    (out_x, out_back, grad_q, grad_k, grad_v, grad_o, grad_g, grad_u, grad_d) = end_assembly(
+        step, qw, kw,
+        (bqkv0, tqkv0, bgu0, tgu0, so0, ro0, sd0, rd0, bqkv1, tqkv1, bgu1, tgu1, so1, ro1, sd1, rd1),
+        (low1_back, low2_back), back,
+    )
+    return (
+        out_x, out_back, own_gain[:2], grad_q, grad_k, grad_v, grad_o, own_gain[2:], grad_g, grad_u, grad_d,
+    )
+
+
+def per_device(*arrays):
+    tokens, w_query, w_key, w_gate = arrays[0], arrays[2], arrays[3], arrays[7]
+    dp_size, z_size = lax.axis_size("dp"), lax.axis_size("fsdp")
+    suits = (
+        dp_size == 2 * TP
+        and z_size == TP
+        and w_key.shape[2] // HEAD_DIM == dp_size
+        and w_query.shape[2] == 2 * w_key.shape[2]
+        and tokens.shape[0] % 128 == 0
+        and w_query.shape[1] % 16 == 0
+        and w_gate.shape[2] % (TP * dp_size * 128) == 0
+    )
+    return (fast_device if suits else general_device)(*arrays)
+
+
 def solution(mesh):
     placed = (
         P(("dp", "fsdp"), None),

time: 3040 us -> 961 us (0.32)
  waiting for transfers between devices: 2260 us -> 0 us
  Pallas kernels: 0 us -> 896 us
  matrix products: 409 us -> 0 us
  local copies, waits for them, and re-layouts: 128 us -> 18.9 us
  blocking collectives: 77.8 us -> 0 us
  other arithmetic: 84.2 us -> 36.2 us
  loops' own time: 43.6 us -> 0 us
    reduce_scatter x30 -> x0, waiting for transfers between devices: 1330 us -> none  [the longest x2 192 us: layer_backward(): lax.psum_scatter(grad_up_w.astype(jnp.bfloat16), 'dp', scatter_dimension=...]
    all_gather x16 -> x0, waiting for transfers between devices: 931 us -> none  [the longest x2 179 us: fetch_ffn(): lax.all_gather(w_down[layer_index], ('dp', 'fsdp'), axis=0, tiled=True)]
    pallas_call x0 -> x11, Pallas kernels: none -> 896 us  [the longest x2 300 us: forward_layer(): pl.pallas_call(functools.partial(forward_kernel, programs, bool(c), conts...]
    dot_general x154 -> x0, matrix products: 409 us -> none  [the longest x42 251 us: matmul(): return jnp.dot(left, right, preferred_element_type=jnp.float32)]
    unnamed x3 -> x0, blocking collectives: 77.8 us -> none
    dynamic_slice x64 -> x0, local copies, waits for them, and re-layouts: 49.1 us -> none  [the longest x32 20 us: attend_forward(): lax.map(per_head, jnp.arange(kv_heads, dtype=jnp.int32))]
    another operation x4 -> x0, loops' own time: 43.6 us -> none  [the longest x2 22.1 us: attend_backward(): lax.map(per_head, (jnp.arange(kv_heads, dtype=jnp.int32), peak_score, tot...]
    unnamed x149 -> x44, local copies, waits for them, and re-layouts: 32.8 us -> 1.76 us
  transfers between devices with their start and end apart: 46 -> 0, of which waited for: 42 -> 0; matrix products, arithmetic and copies ran while one was open for 11% -> 0% of each run, Pallas kernels for 0% -> 0%
where the time goes in v3:
time: 961 us; the launch traced here: 953 us
  Pallas kernels  896 us (93%)
  other arithmetic  36.2 us (4%)
  local copies, waits for them, and re-layouts  18.9 us (2%)
    pallas_call x2, Pallas kernels, forward_layer(): pl.pallas_call(functools.partial(forward_kernel, programs, bool(c), conts...  300 us
    pallas_call x2, Pallas kernels, attn_backward(): pl.pallas_call(functools.partial(attn_backward_kernel, kinds, conts), out...  189 us
    pallas_call x2, Pallas kernels, ffn_backward(): pl.pallas_call(functools.partial(ffn_backward_kernel, kinds, given), out_...  147 us
    pallas_call x3, Pallas kernels, run_moves(): pl.pallas_call(functools.partial(move_kernel, kinds), out_shape=[moved_sh...  141 us
    pallas_call x1, Pallas kernels, start_exchange(): pl.pallas_call(functools.partial(start_kernel, conts), out_shape=outs, in...  110 us

profile of v3, /device:TPU:0, one launch (start us, length us, event | category | flops | bytes accessed | tf_op | source)
XLA Modules:
  0.0 952.9 jit_solution(8335716222191883516)
XLA Ops:
  0.7 0.8 fusion.4.spread_sin
  1.5 0.8 fusion.5.spread_cos
  2.2 1.4 reshape.99
  5.3 0.9 pad_maximum_fusion.qkv_pack
  6.3 0.6 fusion.21.gain_tile
  6.9 0.6 pad.16.lengths
  8.0 110.0 %shard_map.203 = (f32[256,1536]{1,0:T(8,128)}, f32[1024,768]{1,0:T(8,128)}, f32[1024,768]{1,0:T(8,128)}, s32[8,128]{1,0:T(8,128)}, bf16[2,4,4,48,768]{4,3,2,1,0:...) custom-call(bf16[2,4,48,768]{3,2,1,0:T(8,128)(2,1)} %pad_maximum_fus, ...), custom_call_target="tpu_custom_call" | custom-call | bytes 314572800 | tf_op jit(solution)/shard_map/pallas_call | solution.py:717
  118.0 0.9 slice_bitcast_fusion
  119.1 0.7 squeeze.22.refs_1_.refs_2_
  119.8 0.7 squeeze.23.refs_2_.refs_1_
  120.5 182.4 %shard_map.204 = (bf16[2,4,4,48,768]{4,3,2,1,0:T(8,128)(2,1)}, bf16[2,1,4,48,1536]{4,3,2,1,0:T(8,128)(2,1)}, bf16[2,4,4,48,2048]{4,3,2,1,0:T(8,128)(2,1)}, bf16[...) custom-call(f32[256,1536]{1,0:T(8,128)} %get-tuple-element.117.refs_, ...), custom_call_target="tpu_custom_call", output_to_operand_aliasing={{0}: (7, {}), {1}: (8, {}), {2}: (9, {}), {3}: (10, {}), {4... | custom-call | flops 16000000000 | bytes 419430400 | tf_op jit(solution)/shard_map/pallas_call | solution.py:968
  302.9 0.7 squeeze.24.refs_1_.refs_2_
  303.6 0.7 squeeze.25.refs_2_.refs_1_
  304.2 117.3 %shard_map.205 = (bf16[2,4,4,48,768]{4,3,2,1,0:T(8,128)(2,1)}, bf16[2,1,4,48,1536]{4,3,2,1,0:T(8,128)(2,1)}, bf16[2,4,4,48,2048]{4,3,2,1,0:T(8,128)(2,1)}, bf16[...) custom-call(f32[256,1536]{1,0:T(8,128)} %get-tuple-element.131.refs_, ...), custom_call_target="tpu_custom_call", output_to_operand_aliasing={{0}: (6, {}), {1}: (7, {}), {2}: (8, {}), {3}: (9, {})} | custom-call | flops 16000000000 | bytes 419430400 | tf_op jit(solution)/shard_map/pallas_call | solution.py:968
  421.5 61.1 %shard_map.206 = (bf16[256,1536]{1,0:T(8,128)(2,1)}, f32[256,1536]{1,0:T(8,128)}, f32[1,1536]{1,0:T(1,128)}, bf16[1024,384]{1,0:T(8,128)(2,1)}, bf16[4,128,1536]...) custom-call(f32[256,1536]{1,0:T(8,128)} %get-tuple-element.136.refs_, ...), custom_call_target="tpu_custom_call" | custom-call | flops 24000000000 | bytes 209715200 | tf_op jit(solution)/shard_map/pallas_call | solution.py:1252
  482.7 3.5 add_convert_fusion.3.refs_14_
  486.2 97.7 %shard_map.207 = (bf16[4,4,48,2048]{3,2,1,0:T(8,128)(2,1)}, bf16[4,48,1536]{2,1,0:T(8,128)(2,1)}, bf16[3,128,1536]{2,1,0:T(8,128)(2,1)}, bf16[256,1536]{1,0:T(8,...) custom-call(f32[256,1536]{1,0:T(8,128)} %get-tuple-element.147.refs_, ...), custom_call_target="tpu_custom_call" | custom-call | flops 16000000000 | bytes 209715200 | tf_op jit(solution)/shard_map/pallas_call | solution.py:1390
  583.8 2.0 add_convert_fusion.7.refs_13_.refs_12_
  585.9 4.2 add_convert_fusion.1
  590.1 2.1 copy.40.refs_12_
  592.7 85.8 %shard_map.208 = (bf16[4,4,48,768]{3,2,1,0:T(8,128)(2,1)}, bf16[3,4,48,2048]{3,2,1,0:T(8,128)(2,1)}, bf16[3,48,1536]{2,1,0:T(8,128)(2,1)}, f32[256,1536]{1,0:T(8...) custom-call(f32[256,1536]{1,0:T(8,128)} %get-tuple-element.130.refs_, ...), custom_call_target="tpu_custom_call" | custom-call | flops 24000000000 | bytes 209715200 | tf_op jit(solution)/shard_map/pallas_call | solution.py:1252
  678.5 2.3 convert_reduce_fusion.1
  680.9 2.3 fusion.1.refs_16_.refs_10_
  683.2 1.6 add_convert_fusion.2.refs_15_.refs_6_
  684.8 0.6 copy-done.7
  685.7 1.1 copy.43.refs_14_
  686.8 91.7 %shard_map.209 = (bf16[4,4,48,2048]{3,2,1,0:T(8,128)(2,1)}, bf16[4,48,1536]{2,1,0:T(8,128)(2,1)}, bf16[3,4,48,768]{3,2,1,0:T(8,128)(2,1)}, bf16[3,128,1536]{2,1,...) custom-call(f32[256,1536]{1,0:T(8,128)} %get-tuple-element.172.refs_, ...), custom_call_target="tpu_custom_call" | custom-call | flops 16000000000 | bytes 209715200 | tf_op jit(solution)/shard_map/pallas_call | solution.py:1390
  778.5 1.4 concatenate.11.refs_4_
  780.0 1.5 convert_reduce_fusion.3
  781.5 0.8 fusion.3.refs_3_.refs_8_
  782.3 1.0 add_convert_fusion.6.refs_2_.refs_4_
  783.2 3.2 add_convert_fusion
  786.5 2.1 copy.47.refs_1_
  789.1 91.5 %shard_map.210 = (bf16[4,4,48,768]{3,2,1,0:T(8,128)(2,1)}, bf16[3,4,48,2048]{3,2,1,0:T(8,128)(2,1)}, bf16[3,48,1536]{2,1,0:T(8,128)(2,1)}, bf16[3,48,768]{2,1,0:...) custom-call(bf16[4,4,48,768]{3,2,1,0:T(8,128)(2,1)} %get-tuple-element.186.refs_0_, ...), custom_call_target="tpu_custom_call" | custom-call | bytes 209715200 | tf_op jit(solution)/shard_map/pallas_call | solution.py:1045
  880.6 0.9 reduce_sum.57
  881.5 0.6 add.101.refs_2_
  882.1 2.3 convert_reduce_fusion
  884.5 2.4 fusion.refs_1_.refs_2_
  887.2 1.1 copy.49.refs_0_
  888.3 43.7 %shard_map.211 = (bf16[3,4,48,768]{3,2,1,0:T(8,128)(2,1)}, bf16[3,48,2048]{2,1,0:T(8,128)(2,1)}, f32[3,8,1536]{2,1,0:T(8,128)}) custom-call(bf16[4,4,48,768]{3,2,1,0:T(8,128)(2,1)} %copy.49.refs_0_, bf16[4,48,2048]{2,1,0:T(8,128)(2,1)} %fusion.refs_1_.refs_2_, f32[8,1536]{1,0:T(8,128)} %add.101.refs_2_), custom_call_target="tpu_custom_call" | custom-call | bytes 209715200 | tf_op jit(solution)/shard_map/pallas_call | solution.py:1045
  932.0 0.9 reduce_sum.59
  932.9 0.6 add.103.refs_1_
  933.6 1.4 convert_reduce_fusion.2
  934.9 0.8 fusion.2.refs_0_
  935.7 6.3 shard_map.212
  942.0 0.8 slice.45
  942.9 0.6 fusion.22
  943.5 8.9 shard_map.213
  (62 shorter events, 4.2 us)
Async XLA Ops:
  0.6 3.5 copy-start.14
  2.2 2.5 copy-start.15
  4.4 1.8 copy-start.19
  4.4 1.8 copy-start.20
  4.4 2.4 copy-start.21
  486.2 97.7 %copy-start.10 = (bf16[4,48,1536]{2,1,0:T(8,128)(2,1)S(1)}, bf16[4,48,1536]{2,1,0:T(8,128)(2,1)}, u32[]{:S(2)}) copy-start(bf16[4,48,1536]{2,1,0:T(8,128)(2,1)} %get-tuple-element.170) | copy-start | bytes 1769476
  590.1 2.6 copy-start
  680.8 2.4 copy-start.3
  680.8 2.4 copy-start.4
  683.2 1.6 copy-start.5
  683.2 2.2 copy-start.7
  686.8 91.7 %copy-start.16 = (f32[1,1536]{1,0:T(1,128)S(1)}, f32[1,1536]{1,0:T(1,128)}, u32[]{:S(2)}) copy-start(f32[1,1536]{1,0:T(1,128)} %get-tuple-element.195) | copy-start | bytes 18436
  686.8 91.7 %copy-start.17 = (f32[1,1536]{1,0:T(1,128)S(1)}, f32[1,1536]{1,0:T(1,128)}, u32[]{:S(2)}) copy-start(f32[1,1536]{1,0:T(1,128)} %get-tuple-element.193) | copy-start | bytes 18436
  686.8 91.7 %copy-start.18 = (f32[1,1536]{1,0:T(1,128)S(1)}, f32[1,1536]{1,0:T(1,128)}, u32[]{:S(2)}) copy-start(f32[1,1536]{1,0:T(1,128)} %get-tuple-element.194) | copy-start | bytes 18436
  778.5 3.8 copy-start.9
  778.5 3.8 copy-start.11
  780.0 3.3 copy-start.2
  786.5 2.6 copy-start.1
  789.1 92.4 %copy-start.12 = (f32[8,1536]{1,0:T(8,128)S(1)}, f32[8,1536]{1,0:T(8,128)}, u32[]{:S(2)}) copy-start(f32[8,1536]{1,0:T(8,128)} %concatenate.11.refs_4_) | copy-start | bytes 147460
  884.5 2.4 copy-start.6
  884.5 2.4 copy-start.8
  888.3 44.6 %copy-start.13 = (f32[8,1536]{1,0:T(8,128)S(1)}, f32[8,1536]{1,0:T(8,128)}, u32[]{:S(2)}) copy-start(f32[8,1536]{1,0:T(8,128)} %add.101.refs_2_) | copy-start | bytes 147460
  933.6 9.3 slice-start

commit v4 on v3

--- a/solution.py
+++ b/solution.py
@@ -543,6 +543,10 @@
             part = lambda bits: ref.at[self.y, pl.ds(low, count), flip_index(self.z, bits)]
             if stage == 1:
                 sent = ((0, "z2"), (0, "z1"), (0, "y"))
+            elif stage == 4:
+                sent = ((0, "y"),)
+            elif stage == 5:
+                sent = ((0, "z2"), (0, "z1"))
             elif stage == 2:
                 sent = ((2, "z1"), (1, "y"), (2, "y"))
             else:
@@ -681,14 +685,16 @@
 
     table(0)
     net.advance(((2, g_out0, 0, 1), (2, g_qkv0, 0, TP), (2, g_gain, 0, TP)))
+    for copy in second[:16] + placed[2:]:
+        copy.wait()
+    second = second[16:]
+    net.advance(((4, g_gu0, 0, TP), (4, g_down1, 0, 1), (4, g_out1, 0, 1)))
     table(1)
     net.advance(((3, g_out0, 0, 1), (3, g_qkv0, 0, TP), (3, g_gain, 0, TP), (2, g_down0, 0, 1)))
     table(2)
     table(3)
     bring[1].wait()
     tok_out[...] = tok_buf[...].astype(jnp.float32)
-    for copy in placed[2:]:
-        copy.wait()
     for copy in second:
         copy.wait()
     net.finish()
@@ -1031,28 +1037,128 @@
     net.greet(PEERS, "home" if "g" in kinds else None)
 
 
-def move_kernel(kinds, *refs):
-    n = len(kinds)
-    net = Net(*refs[2 * n :])
-    greet_all(net, kinds)
-    begin_moves(net, kinds, refs[:n], refs[n : 2 * n])
+def tail_kernel(
+    gain_part, sgu_in, so_in, qkv_own_in, qkv_other, bqkv, up_low,
+    gain_out, out_sum, b_gu, b_qkv, t_gu, t_qkv, t_qkv1, back,
+    sgu, so, s_qkv, qkv_got, gu_one, gu_pass, gu_two, o_one, o_pass, o_two, q_one, q_pass, q_two,
+    gain_t, gain_a, gain_z, gain_b, gain_y, send_sems, recv_sems, local_sems,
+):
+    net = Net(send_sems, recv_sems, local_sems)
+    f32, bf = jnp.float32, jnp.bfloat16
+    z, q = net.z, net.q
+    z1, z2, z3 = (flip_index(z, bits) for bits in (1, 2, 3))
+    loads = [net.local(sgu_in, sgu), net.local(so_in, so), net.local(qkv_own_in, s_qkv)]
+    net.greet(PEERS, "home")
+    over_y = net.remote(qkv_other, qkv_got, "y")
+
+    def first_hop(source, target, part):
+        return [
+            net.remote(source.at[part + (z3,)], target.at[(1,) + part], "z1"),
+            net.remote(source.at[part + (z1,)], target.at[(0,) + part], "z1"),
+        ]
+
+    halves = [(pl.ds(0, 2),), (pl.ds(2, 2),)]
+    gu_first = [first_hop(sgu_in, gu_one, part) for part in halves]
+    o_first = first_hop(so_in, o_one, ())
+    gains = [net.remote(gain_part, gain_t.at[bits - 1], name) for name, bits in RANK_PEERS]
+    net.flying += begin_move(net, "t", bqkv, t_qkv1)
+    net.flying += begin_move(net, "g", up_low, back)
+    for copy in loads:
+        copy.wait()
+    over_y.wait()
+    s_qkv[...] = (s_qkv[...].astype(f32) + qkv_got[...].astype(f32)).astype(bf)
+    every = (pl.ds(0, TP),)
+    q_first = first_hop(s_qkv, q_one, every)
+    for copy in gains:
+        copy.wait()
+    gain_a[...] = gain_part[...] + gain_t[0] + gain_t[1] + gain_t[2]
+    gains = [net.remote(gain_a, gain_z.at[bits - 1], f"z{bits}") for bits in (1, 2, 3)]
+
+    def second_hop(own, one, passing, two, part, first):
+        first[0].wait()
+        passing[part or (Ellipsis,)] = (
+            own[part + (z2,)].astype(f32) + one[(1,) + part].astype(f32)
+        ).astype(bf)
+        at = (lambda ref: ref.at[part]) if part else (lambda ref: ref)
+        return net.remote(at(passing), at(two), "z2")
+
+    gu_second = [
+        second_hop(sgu, gu_one, gu_pass, gu_two, part, first) for part, first in zip(halves, gu_first)
+    ]
+    o_second = second_hop(so, o_one, o_pass, o_two, (), o_first)
+    q_second = second_hop(s_qkv, q_one, q_pass, q_two, every, q_first)
+    for copy in gains:
+        copy.wait()
+    gain_b[...] = gain_a[...] + gain_z[0] + gain_z[1] + gain_z[2]
+    gain_over_y = net.remote(gain_b, gain_y, "y")
+
+    def total(own, one, two, part):
+        whole = part or (Ellipsis,)
+        return (
+            own[part + (z,)].astype(f32) + one[(0,) + part].astype(f32) + two[whole].astype(f32)
+        )
+
+    for part, first, second in zip(halves, gu_first, gu_second):
+        first[1].wait()
+        second.wait()
+        b_gu[part] = total(sgu, gu_one, gu_two, part).astype(bf)
+    net.flying += begin_move(net, "t", b_gu, t_gu)
+    o_first[1].wait()
+    o_second.wait()
+    out_sum[...] = total(so, o_one, o_two, ())
+    q_first[1].wait()
+    q_second.wait()
+    b_qkv[...] = total(s_qkv, q_one, q_two, every).astype(bf)
+    net.flying += begin_move(net, "t", b_qkv, t_qkv)
+    gain_over_y.wait()
+    gain_out[...] = gain_b[...] + gain_y[...]
     net.finish()
 
 
-def run_moves(cid, moves):
-    kinds = tuple(kind for kind, _ in moves)
-    sources = [source for _, source in moves]
+def run_tail(cid, gain_part, sgu, so, qkv_own, qkv_other, bqkv, up_low):
+    bf, f32 = jnp.bfloat16, jnp.float32
+    shape = jax.ShapeDtypeStruct
+    gu_block = (TP,) + sgu.shape[2:]
+    o_block = so.shape[1:]
+    q_block = (TP,) + qkv_own.shape[2:]
+    three = lambda block: (3,) + block[1:]
     return pl.pallas_call(
-        functools.partial(move_kernel, kinds),
-        out_shape=[moved_shape(kind, source) for kind, source in moves],
-        in_specs=[ANYWHERE] * len(moves),
-        out_specs=[ANYWHERE] * len(moves),
-        scratch_shapes=sems(32, 4),
+        tail_kernel,
+        out_shape=[
+            shape(gain_part.shape, f32),
+            shape(o_block, f32),
+            shape(gu_block, bf),
+            shape(q_block, bf),
+            shape(three(gu_block), bf),
+            shape(three(q_block), bf),
+            shape(three(q_block), bf),
+            shape(up_low.shape, bf),
+        ],
+        in_specs=[IN_VMEM] + [ANYWHERE] * 6,
+        out_specs=[IN_VMEM] * 4 + [ANYWHERE] * 4,
+        scratch_shapes=[
+            pltpu.VMEM(sgu.shape, bf),
+            pltpu.VMEM(so.shape, bf),
+            pltpu.VMEM(qkv_own.shape, bf),
+            pltpu.VMEM(qkv_own.shape, bf),
+        ]
+        + [
+            pltpu.VMEM(dims, bf)
+            for block in (gu_block, o_block, q_block)
+            for dims in ((2,) + block, block, block)
+        ]
+        + [
+            pltpu.VMEM(dims, f32)
+            for dims in (
+                (3,) + gain_part.shape, gain_part.shape, (3,) + gain_part.shape, gain_part.shape, gain_part.shape
+            )
+        ]
+        + sems(48, 8),
         compiler_params=pltpu.CompilerParams(
             collective_id=cid, has_side_effects=True, vmem_limit_bytes=VMEM_LIMIT
         ),
         cost_estimate=pl.CostEstimate(flops=0, bytes_accessed=200 * 2**20, transcendentals=0),
-    )(*sources)
+    )(gain_part, sgu, so, qkv_own, qkv_other, bqkv, up_low)
 
 
 def norm_backward(values, gain_row, incoming):
@@ -1412,7 +1518,7 @@
 
 
 def end_kernel(step, qw, kw, *refs):
-    layers, refs = refs[:16], refs[16:]
+    layers, refs = (refs[:7], refs[7:15]), refs[15:]
     x_outs, back, refs = refs[:2], refs[2], refs[3:]
     out_x, out_back, out_q, out_k, out_v, out_o, out_g, out_u, out_d = refs
     q = lax.rem(lax.axis_index("dp"), TP)
@@ -1432,7 +1538,7 @@
                 target[layer, :, to : to + half] = piece[:, at + side * half : at + (side + 1) * half]
 
     for layer in range(2):
-        bqkv, tqkv, bgu, tgu, so, ro, sd, rd = layers[8 * layer : 8 * layer + 8]
+        bqkv, tqkv, bgu, tgu = layers[layer][:4]
         pieces = columns(bqkv, tqkv)
         lay(out_q, layer, pieces, 0, qw)
         lay(out_k, layer, pieces, qw, kw)
@@ -1440,7 +1546,12 @@
         pieces = columns(bgu, tgu)
         lay(out_g, layer, pieces, 0, 2 * step)
         lay(out_u, layer, pieces, 2 * step, 2 * step)
-        for summed, got, target in ((so, ro, out_o), (sd, rd, out_d)):
+        sums = [(*layers[layer][-2:], out_d)]
+        if layer == 0:
+            out_o[0] = layers[0][4][...]
+        else:
+            sums.append((*layers[1][4:6], out_o))
+        for summed, got, target in sums:
             value = summed[z].astype(jnp.float32)
             for k in range(3):
                 value = value + got[k].astype(jnp.float32)
@@ -1454,7 +1565,7 @@
     shape = jax.ShapeDtypeStruct
     block, depth = back.shape
     rows = pieces[0].shape[1]
-    drows = pieces[6].shape[1]
+    drows = pieces[5].shape[1]
     outs = [
         shape((2, block, depth), jnp.bfloat16),
         shape((block, depth), f32),
@@ -1469,7 +1580,7 @@
     return pl.pallas_call(
         functools.partial(end_kernel, step, qw, kw),
         out_shape=outs,
-        in_specs=[IN_VMEM] * 19,
+        in_specs=[IN_VMEM] * 18,
         out_specs=[IN_VMEM] * 9,
         compiler_params=pltpu.CompilerParams(vmem_limit_bytes=VMEM_LIMIT),
     )(*pieces, *x_outs, back)
@@ -1513,11 +1624,11 @@
     gains = jnp.transpose(g_gain[..., :4, :shard], (3, 0, 1, 2, 4)).reshape(4, 1, depth)
     qkv, out, gu, down, qkv_next, out_next, gu_next, down_next = range(8)
     programs0 = (
-        ((3, down, 0, 1), (1, gu, 0, 2), (1, gu, 2, 2)),
+        ((3, down, 0, 1), (5, gu, 0, 2), (5, gu, 2, 2)),
         ((2, gu, 0, 2),),
         ((2, gu, 2, 2), (3, gu, 0, 2)),
-        ((3, gu, 2, 2), (1, qkv_next, 0, 4), (1, out_next, 0, 1)),
-        ((2, qkv_next, 0, 4), (2, out_next, 0, 1), (1, down_next, 0, 1), (1, gu_next, 0, 2)),
+        ((3, gu, 2, 2), (1, qkv_next, 0, 4), (5, out_next, 0, 1)),
+        ((2, qkv_next, 0, 4), (2, out_next, 0, 1), (5, down_next, 0, 1), (1, gu_next, 0, 2)),
         ((3, qkv_next, 0, 4), (3, out_next, 0, 1), (2, down_next, 0, 1)),
     )
     programs1 = (
@@ -1565,23 +1676,15 @@
     so0 = add_low(o_own0, o_got0)
     bqkv1 = z_total(sqkv1, rqkv1, 1)
     gain_part = jnp.concatenate([gga0, gga1, ggf0, ggf1, jnp.zeros((4, depth), jnp.float32)], axis=0)
-    (qkv_got0, rgu0, ro0, tqkv1, gain_t, back) = run_moves(
-        8,
-        (("y", qkv_other0), ("zc", sgu0), ("z", so0), ("t", bqkv1), ("whole_t", gain_part), ("g", up_low)),
-    )
-    sqkv0 = add_low(qkv_own0, qkv_got0)
-    bgu0 = z_total(sgu0, rgu0, 1)
-    gain_part = gain_part + jnp.sum(gain_t, axis=0)
-    (rqkv0, tgu0, gain_z) = run_moves(9, (("zc", sqkv0), ("t", bgu0), ("whole_z", gain_part)))
-    bqkv0 = z_total(sqkv0, rqkv0, 1)
-    gain_part = gain_part + jnp.sum(gain_z, axis=0)
-    (tqkv0, gain_y) = run_moves(10, (("t", bqkv0), ("whole_y", gain_part)))
-    gain_sums = (gain_part + gain_y)[:4]
+    (gain_sums, osum0, bgu0, bqkv0, tgu0, tqkv0, tqkv1, back) = run_tail(
+        8, gain_part, sgu0, so0, qkv_own0, qkv_other0, bqkv1, up_low
+    )
+    gain_sums = gain_sums[:4]
     device = lax.axis_index("dp") * lax.axis_size("fsdp") + lax.axis_index("fsdp")
     own_gain = lax.dynamic_slice_in_dim(gain_sums, device * shard, shard, 1)
     (out_x, out_back, grad_q, grad_k, grad_v, grad_o, grad_g, grad_u, grad_d) = end_assembly(
         step, qw, kw,
-        (bqkv0, tqkv0, bgu0, tgu0, so0, ro0, sd0, rd0, bqkv1, tqkv1, bgu1, tgu1, so1, ro1, sd1, rd1),
+        (bqkv0, tqkv0, bgu0, tgu0, osum0, sd0, rd0, bqkv1, tqkv1, bgu1, tgu1, so1, ro1, sd1, rd1),
         (low1_back, low2_back), back,
     )
     return (

time: 961 us -> 941 us (0.979)
    pallas_call x3 -> x1, Pallas kernels: 141 us -> 118 us  [run_tail(): pl.pallas_call(tail_kernel, out_shape=[shape(gain_part.shape, f32), shape...]
    pallas_call x1, Pallas kernels: 110 us -> 133 us  [start_exchange(): pl.pallas_call(functools.partial(start_kernel, conts), out_shape=outs, in...]
where the time goes in v4:
time: 941 us; the launch traced here: 933 us
  Pallas kernels  890 us (95%)
  other arithmetic  27.5 us (3%)
  local copies, waits for them, and re-layouts  13.6 us (1%)
    pallas_call x2, Pallas kernels, forward_layer(): pl.pallas_call(functools.partial(forward_kernel, programs, bool(c), conts...  296 us
    pallas_call x2, Pallas kernels, attn_backward(): pl.pallas_call(functools.partial(attn_backward_kernel, kinds, conts), out...  188 us
    pallas_call x2, Pallas kernels, ffn_backward(): pl.pallas_call(functools.partial(ffn_backward_kernel, kinds, given), out_...  147 us
    pallas_call x1, Pallas kernels, start_exchange(): pl.pallas_call(functools.partial(start_kernel, conts), out_shape=outs, in...  133 us
    pallas_call x1, Pallas kernels, run_tail(): pl.pallas_call(tail_kernel, out_shape=[shape(gain_part.shape, f32), shape...  118 us

profile of v4, /device:TPU:0, one launch (start us, length us, event | category | flops | bytes accessed | tf_op | source)
XLA Modules:
  0.0 932.8 jit_solution(12496699987105533696)
XLA Ops:
  0.7 0.8 fusion.2.spread_sin
  1.5 0.8 fusion.3.spread_cos
  2.2 1.3 reshape.95
  3.6 0.3 copy.51
  3.9 0.2 reshape.96
  4.2 0.2 reshape.99
  4.4 0.2 copy.52
  4.6 0.1 reshape.100
  4.7 0.2 reshape.97
  5.0 0.2 copy.53
  5.1 0.1 reshape.98
  5.3 0.9 pad_maximum_fusion.qkv_pack
  6.2 0.6 fusion.19.gain_tile
  6.8 0.6 pad.16.lengths
  7.4 0.5 pad_bitcast_fusion.frequency
  8.0 133.2 %shard_map.203 = (f32[256,1536]{1,0:T(8,128)}, f32[1024,768]{1,0:T(8,128)}, f32[1024,768]{1,0:T(8,128)}, s32[8,128]{1,0:T(8,128)}, bf16[2,4,4,48,768]{4,3,2,1,0:...) custom-call(bf16[2,4,48,768]{3,2,1,0:T(8,128)(2,1)} %pad_maximum_fus, ...), custom_call_target="tpu_custom_call" | custom-call | bytes 314572800 | tf_op jit(solution)/shard_map/pallas_call | solution.py:723
  141.2 0.9 slice_bitcast_fusion
  142.1 0.2 slice_reduce_fusion
  142.3 0.7 squeeze.20.refs_1_.refs_2_
  143.0 0.7 squeeze.21.refs_2_.refs_1_
  143.7 178.7 %shard_map.204 = (bf16[2,4,4,48,768]{4,3,2,1,0:T(8,128)(2,1)}, bf16[2,1,4,48,1536]{4,3,2,1,0:T(8,128)(2,1)}, bf16[2,4,4,48,2048]{4,3,2,1,0:T(8,128)(2,1)}, bf16[...) custom-call(f32[256,1536]{1,0:T(8,128)} %get-tuple-element.114.refs_, ...), custom_call_target="tpu_custom_call", output_to_operand_aliasing={{0}: (7, {}), {1}: (8, {}), {2}: (9, {}), {3}: (10, {}), {4... | custom-call | flops 16000000000 | bytes 419430400 | tf_op jit(solution)/shard_map/pallas_call | solution.py:974
  322.5 0.7 squeeze.22.refs_1_.refs_2_
  323.1 0.7 squeeze.23.refs_2_.refs_1_
  323.8 117.3 %shard_map.205 = (bf16[2,4,4,48,768]{4,3,2,1,0:T(8,128)(2,1)}, bf16[2,1,4,48,1536]{4,3,2,1,0:T(8,128)(2,1)}, bf16[2,4,4,48,2048]{4,3,2,1,0:T(8,128)(2,1)}, bf16[...) custom-call(f32[256,1536]{1,0:T(8,128)} %get-tuple-element.128.refs_, ...), custom_call_target="tpu_custom_call", output_to_operand_aliasing={{0}: (6, {}), {1}: (7, {}), {2}: (8, {}), {3}: (9, {})} | custom-call | flops 16000000000 | bytes 419430400 | tf_op jit(solution)/shard_map/pallas_call | solution.py:974
  441.1 61.1 %shard_map.206 = (bf16[256,1536]{1,0:T(8,128)(2,1)}, f32[256,1536]{1,0:T(8,128)}, f32[1,1536]{1,0:T(1,128)}, bf16[1024,384]{1,0:T(8,128)(2,1)}, bf16[4,128,1536]...) custom-call(f32[256,1536]{1,0:T(8,128)} %get-tuple-element.133.refs_, ...), custom_call_target="tpu_custom_call" | custom-call | flops 24000000000 | bytes 209715200 | tf_op jit(solution)/shard_map/pallas_call | solution.py:1358
  502.3 3.5 add_convert_fusion.3.refs_14_.refs_13_
  505.8 97.0 %shard_map.207 = (bf16[4,4,48,2048]{3,2,1,0:T(8,128)(2,1)}, bf16[4,48,1536]{2,1,0:T(8,128)(2,1)}, bf16[3,128,1536]{2,1,0:T(8,128)(2,1)}, bf16[256,1536]{1,0:T(8,...) custom-call(f32[256,1536]{1,0:T(8,128)} %get-tuple-element.144.refs_, ...), custom_call_target="tpu_custom_call" | custom-call | flops 16000000000 | bytes 209715200 | tf_op jit(solution)/shard_map/pallas_call | solution.py:1496
  602.8 2.0 add_convert_fusion.6.refs_13_.refs_11_
  604.8 4.2 add_convert_fusion.1
  609.0 2.1 copy.40.refs_12_
  611.1 0.5 copy-done
  611.7 85.9 %shard_map.208 = (bf16[4,4,48,768]{3,2,1,0:T(8,128)(2,1)}, bf16[3,4,48,2048]{3,2,1,0:T(8,128)(2,1)}, bf16[3,48,1536]{2,1,0:T(8,128)(2,1)}, f32[256,1536]{1,0:T(8...) custom-call(f32[256,1536]{1,0:T(8,128)} %get-tuple-element.127.refs_, ...), custom_call_target="tpu_custom_call" | custom-call | flops 24000000000 | bytes 209715200 | tf_op jit(solution)/shard_map/pallas_call | solution.py:1358
  697.6 2.3 convert_reduce_fusion
  699.9 2.4 fusion.refs_16_.refs_9_
  702.2 1.6 add_convert_fusion.2.refs_15_.refs_5_
  703.9 0.6 copy-done.5
  704.4 0.3 add_convert_fusion.4
  704.7 1.1 copy.43.refs_14_
  705.8 90.5 %shard_map.209 = (bf16[4,4,48,2048]{3,2,1,0:T(8,128)(2,1)}, bf16[4,48,1536]{2,1,0:T(8,128)(2,1)}, bf16[3,4,48,768]{3,2,1,0:T(8,128)(2,1)}, bf16[3,128,1536]{2,1,...) custom-call(f32[256,1536]{1,0:T(8,128)} %get-tuple-element.169.refs_, ...), custom_call_target="tpu_custom_call" | custom-call | flops 16000000000 | bytes 209715200 | tf_op jit(solution)/shard_map/pallas_call | solution.py:1496
  796.4 1.5 convert_reduce_fusion.1
  797.9 0.8 fusion.1.bqkv.refs_7_
  798.6 1.0 add_convert_fusion.5.so_in
  799.6 5.0 add_convert_fusion.sgu_in
  804.6 0.7 concatenate.11.gain_part
  805.3 117.7 %shard_map.210 = (f32[8,1536]{1,0:T(8,128)}, f32[48,1536]{1,0:T(8,128)}, bf16[4,48,2048]{2,1,0:T(8,128)(2,1)}, bf16[4,48,768]{2,1,0:T(8,128)(2,1)}, bf16[3,48,20...) custom-call(f32[8,1536]{1,0:T(8,128)} %concatenate.11.gain_part, ...), custom_call_target="tpu_custom_call" | custom-call | bytes 209715200 | tf_op jit(solution)/shard_map/pallas_call | solution.py:1125
  922.9 8.8 shard_map.211
  931.7 0.1 constant_dynamic-slice_fusion
  931.8 0.6 fusion.20
  (41 shorter events, 0.1 us)
Async XLA Ops:
  0.6 3.5 copy-start.9
  1.5 3.3 copy-start.10
  4.1 2.1 copy-start.16
  4.2 2.1 copy-start.17
  4.2 2.7 copy-start.18
  505.8 97.0 %copy-start.7 = (bf16[4,48,1536]{2,1,0:T(8,128)(2,1)S(1)}, bf16[4,48,1536]{2,1,0:T(8,128)(2,1)}, u32[]{:S(2)}) copy-start(bf16[4,48,1536]{2,1,0:T(8,128)(2,1)} %get-tuple-element.167) | copy-start | bytes 1769476
  609.0 2.7 copy-start
  699.9 2.4 copy-start.2
  699.9 2.4 copy-start.3
  702.2 1.6 copy-start.4
  702.2 2.2 copy-start.5
  796.3 2.3 copy-start.6
  796.3 2.3 copy-start.8
  796.3 3.2 copy-start.1
  799.6 5.0 copy-start.12
  799.6 5.0 copy-start.13
  799.6 5.0 copy-start.14
  799.6 5.0 copy-start.15
  922.9 8.8 copy-start.11

commit v5 on v4

--- a/solution.py
+++ b/solution.py
@@ -685,10 +685,10 @@
 
     table(0)
     net.advance(((2, g_out0, 0, 1), (2, g_qkv0, 0, TP), (2, g_gain, 0, TP)))
-    for copy in second[:16] + placed[2:]:
+    for copy in second[:16]:
         copy.wait()
-    second = second[16:]
-    net.advance(((4, g_gu0, 0, TP), (4, g_down1, 0, 1), (4, g_out1, 0, 1)))
+    second = second[16:] + placed[2:]
+    net.advance(((4, g_gu0, 0, TP),))
     table(1)
     net.advance(((3, g_out0, 0, 1), (3, g_qkv0, 0, TP), (3, g_gain, 0, TP), (2, g_down0, 0, 1)))
     table(2)
@@ -1038,18 +1038,18 @@
 
 
 def tail_kernel(
-    gain_part, sgu_in, so_in, qkv_own_in, qkv_other, bqkv, up_low,
+    gain_part, sgu_in, o_own_in, o_other, qkv_own_in, qkv_other, bqkv, up_low,
     gain_out, out_sum, b_gu, b_qkv, t_gu, t_qkv, t_qkv1, back,
-    sgu, so, s_qkv, qkv_got, gu_one, gu_pass, gu_two, o_one, o_pass, o_two, q_one, q_pass, q_two,
+    sgu, so, s_qkv, qkv_got, o_got, gu_one, gu_pass, gu_two, o_one, o_pass, o_two, q_one, q_pass, q_two,
     gain_t, gain_a, gain_z, gain_b, gain_y, send_sems, recv_sems, local_sems,
 ):
     net = Net(send_sems, recv_sems, local_sems)
     f32, bf = jnp.float32, jnp.bfloat16
     z, q = net.z, net.q
     z1, z2, z3 = (flip_index(z, bits) for bits in (1, 2, 3))
-    loads = [net.local(sgu_in, sgu), net.local(so_in, so), net.local(qkv_own_in, s_qkv)]
+    loads = [net.local(sgu_in, sgu), net.local(o_own_in, so), net.local(qkv_own_in, s_qkv)]
     net.greet(PEERS, "home")
-    over_y = net.remote(qkv_other, qkv_got, "y")
+    over_y = [net.remote(o_other, o_got, "y"), net.remote(qkv_other, qkv_got, "y")]
 
     def first_hop(source, target, part):
         return [
@@ -1059,13 +1059,15 @@
 
     halves = [(pl.ds(0, 2),), (pl.ds(2, 2),)]
     gu_first = [first_hop(sgu_in, gu_one, part) for part in halves]
-    o_first = first_hop(so_in, o_one, ())
     gains = [net.remote(gain_part, gain_t.at[bits - 1], name) for name, bits in RANK_PEERS]
     net.flying += begin_move(net, "t", bqkv, t_qkv1)
     net.flying += begin_move(net, "g", up_low, back)
     for copy in loads:
         copy.wait()
-    over_y.wait()
+    over_y[0].wait()
+    so[...] = (so[...].astype(f32) + o_got[...].astype(f32)).astype(bf)
+    o_first = first_hop(so, o_one, ())
+    over_y[1].wait()
     s_qkv[...] = (s_qkv[...].astype(f32) + qkv_got[...].astype(f32)).astype(bf)
     every = (pl.ds(0, TP),)
     q_first = first_hop(s_qkv, q_one, every)
@@ -1115,7 +1117,7 @@
     net.finish()
 
 
-def run_tail(cid, gain_part, sgu, so, qkv_own, qkv_other, bqkv, up_low):
+def run_tail(cid, gain_part, sgu, so, o_other, qkv_own, qkv_other, bqkv, up_low):
     bf, f32 = jnp.bfloat16, jnp.float32
     shape = jax.ShapeDtypeStruct
     gu_block = (TP,) + sgu.shape[2:]
@@ -1134,13 +1136,14 @@
             shape(three(q_block), bf),
             shape(up_low.shape, bf),
         ],
-        in_specs=[IN_VMEM] + [ANYWHERE] * 6,
+        in_specs=[IN_VMEM] + [ANYWHERE] * 7,
         out_specs=[IN_VMEM] * 4 + [ANYWHERE] * 4,
         scratch_shapes=[
             pltpu.VMEM(sgu.shape, bf),
             pltpu.VMEM(so.shape, bf),
             pltpu.VMEM(qkv_own.shape, bf),
             pltpu.VMEM(qkv_own.shape, bf),
+            pltpu.VMEM(so.shape, bf),
         ]
         + [
             pltpu.VMEM(dims, bf)
@@ -1158,7 +1161,7 @@
             collective_id=cid, has_side_effects=True, vmem_limit_bytes=VMEM_LIMIT
         ),
         cost_estimate=pl.CostEstimate(flops=0, bytes_accessed=200 * 2**20, transcendentals=0),
-    )(gain_part, sgu, so, qkv_own, qkv_other, bqkv, up_low)
+    )(gain_part, sgu, so, o_other, qkv_own, qkv_other, bqkv, up_low)
 
 
 def norm_backward(values, gain_row, incoming):
@@ -1627,57 +1630,56 @@
         ((3, down, 0, 1), (5, gu, 0, 2), (5, gu, 2, 2)),
         ((2, gu, 0, 2),),
         ((2, gu, 2, 2), (3, gu, 0, 2)),
-        ((3, gu, 2, 2), (1, qkv_next, 0, 4), (5, out_next, 0, 1)),
-        ((2, qkv_next, 0, 4), (2, out_next, 0, 1), (5, down_next, 0, 1), (1, gu_next, 0, 2)),
+        ((3, gu, 2, 2), (1, qkv_next, 0, 4), (1, out_next, 0, 1)),
+        ((2, qkv_next, 0, 4), (2, out_next, 0, 1), (1, down_next, 0, 1)),
         ((3, qkv_next, 0, 4), (3, out_next, 0, 1), (2, down_next, 0, 1)),
     )
     programs1 = (
-        ((3, down, 0, 1), (2, gu, 0, 2), (1, gu, 2, 2)),
-        ((3, gu, 0, 2), (2, gu, 2, 2)),
-        (),
+        ((3, down, 0, 1), (1, gu, 0, 2), (1, gu, 2, 2)),
+        ((2, gu, 0, 2),),
+        ((2, gu, 2, 2), (3, gu, 0, 2)),
         ((3, gu, 2, 2),),
         (),
         (),
     )
     tables = (cosine, sine, lens)
     res = forward_layer(
-        programs0, cotangent, 2, conts, hidden, gains[0], gains[2], *tables,
+        programs0, None, 2, conts, hidden, gains[0], gains[2], *tables,
         (g_qkv0, g_out0, g_gu0, g_down0, g_qkv1, g_out1, g_gu1, g_down1),
     )
     weights0, moving1, acts0 = res[:4], res[4:8], res[8:]
-    (x1, mid0, lse0, low1, rows0, qkv0, mix0, frows0, gate0, up0, act0, branch) = acts0
-    res = forward_layer(programs1, None, 3, conts, x1, gains[1], gains[3], *tables, moving1)
+    (x1, mid0, lse0, low1, rows0, qkv0, mix0, frows0, gate0, up0, act0) = acts0
+    res = forward_layer(programs1, cotangent, 3, conts, x1, gains[1], gains[3], *tables, moving1)
     weights1, acts1 = res[:4], res[4:]
-    (x2, mid1, lse1, low2, rows1, qkv1, mix1, frows1, gate1, up1, act1) = acts1
+    (x2, mid1, lse1, low2, rows1, qkv1, mix1, frows1, gate1, up1, act1, branch) = acts1
 
     (low1_back, gmid1, ggf1, dmix1, d_own, d_got, gu_own, gu_other, o_own, o_other) = ffn_backward(
         4, (("g", low1),), branch, True, mid1, gains[3], act1, frows1, gate1, up1, mix1,
         weights1[3], weights1[2], weights1[1],
     )
     sd1 = add_low(d_own, d_got)
-    (gu_got, o_got, rd1, low2_back, up_1, _, gga1, qkv_own1, qkv_other1) = attn_backward(
-        5, (("y", gu_other), ("y", o_other), ("z", sd1), ("g", low2)), conts,
+    (gu_got, rd1, low2_back, up_1, _, gga1, qkv_own1, qkv_other1) = attn_backward(
+        5, (("y", gu_other), ("z", sd1), ("g", low2)), conts,
         gmid1, x1, gains[1], qkv1, dmix1, mix1, lse1, lens, cosine, sine, rows1, weights1[0],
     )
     sgu1 = add_low(gu_own, gu_got)
+    (qkv_got1, o_got, rgu1, gmid0, ggf0, dmix0, d_own0, d_got0, gu_own0, gu_other0, o_own0, o_other0) = ffn_backward(
+        6, (("y", qkv_other1), ("y", o_other), ("zc", sgu1)), up_1, False, mid0, gains[2], act0, frows0, gate0, up0, mix0,
+        weights0[3], weights0[2], weights0[1],
+    )
+    sqkv1 = add_low(qkv_own1, qkv_got1)
     so1 = add_low(o_own, o_got)
-    (qkv_got1, rgu1, ro1, gmid0, ggf0, dmix0, d_own0, d_got0, gu_own0, gu_other0, o_own0, o_other0) = ffn_backward(
-        6, (("y", qkv_other1), ("zc", sgu1), ("z", so1)), up_1, False, mid0, gains[2], act0, frows0, gate0, up0, mix0,
-        weights0[3], weights0[2], weights0[1],
-    )
-    sqkv1 = add_low(qkv_own1, qkv_got1)
     sd0 = add_low(d_own0, d_got0)
     bgu1 = z_total(sgu1, rgu1, 1)
-    (gu_got0, o_got0, rqkv1, rd0, tgu1, _, up_low, gga0, qkv_own0, qkv_other0) = attn_backward(
-        7, (("y", gu_other0), ("y", o_other0), ("zc", sqkv1), ("z", sd0), ("t", bgu1)), conts,
+    (gu_got0, rqkv1, rd0, ro1, tgu1, _, up_low, gga0, qkv_own0, qkv_other0) = attn_backward(
+        7, (("y", gu_other0), ("zc", sqkv1), ("z", sd0), ("z", so1), ("t", bgu1)), conts,
         gmid0, hidden, gains[0], qkv0, dmix0, mix0, lse0, lens, cosine, sine, rows0, weights0[0],
     )
     sgu0 = add_low(gu_own0, gu_got0)
-    so0 = add_low(o_own0, o_got0)
     bqkv1 = z_total(sqkv1, rqkv1, 1)
     gain_part = jnp.concatenate([gga0, gga1, ggf0, ggf1, jnp.zeros((4, depth), jnp.float32)], axis=0)
     (gain_sums, osum0, bgu0, bqkv0, tgu0, tqkv0, tqkv1, back) = run_tail(
-        8, gain_part, sgu0, so0, qkv_own0, qkv_other0, bqkv1, up_low
+        8, gain_part, sgu0, o_own0, o_other0, qkv_own0, qkv_other0, bqkv1, up_low
     )
     gain_sums = gain_sums[:4]
     device = lax.axis_index("dp") * lax.axis_size("fsdp") + lax.axis_index("fsdp")

time: 941 us -> 914 us (0.971)
  Pallas kernels: 890 us -> 870 us
    pallas_call x2, Pallas kernels: 188 us -> 165 us  [attn_backward(): pl.pallas_call(functools.partial(attn_backward_kernel, kinds, conts), out...]
    pallas_call x2, Pallas kernels: 296 us -> 316 us  [forward_layer(): pl.pallas_call(functools.partial(forward_kernel, programs, bool(c), conts...]
    pallas_call x1, Pallas kernels: 133 us -> 122 us  [start_exchange(): pl.pallas_call(functools.partial(start_kernel, conts), out_shape=outs, in...]
where the time goes in v5:
time: 914 us; the launch traced here: 912 us
  Pallas kernels  870 us (95%)
  other arithmetic  26.5 us (3%)
  local copies, waits for them, and re-layouts  13.6 us (1%)
    pallas_call x2, Pallas kernels, forward_layer(): pl.pallas_call(functools.partial(forward_kernel, programs, bool(c), conts...  316 us
    pallas_call x2, Pallas kernels, attn_backward(): pl.pallas_call(functools.partial(attn_backward_kernel, kinds, conts), out...  165 us
    pallas_call x2, Pallas kernels, ffn_backward(): pl.pallas_call(functools.partial(ffn_backward_kernel, kinds, given), out_...  140 us
    pallas_call x1, Pallas kernels, start_exchange(): pl.pallas_call(functools.partial(start_kernel, conts), out_shape=outs, in...  122 us
    pallas_call x1, Pallas kernels, run_tail(): pl.pallas_call(tail_kernel, out_shape=[shape(gain_part.shape, f32), shape...  118 us

profile of v5, /device:TPU:0, one launch (start us, length us, event | category | flops | bytes accessed | tf_op | source)
XLA Modules:
  0.0 911.6 jit_solution(11613452573150608117)
XLA Ops:
  0.7 0.8 fusion.2.spread_sin
  1.5 0.8 fusion.3.spread_cos
  2.2 1.3 reshape.95
  3.6 0.3 copy.51
  3.9 0.0 copy-start.16
  3.9 0.2 reshape.96
  4.2 0.2 reshape.99
  4.4 0.2 copy.52
  4.6 0.1 reshape.100
  4.7 0.2 reshape.97
  5.0 0.2 copy.53
  5.2 0.1 reshape.98
  5.3 0.9 pad_maximum_fusion.qkv_pack
  6.2 0.6 fusion.19.gain_tile
  6.8 0.6 pad.16.lengths
  7.5 0.5 pad_bitcast_fusion.frequency
  8.0 121.6 %shard_map.203 = (f32[256,1536]{1,0:T(8,128)}, f32[1024,768]{1,0:T(8,128)}, f32[1024,768]{1,0:T(8,128)}, s32[8,128]{1,0:T(8,128)}, bf16[2,4,4,48,768]{4,3,2,1,0:...) custom-call(bf16[2,4,48,768]{3,2,1,0:T(8,128)(2,1)} %pad_maximum_fus, ...), custom_call_target="tpu_custom_call" | custom-call | bytes 314572800 | tf_op jit(solution)/shard_map/pallas_call | solution.py:723
  129.6 0.9 slice_bitcast_fusion
  130.5 0.2 slice_reduce_fusion
  130.7 0.7 squeeze.20.refs_1_.refs_2_
  131.4 0.7 squeeze.21.refs_2_.refs_1_
  132.1 151.7 %shard_map.204 = (bf16[2,4,4,48,768]{4,3,2,1,0:T(8,128)(2,1)}, bf16[2,1,4,48,1536]{4,3,2,1,0:T(8,128)(2,1)}, bf16[2,4,4,48,2048]{4,3,2,1,0:T(8,128)(2,1)}, bf16[...) custom-call(f32[256,1536]{1,0:T(8,128)} %get-tuple-element.113.refs_, ...), custom_call_target="tpu_custom_call", output_to_operand_aliasing={{0}: (6, {}), {1}: (7, {}), {2}: (8, {}), {3}: (9, {}), {4}... | custom-call | flops 16000000000 | bytes 419430400 | tf_op jit(solution)/shard_map/pallas_call | solution.py:974
  283.8 0.7 squeeze.22.refs_1_.refs_2_
  284.5 0.7 squeeze.23.refs_2_.refs_1_
  285.1 164.1 %shard_map.205 = (bf16[2,4,4,48,768]{4,3,2,1,0:T(8,128)(2,1)}, bf16[2,1,4,48,1536]{4,3,2,1,0:T(8,128)(2,1)}, bf16[2,4,4,48,2048]{4,3,2,1,0:T(8,128)(2,1)}, bf16[...) custom-call(f32[256,1536]{1,0:T(8,128)} %get-tuple-element.127.refs_, ...), custom_call_target="tpu_custom_call", output_to_operand_aliasing={{0}: (7, {}), {1}: (8, {}), {2}: (9, {}), {3}: (10, {})} | custom-call | flops 16000000000 | bytes 419430400 | tf_op jit(solution)/shard_map/pallas_call | solution.py:974
  449.2 61.1 %shard_map.206 = (bf16[256,1536]{1,0:T(8,128)(2,1)}, f32[256,1536]{1,0:T(8,128)}, f32[1,1536]{1,0:T(1,128)}, bf16[1024,384]{1,0:T(8,128)(2,1)}, bf16[4,128,1536]...) custom-call(f32[256,1536]{1,0:T(8,128)} %get-tuple-element.132.refs_, ...), custom_call_target="tpu_custom_call" | custom-call | flops 24000000000 | bytes 209715200 | tf_op jit(solution)/shard_map/pallas_call | solution.py:1361
  510.3 3.4 add_convert_fusion.3.refs_13_
  513.8 84.9 %shard_map.207 = (bf16[4,4,48,2048]{3,2,1,0:T(8,128)(2,1)}, bf16[3,128,1536]{2,1,0:T(8,128)(2,1)}, bf16[256,1536]{1,0:T(8,128)(2,1)}, f32[256,1536]{1,0:T(8,128)...) custom-call(f32[256,1536]{1,0:T(8,128)} %get-tuple-element.143.refs_, ...), custom_call_target="tpu_custom_call" | custom-call | flops 16000000000 | bytes 209715200 | tf_op jit(solution)/shard_map/pallas_call | solution.py:1499
  598.7 4.2 add_convert_fusion.1
  602.9 2.1 copy.40.refs_13_
  605.0 0.5 copy-done
  605.6 79.1 %shard_map.208 = (bf16[4,4,48,768]{3,2,1,0:T(8,128)(2,1)}, bf16[4,48,1536]{2,1,0:T(8,128)(2,1)}, bf16[3,4,48,2048]{3,2,1,0:T(8,128)(2,1)}, f32[256,1536]{1,0:T(8...) custom-call(f32[256,1536]{1,0:T(8,128)} %get-tuple-element.126.refs_, ...), custom_call_target="tpu_custom_call" | custom-call | flops 24000000000 | bytes 209715200 | tf_op jit(solution)/shard_map/pallas_call | solution.py:1361
  684.6 2.3 convert_reduce_fusion
  687.0 2.4 fusion.refs_16_.refs_9_
  689.3 1.0 add_convert_fusion.5.refs_15_.refs_11_
  690.3 1.6 add_convert_fusion.2.refs_14_.refs_5_
  691.9 0.6 copy-done.4
  692.5 0.3 add_convert_fusion.4
  692.8 1.1 copy.43.refs_13_
  693.9 80.5 %shard_map.209 = (bf16[4,4,48,2048]{3,2,1,0:T(8,128)(2,1)}, bf16[3,4,48,768]{3,2,1,0:T(8,128)(2,1)}, bf16[3,128,1536]{2,1,0:T(8,128)(2,1)}, bf16[3,48,1536]{2,1,...) custom-call(f32[256,1536]{1,0:T(8,128)} %get-tuple-element.166.refs_, ...), custom_call_target="tpu_custom_call" | custom-call | flops 16000000000 | bytes 209715200 | tf_op jit(solution)/shard_map/pallas_call | solution.py:1499
  774.4 1.4 convert_reduce_fusion.1
  775.8 0.8 fusion.1.bqkv.refs_7_
  776.6 6.2 add_convert_fusion.sgu_in
  782.8 0.7 concatenate.11.gain_part
  783.4 118.4 %shard_map.210 = (f32[8,1536]{1,0:T(8,128)}, f32[48,1536]{1,0:T(8,128)}, bf16[4,48,2048]{2,1,0:T(8,128)(2,1)}, bf16[4,48,768]{2,1,0:T(8,128)(2,1)}, bf16[3,48,20...) custom-call(f32[8,1536]{1,0:T(8,128)} %concatenate.11.gain_part, ...), custom_call_target="tpu_custom_call" | custom-call | bytes 209715200 | tf_op jit(solution)/shard_map/pallas_call | solution.py:1127
  901.9 8.8 shard_map.211
  910.7 0.1 constant_dynamic-slice_fusion
  910.8 0.6 fusion.20
  (36 shorter events, 0.1 us)
Async XLA Ops:
  0.6 3.5 copy-start.7
  0.7 4.1 copy-start.8
  3.9 2.3 copy-start.14
  3.9 2.3 copy-start.15
  3.9 2.9 copy-start.16
  602.9 2.7 copy-start
  686.9 2.4 copy-start.5
  686.9 2.4 copy-start.6
  687.0 3.4 copy-start.1
  687.0 3.4 copy-start.2
  690.3 1.6 copy-start.3
  690.3 2.2 copy-start.4
  776.6 6.2 copy-start.10
  776.6 6.2 copy-start.11
  776.6 6.2 copy-start.12
  776.6 6.2 copy-start.13
  901.9 8.8 copy-start.9

commit v6 on v5

--- a/solution.py
+++ b/solution.py
@@ -685,10 +685,7 @@
 
     table(0)
     net.advance(((2, g_out0, 0, 1), (2, g_qkv0, 0, TP), (2, g_gain, 0, TP)))
-    for copy in second[:16]:
-        copy.wait()
-    second = second[16:] + placed[2:]
-    net.advance(((4, g_gu0, 0, TP),))
+    second += placed[2:]
     table(1)
     net.advance(((3, g_out0, 0, 1), (3, g_qkv0, 0, TP), (3, g_gain, 0, TP), (2, g_down0, 0, 1)))
     table(2)
@@ -842,8 +839,6 @@
     load_o = net.local(moving[1], w_o)
     net.greet(("core", "x", "y", "z1", "z2", "z3"), "group" if has_cot else None)
     net.advance(steps[0])
-    if has_cot:
-        bring = net.regroup(cot, branch.at[0], "group")
     rows[0] = normalize(x_own[...], gain_a[...])
     begun = spread_begin(net, rows)
     load_qkv.wait()
@@ -860,6 +855,8 @@
     net.keep(rows, rows_out)
     net.keep(qkv, qkv_out)
     net.advance(steps[1])
+    if has_cot:
+        bring = net.regroup(cot, branch.at[0], "group")
     attend_forward_block(net, qkv, lengths, conts, mixed, lse_ref)
     net.keep(mixed, mixed_out)
     net.advance(steps[2])
@@ -1627,31 +1624,31 @@
     gains = jnp.transpose(g_gain[..., :4, :shard], (3, 0, 1, 2, 4)).reshape(4, 1, depth)
     qkv, out, gu, down, qkv_next, out_next, gu_next, down_next = range(8)
     programs0 = (
-        ((3, down, 0, 1), (5, gu, 0, 2), (5, gu, 2, 2)),
+        ((3, down, 0, 1), (1, gu, 0, 2), (1, gu, 2, 2)),
         ((2, gu, 0, 2),),
         ((2, gu, 2, 2), (3, gu, 0, 2)),
         ((3, gu, 2, 2), (1, qkv_next, 0, 4), (1, out_next, 0, 1)),
-        ((2, qkv_next, 0, 4), (2, out_next, 0, 1), (1, down_next, 0, 1)),
+        ((2, qkv_next, 0, 4), (2, out_next, 0, 1), (1, down_next, 0, 1), (1, gu_next, 0, 2)),
         ((3, qkv_next, 0, 4), (3, out_next, 0, 1), (2, down_next, 0, 1)),
     )
     programs1 = (
-        ((3, down, 0, 1), (1, gu, 0, 2), (1, gu, 2, 2)),
-        ((2, gu, 0, 2),),
-        ((2, gu, 2, 2), (3, gu, 0, 2)),
+        ((3, down, 0, 1), (2, gu, 0, 2), (1, gu, 2, 2)),
+        ((3, gu, 0, 2), (2, gu, 2, 2)),
+        (),
         ((3, gu, 2, 2),),
         (),
         (),
     )
     tables = (cosine, sine, lens)
     res = forward_layer(
-        programs0, None, 2, conts, hidden, gains[0], gains[2], *tables,
+        programs0, cotangent, 2, conts, hidden, gains[0], gains[2], *tables,
         (g_qkv0, g_out0, g_gu0, g_down0, g_qkv1, g_out1, g_gu1, g_down1),
     )
     weights0, moving1, acts0 = res[:4], res[4:8], res[8:]
-    (x1, mid0, lse0, low1, rows0, qkv0, mix0, frows0, gate0, up0, act0) = acts0
-    res = forward_layer(programs1, cotangent, 3, conts, x1, gains[1], gains[3], *tables, moving1)
+    (x1, mid0, lse0, low1, rows0, qkv0, mix0, frows0, gate0, up0, act0, branch) = acts0
+    res = forward_layer(programs1, None, 3, conts, x1, gains[1], gains[3], *tables, moving1)
     weights1, acts1 = res[:4], res[4:]
-    (x2, mid1, lse1, low2, rows1, qkv1, mix1, frows1, gate1, up1, act1, branch) = acts1
+    (x2, mid1, lse1, low2, rows1, qkv1, mix1, frows1, gate1, up1, act1) = acts1
 
     (low1_back, gmid1, ggf1, dmix1, d_own, d_got, gu_own, gu_other, o_own, o_other) = ffn_backward(
         4, (("g", low1),), branch, True, mid1, gains[3], act1, frows1, gate1, up1, mix1,

time: 914 us -> 887 us (0.970)
  Pallas kernels: 870 us -> 837 us
    pallas_call x2, Pallas kernels: 316 us -> 295 us  [forward_layer(): pl.pallas_call(functools.partial(forward_kernel, programs, bool(c), conts...]
    pallas_call x1, Pallas kernels: 122 us -> 110 us  [start_exchange(): pl.pallas_call(functools.partial(start_kernel, conts), out_shape=outs, in...]
where the time goes in v6:
time: 887 us; the launch traced here: 879 us
  Pallas kernels  837 us (94%)
  other arithmetic  26.5 us (3%)
  local copies, waits for them, and re-layouts  13.6 us (2%)
    pallas_call x2, Pallas kernels, forward_layer(): pl.pallas_call(functools.partial(forward_kernel, programs, bool(c), conts...  295 us
    pallas_call x2, Pallas kernels, attn_backward(): pl.pallas_call(functools.partial(attn_backward_kernel, kinds, conts), out...  166 us
    pallas_call x2, Pallas kernels, ffn_backward(): pl.pallas_call(functools.partial(ffn_backward_kernel, kinds, given), out_...  140 us
    pallas_call x1, Pallas kernels, run_tail(): pl.pallas_call(tail_kernel, out_shape=[shape(gain_part.shape, f32), shape...  118 us
    pallas_call x1, Pallas kernels, start_exchange(): pl.pallas_call(functools.partial(start_kernel, conts), out_shape=outs, in...  110 us

profile of v6, /device:TPU:0, one launch (start us, length us, event | category | flops | bytes accessed | tf_op | source)
XLA Modules:
  0.0 879.0 jit_solution(9747741834196903638)
XLA Ops:
  0.7 0.8 fusion.2.spread_sin
  1.5 0.8 fusion.3.spread_cos
  2.2 1.3 reshape.95
  3.6 0.3 copy.51
  3.9 0.0 copy-start.14
  3.9 0.2 reshape.96
  4.2 0.2 reshape.99
  4.4 0.2 copy.52
  4.6 0.1 reshape.100
  4.7 0.2 reshape.97
  5.0 0.2 copy.53
  5.2 0.1 reshape.98
  5.3 0.9 pad_maximum_fusion.qkv_pack
  6.2 0.6 fusion.19.gain_tile
  6.8 0.6 pad.16.lengths
  7.5 0.5 pad_bitcast_fusion.frequency
  8.0 110.0 %shard_map.203 = (f32[256,1536]{1,0:T(8,128)}, f32[1024,768]{1,0:T(8,128)}, f32[1024,768]{1,0:T(8,128)}, s32[8,128]{1,0:T(8,128)}, bf16[2,4,4,48,768]{4,3,2,1,0:...) custom-call(bf16[2,4,48,768]{3,2,1,0:T(8,128)(2,1)} %pad_maximum_fus, ...), custom_call_target="tpu_custom_call" | custom-call | bytes 314572800 | tf_op jit(solution)/shard_map/pallas_call | solution.py:720
  118.0 0.9 slice_bitcast_fusion
  118.9 0.2 slice_reduce_fusion
  119.1 0.7 squeeze.20.refs_1_.refs_2_
  119.8 0.7 squeeze.21.refs_2_.refs_1_
  120.5 177.2 %shard_map.204 = (bf16[2,4,4,48,768]{4,3,2,1,0:T(8,128)(2,1)}, bf16[2,1,4,48,1536]{4,3,2,1,0:T(8,128)(2,1)}, bf16[2,4,4,48,2048]{4,3,2,1,0:T(8,128)(2,1)}, bf16[...) custom-call(f32[256,1536]{1,0:T(8,128)} %get-tuple-element.113.refs_, ...), custom_call_target="tpu_custom_call", output_to_operand_aliasing={{0}: (7, {}), {1}: (8, {}), {2}: (9, {}), {3}: (10, {}), {4... | custom-call | flops 16000000000 | bytes 419430400 | tf_op jit(solution)/shard_map/pallas_call | solution.py:971
  297.7 0.7 squeeze.22.refs_1_.refs_2_
  298.4 0.7 squeeze.23.refs_2_.refs_1_
  299.1 117.6 %shard_map.205 = (bf16[2,4,4,48,768]{4,3,2,1,0:T(8,128)(2,1)}, bf16[2,1,4,48,1536]{4,3,2,1,0:T(8,128)(2,1)}, bf16[2,4,4,48,2048]{4,3,2,1,0:T(8,128)(2,1)}, bf16[...) custom-call(f32[256,1536]{1,0:T(8,128)} %get-tuple-element.127.refs_, ...), custom_call_target="tpu_custom_call", output_to_operand_aliasing={{0}: (6, {}), {1}: (7, {}), {2}: (8, {}), {3}: (9, {})} | custom-call | flops 16000000000 | bytes 419430400 | tf_op jit(solution)/shard_map/pallas_call | solution.py:971
  416.6 61.1 %shard_map.206 = (bf16[256,1536]{1,0:T(8,128)(2,1)}, f32[256,1536]{1,0:T(8,128)}, f32[1,1536]{1,0:T(1,128)}, bf16[1024,384]{1,0:T(8,128)(2,1)}, bf16[4,128,1536]...) custom-call(f32[256,1536]{1,0:T(8,128)} %get-tuple-element.132.refs_, ...), custom_call_target="tpu_custom_call" | custom-call | flops 24000000000 | bytes 209715200 | tf_op jit(solution)/shard_map/pallas_call | solution.py:1358
  477.8 3.5 add_convert_fusion.3.refs_13_
  481.3 85.3 %shard_map.207 = (bf16[4,4,48,2048]{3,2,1,0:T(8,128)(2,1)}, bf16[3,128,1536]{2,1,0:T(8,128)(2,1)}, bf16[256,1536]{1,0:T(8,128)(2,1)}, f32[256,1536]{1,0:T(8,128)...) custom-call(f32[256,1536]{1,0:T(8,128)} %get-tuple-element.143.refs_, ...), custom_call_target="tpu_custom_call" | custom-call | flops 16000000000 | bytes 209715200 | tf_op jit(solution)/shard_map/pallas_call | solution.py:1496
  566.6 4.2 add_convert_fusion.1
  570.8 2.1 copy.40.refs_13_
  572.9 0.5 copy-done
  573.4 78.6 %shard_map.208 = (bf16[4,4,48,768]{3,2,1,0:T(8,128)(2,1)}, bf16[4,48,1536]{2,1,0:T(8,128)(2,1)}, bf16[3,4,48,2048]{3,2,1,0:T(8,128)(2,1)}, f32[256,1536]{1,0:T(8...) custom-call(f32[256,1536]{1,0:T(8,128)} %get-tuple-element.126.refs_, ...), custom_call_target="tpu_custom_call" | custom-call | flops 24000000000 | bytes 209715200 | tf_op jit(solution)/shard_map/pallas_call | solution.py:1358
  652.0 2.3 convert_reduce_fusion
  654.4 2.4 fusion.refs_16_.refs_9_
  656.8 0.9 add_convert_fusion.5.refs_15_.refs_11_
  657.7 1.6 add_convert_fusion.2.refs_14_.refs_5_
  659.3 0.6 copy-done.4
  659.9 0.3 add_convert_fusion.4
  660.2 1.1 copy.43.refs_13_
  661.3 80.5 %shard_map.209 = (bf16[4,4,48,2048]{3,2,1,0:T(8,128)(2,1)}, bf16[3,4,48,768]{3,2,1,0:T(8,128)(2,1)}, bf16[3,128,1536]{2,1,0:T(8,128)(2,1)}, bf16[3,48,1536]{2,1,...) custom-call(f32[256,1536]{1,0:T(8,128)} %get-tuple-element.166.refs_, ...), custom_call_target="tpu_custom_call" | custom-call | flops 16000000000 | bytes 209715200 | tf_op jit(solution)/shard_map/pallas_call | solution.py:1496
  741.8 1.4 convert_reduce_fusion.1
  743.2 0.8 fusion.1.bqkv.refs_7_
  743.9 6.2 add_convert_fusion.sgu_in
  750.1 0.7 concatenate.11.gain_part
  750.8 118.2 %shard_map.210 = (f32[8,1536]{1,0:T(8,128)}, f32[48,1536]{1,0:T(8,128)}, bf16[4,48,2048]{2,1,0:T(8,128)(2,1)}, bf16[4,48,768]{2,1,0:T(8,128)(2,1)}, bf16[3,48,20...) custom-call(f32[8,1536]{1,0:T(8,128)} %concatenate.11.gain_part, ...), custom_call_target="tpu_custom_call" | custom-call | bytes 209715200 | tf_op jit(solution)/shard_map/pallas_call | solution.py:1124
  869.1 8.8 %shard_map.211 = (bf16[2,256,1536]{2,1,0:T(8,128)(2,1)}, f32[256,1536]{1,0:T(8,128)}, f32[2,48,1536]{2,1,0:T(8,128)}, f32[2,48,768]{2,1,0:T(8,128)}, f32[2,48,76...) custom-call(bf16[4,48,768]{2,1,0:T(8,128)(2,1)} %get-tuple-element.1, ...), custom_call_target="tpu_custom_call" | custom-call | tf_op jit(solution)/shard_map/pallas_call | solution.py:1580
  877.9 0.1 constant_dynamic-slice_fusion
  878.0 0.6 fusion.20
  (36 shorter events, 0.1 us)
Async XLA Ops:
  0.6 3.5 copy-start.7
  0.7 4.1 copy-start.8
  3.9 2.3 copy-start.14
  3.9 2.3 copy-start.15
  3.9 2.9 copy-start.16
  570.8 2.7 copy-start
  654.3 2.4 copy-start.5
  654.4 2.4 copy-start.6
  654.4 3.3 copy-start.1
  654.4 3.3 copy-start.2
  657.7 1.6 copy-start.3
  657.7 2.2 copy-start.4
  743.9 6.2 copy-start.10
  743.9 6.2 copy-start.11
  743.9 6.2 copy-start.12
  743.9 6.2 copy-start.13
  869.1 8.8 %copy-start.9 = (f32[8,1536]{1,0:T(8,128)S(1)}, f32[8,1536]{1,0:T(8,128)}, u32[]{:S(2)}) copy-start(f32[8,1536]{1,0:T(8,128)} %get-tuple-element.207) | copy-start | bytes 147460

commit v7 on v6

--- a/solution.py
+++ b/solution.py
@@ -1058,7 +1058,6 @@
     gu_first = [first_hop(sgu_in, gu_one, part) for part in halves]
     gains = [net.remote(gain_part, gain_t.at[bits - 1], name) for name, bits in RANK_PEERS]
     net.flying += begin_move(net, "t", bqkv, t_qkv1)
-    net.flying += begin_move(net, "g", up_low, back)
     for copy in loads:
         copy.wait()
     over_y[0].wait()
@@ -1086,6 +1085,7 @@
     ]
     o_second = second_hop(so, o_one, o_pass, o_two, (), o_first)
     q_second = second_hop(s_qkv, q_one, q_pass, q_two, every, q_first)
+    net.flying += begin_move(net, "g", up_low, back)
     for copy in gains:
         copy.wait()
     gain_b[...] = gain_a[...] + gain_z[0] + gain_z[1] + gain_z[2]

time: 887 us -> 892 us (level)
  no operation moved by 1% of the time
where the time goes in v7:
time: 892 us; the launch traced here: 878 us
  Pallas kernels  837 us (94%)
  other arithmetic  26.5 us (3%)
  local copies, waits for them, and re-layouts  13.6 us (2%)
    pallas_call x2, Pallas kernels, forward_layer(): pl.pallas_call(functools.partial(forward_kernel, programs, bool(c), conts...  295 us
    pallas_call x2, Pallas kernels, attn_backward(): pl.pallas_call(functools.partial(attn_backward_kernel, kinds, conts), out...  166 us
    pallas_call x2, Pallas kernels, ffn_backward(): pl.pallas_call(functools.partial(ffn_backward_kernel, kinds, given), out_...  140 us
    pallas_call x1, Pallas kernels, run_tail(): pl.pallas_call(tail_kernel, out_shape=[shape(gain_part.shape, f32), shape...  117 us
    pallas_call x1, Pallas kernels, start_exchange(): pl.pallas_call(functools.partial(start_kernel, conts), out_shape=outs, in...  110 us

profile of v7, /device:TPU:0, one launch (start us, length us, event | category | flops | bytes accessed | tf_op | source)
XLA Modules:
  0.0 878.1 jit_solution(11541456033888451884)
XLA Ops:
  0.7 0.8 fusion.2.spread_sin
  1.5 0.8 fusion.3.spread_cos
  2.2 1.3 reshape.95
  3.6 0.3 copy.51
  3.9 0.0 copy-start.16
  3.9 0.2 reshape.96
  4.2 0.2 reshape.99
  4.4 0.2 copy.52
  4.6 0.1 reshape.100
  4.7 0.2 reshape.97
  5.0 0.2 copy.53
  5.2 0.1 reshape.98
  5.3 0.9 pad_maximum_fusion.qkv_pack
  6.2 0.6 fusion.19.gain_tile
  6.8 0.6 pad.16.lengths
  7.5 0.5 pad_bitcast_fusion.frequency
  8.0 110.0 %shard_map.203 = (f32[256,1536]{1,0:T(8,128)}, f32[1024,768]{1,0:T(8,128)}, f32[1024,768]{1,0:T(8,128)}, s32[8,128]{1,0:T(8,128)}, bf16[2,4,4,48,768]{4,3,2,1,0:...) custom-call(bf16[2,4,48,768]{3,2,1,0:T(8,128)(2,1)} %pad_maximum_fus, ...), custom_call_target="tpu_custom_call" | custom-call | bytes 314572800 | tf_op jit(solution)/shard_map/pallas_call | solution.py:720
  118.0 0.9 slice_bitcast_fusion
  118.9 0.2 slice_reduce_fusion
  119.1 0.7 squeeze.20.refs_1_.refs_2_
  119.8 0.7 squeeze.21.refs_2_.refs_1_
  120.5 177.2 %shard_map.204 = (bf16[2,4,4,48,768]{4,3,2,1,0:T(8,128)(2,1)}, bf16[2,1,4,48,1536]{4,3,2,1,0:T(8,128)(2,1)}, bf16[2,4,4,48,2048]{4,3,2,1,0:T(8,128)(2,1)}, bf16[...) custom-call(f32[256,1536]{1,0:T(8,128)} %get-tuple-element.113.refs_, ...), custom_call_target="tpu_custom_call", output_to_operand_aliasing={{0}: (7, {}), {1}: (8, {}), {2}: (9, {}), {3}: (10, {}), {4... | custom-call | flops 16000000000 | bytes 419430400 | tf_op jit(solution)/shard_map/pallas_call | solution.py:971
  297.7 0.7 squeeze.22.refs_1_.refs_2_
  298.4 0.7 squeeze.23.refs_2_.refs_1_
  299.1 117.6 %shard_map.205 = (bf16[2,4,4,48,768]{4,3,2,1,0:T(8,128)(2,1)}, bf16[2,1,4,48,1536]{4,3,2,1,0:T(8,128)(2,1)}, bf16[2,4,4,48,2048]{4,3,2,1,0:T(8,128)(2,1)}, bf16[...) custom-call(f32[256,1536]{1,0:T(8,128)} %get-tuple-element.127.refs_, ...), custom_call_target="tpu_custom_call", output_to_operand_aliasing={{0}: (6, {}), {1}: (7, {}), {2}: (8, {}), {3}: (9, {})} | custom-call | flops 16000000000 | bytes 419430400 | tf_op jit(solution)/shard_map/pallas_call | solution.py:971
  416.6 61.1 %shard_map.206 = (bf16[256,1536]{1,0:T(8,128)(2,1)}, f32[256,1536]{1,0:T(8,128)}, f32[1,1536]{1,0:T(1,128)}, bf16[1024,384]{1,0:T(8,128)(2,1)}, bf16[4,128,1536]...) custom-call(f32[256,1536]{1,0:T(8,128)} %get-tuple-element.132.refs_, ...), custom_call_target="tpu_custom_call" | custom-call | flops 24000000000 | bytes 209715200 | tf_op jit(solution)/shard_map/pallas_call | solution.py:1358
  477.8 3.5 add_convert_fusion.3.refs_13_
  481.3 85.3 %shard_map.207 = (bf16[4,4,48,2048]{3,2,1,0:T(8,128)(2,1)}, bf16[3,128,1536]{2,1,0:T(8,128)(2,1)}, bf16[256,1536]{1,0:T(8,128)(2,1)}, f32[256,1536]{1,0:T(8,128)...) custom-call(f32[256,1536]{1,0:T(8,128)} %get-tuple-element.143.refs_, ...), custom_call_target="tpu_custom_call" | custom-call | flops 16000000000 | bytes 209715200 | tf_op jit(solution)/shard_map/pallas_call | solution.py:1496
  566.6 4.2 add_convert_fusion.1
  570.8 2.1 copy.40.refs_13_
  572.9 0.5 copy-done
  573.4 78.6 %shard_map.208 = (bf16[4,4,48,768]{3,2,1,0:T(8,128)(2,1)}, bf16[4,48,1536]{2,1,0:T(8,128)(2,1)}, bf16[3,4,48,2048]{3,2,1,0:T(8,128)(2,1)}, f32[256,1536]{1,0:T(8...) custom-call(f32[256,1536]{1,0:T(8,128)} %get-tuple-element.126.refs_, ...), custom_call_target="tpu_custom_call" | custom-call | flops 24000000000 | bytes 209715200 | tf_op jit(solution)/shard_map/pallas_call | solution.py:1358
  652.0 2.3 convert_reduce_fusion
  654.4 2.4 fusion.refs_16_.refs_9_
  656.8 0.9 add_convert_fusion.5.refs_15_.refs_11_
  657.7 1.6 add_convert_fusion.2.refs_14_.refs_5_
  659.3 0.6 copy-done.4
  659.9 0.3 add_convert_fusion.4
  660.2 1.1 copy.43.refs_13_
  661.3 80.5 %shard_map.209 = (bf16[4,4,48,2048]{3,2,1,0:T(8,128)(2,1)}, bf16[3,4,48,768]{3,2,1,0:T(8,128)(2,1)}, bf16[3,128,1536]{2,1,0:T(8,128)(2,1)}, bf16[3,48,1536]{2,1,...) custom-call(f32[256,1536]{1,0:T(8,128)} %get-tuple-element.166.refs_, ...), custom_call_target="tpu_custom_call" | custom-call | flops 16000000000 | bytes 209715200 | tf_op jit(solution)/shard_map/pallas_call | solution.py:1496
  741.8 1.4 convert_reduce_fusion.1
  743.2 0.8 fusion.1.bqkv.refs_7_
  743.9 6.2 add_convert_fusion.sgu_in
  750.1 0.7 concatenate.11.gain_part
  750.8 117.4 %shard_map.210 = (f32[8,1536]{1,0:T(8,128)}, f32[48,1536]{1,0:T(8,128)}, bf16[4,48,2048]{2,1,0:T(8,128)(2,1)}, bf16[4,48,768]{2,1,0:T(8,128)(2,1)}, bf16[3,48,20...) custom-call(f32[8,1536]{1,0:T(8,128)} %concatenate.11.gain_part, ...), custom_call_target="tpu_custom_call" | custom-call | bytes 209715200 | tf_op jit(solution)/shard_map/pallas_call | solution.py:1124
  868.2 8.8 %shard_map.211 = (bf16[2,256,1536]{2,1,0:T(8,128)(2,1)}, f32[256,1536]{1,0:T(8,128)}, f32[2,48,1536]{2,1,0:T(8,128)}, f32[2,48,768]{2,1,0:T(8,128)}, f32[2,48,76...) custom-call(bf16[4,48,768]{2,1,0:T(8,128)(2,1)} %get-tuple-element.1, ...), custom_call_target="tpu_custom_call" | custom-call | tf_op jit(solution)/shard_map/pallas_call | solution.py:1580
  877.0 0.1 constant_dynamic-slice_fusion
  877.1 0.6 fusion.20
  (36 shorter events, 0.1 us)
Async XLA Ops:
  0.6 3.5 copy-start.7
  0.7 4.1 copy-start.8
  3.9 2.3 copy-start.14
  3.9 2.3 copy-start.15
  3.9 2.9 copy-start.16
  570.8 2.7 copy-start
  654.3 2.4 copy-start.5
  654.4 2.4 copy-start.6
  654.4 3.3 copy-start.1
  654.4 3.3 copy-start.2
  657.7 1.6 copy-start.3
  657.7 2.2 copy-start.4
  743.9 6.2 copy-start.10
  743.9 6.2 copy-start.11
  743.9 6.2 copy-start.12
  743.9 6.2 copy-start.13
  868.2 8.8 %copy-start.9 = (f32[8,1536]{1,0:T(8,128)S(1)}, f32[8,1536]{1,0:T(8,128)}, u32[]{:S(2)}) copy-start(f32[8,1536]{1,0:T(8,128)} %get-tuple-element.207) | copy-start | bytes 147460
